TPU v7x, 32 devices: a whole 2x2x4 slice. The times are simulated.
32 devices in a mesh: batch: 16 (over z, x, core), hid: 2 (over y).
Axes of the slice: x: 2, y: 2, z: 4, core: 2. Of those that a mesh axis runs over, the one named last changes fastest.
Arguments:
- tokens: bfloat16 [4096, 2048], P(('batch', 'hid')), may hold values from -6 to 6
- lengths: int32 [32, 4], P(('batch', 'hid')), may hold values from 0 to 128, as said below
- attention_gain: bfloat16 [2048], P('batch'), may hold values from 0.5 to 1.5
- query_down: bfloat16 [2048, 1024], P('batch'), may hold values from -0.125 to 0.125
- query_gain: bfloat16 [1024], P('batch'), may hold values from 0.5 to 1.5
- query_up: bfloat16 [1024, 4096], P('batch'), may hold values from -0.1875 to 0.1875
- key_value: bfloat16 [2048, 512], P('batch'), may hold values from -0.125 to 0.125
- output_weight: bfloat16 [2048, 4096], P('batch'), may hold values from -0.75 to 0.75
- feed_gain: bfloat16 [2048], P('batch'), may hold values from 0.5 to 1.5
- gate_weight: bfloat16 [2048, 5632], P('batch', 'hid'), may hold values from -0.125 to 0.125
- up_weight: bfloat16 [2048, 5632], P('batch', 'hid'), may hold values from -0.125 to 0.125
- down_weight: bfloat16 [2048, 5632], P('batch', 'hid'), may hold values from -0.078125 to 0.078125
- cotangent: bfloat16 [4096, 2048], P(('batch', 'hid')), may hold values from -6 to 6
Outputs:
- output: bfloat16 [4096, 2048], P(('batch', 'hid'))
- grad_tokens: bfloat16 [4096, 2048], P(('batch', 'hid'))
- grad_attention_gain: float32 [2048], P('batch')
- grad_query_down: float32 [2048, 1024], P('batch')
- grad_query_gain: float32 [1024], P('batch')
- grad_query_up: float32 [1024, 4096], P('batch')
- grad_key_value: float32 [2048, 512], P('batch')
- grad_output_weight: float32 [2048, 4096], P('batch')
- grad_feed_gain: float32 [2048], P('batch')
- grad_gate: float32 [2048, 5632], P('batch', 'hid')
- grad_up: float32 [2048, 5632], P('batch', 'hid')
- grad_down: float32 [2048, 5632], P('batch', 'hid')
Inputs may be any that keep to these rules, and one draw needn't show every extreme that they name: Row g holds the lengths of the sequences of device group g in order; used slots hold 32 or more and come first, the rest hold 0; a row sums to 32 to 128; in every draw some row holds one sequence of 128 tokens.
All inputs are finite; a program needn't handle non-finite values.
Results may differ from a plain program's by a relative error of at most 0.017.
Values may be sent and summed in bfloat16 or wider, within the bound.
A program may use at most 320 MiB of HBM per device.

v0:
```python
import jax
import jax.numpy as jnp
from jax import lax
from jax.sharding import PartitionSpec as P

HEADS = 16
HEAD_DIM = 256


EPS = 1e-05
ROPE_BASE = 10000.0
NEGATIVE = -1e30


def matmul(spec, left, right):
    return jnp.einsum(spec, left, right, preferred_element_type=jnp.float32)


def norm_rows(values, gain):
    return values * lax.rsqrt(jnp.mean(values * values, axis=-1, keepdims=True) + EPS) * gain


def rotate(values, cosine, sine):
    half = values.shape[-1] // 2
    first = values[..., :half]
    second = values[..., half:]
    return jnp.concatenate(
        [first * cosine - second * sine, second * cosine + first * sine], axis=-1
    )


def layout(row_lengths, count_rows):
    ends = jnp.cumsum(row_lengths)
    starts = ends - row_lengths
    places = jnp.arange(count_rows, dtype=jnp.int32)
    segment = jnp.sum((places[:, None] >= ends[None, :]).astype(jnp.int32), axis=1)
    begins = jnp.concatenate([starts, ends[-1:]])
    labels = jnp.arange(begins.shape[0], dtype=jnp.int32)
    firsts = jnp.sum(jnp.where(segment[:, None] == labels[None, :], begins[None, :], 0), axis=1)
    position = places - firsts
    valid = places < ends[-1]
    allowed = (segment[:, None] == segment[None, :]) & (places[None, :] <= places[:, None])
    return (position, valid, allowed)


def angles_of(position, head_size):
    half = head_size // 2
    freqs = ROPE_BASE ** (-(jnp.arange(half, dtype=jnp.float32) * 2.0) / head_size)
    angle = position.astype(jnp.float32)[:, None] * freqs[None, :]
    return (jnp.cos(angle), jnp.sin(angle))


def masked_scores(query_rot, key_rot, allowed, scale):
    raw = matmul("qhd,kd->hqk", query_rot, key_rot) * scale
    return jnp.where(allowed[None], raw, NEGATIVE)


def per_device(
    tokens,
    lengths,
    attention_gain,
    query_down,
    query_gain,
    query_up,
    key_value,
    output_weight,
    feed_gain,
    gate_weight,
    up_weight,
    down_weight,
    cotangent,
):
    count_rows = tokens.shape[0]
    scale = HEAD_DIM ** (-0.5)
    norm_gain, latent_weight, latent_gain, query_weight, pair_weight, out_weight, ffn_gain = (
        lax.all_gather(attention_gain, "batch", axis=0, tiled=True),
        lax.all_gather(query_down, "batch", axis=0, tiled=True),
        lax.all_gather(query_gain, "batch", axis=0, tiled=True),
        lax.all_gather(query_up, "batch", axis=0, tiled=True),
        lax.all_gather(key_value, "batch", axis=0, tiled=True),
        lax.all_gather(output_weight, "batch", axis=0, tiled=True),
        lax.all_gather(feed_gain, "batch", axis=0, tiled=True),
    )
    gate_full, up_full, down_full = (
        lax.all_gather(gate_weight, "batch", axis=0, tiled=True),
        lax.all_gather(up_weight, "batch", axis=0, tiled=True),
        lax.all_gather(down_weight, "batch", axis=0, tiled=True),
    )
    inputs = tokens.astype(jnp.float32)
    position, valid, allowed = layout(lengths[0], count_rows)
    cosine, sine = angles_of(position, HEAD_DIM)
    first_gain = norm_gain.astype(jnp.float32)
    second_gain = latent_gain.astype(jnp.float32)
    third_gain = ffn_gain.astype(jnp.float32)
    normed = norm_rows(inputs, first_gain).astype(jnp.bfloat16)
    latent = matmul("rd,dc->rc", normed, latent_weight)
    latent_normed = norm_rows(latent, second_gain).astype(jnp.bfloat16)
    queries = matmul("rc,cf->rf", latent_normed, query_weight).reshape(count_rows, HEADS, HEAD_DIM)
    keyvals = matmul("rd,de->re", normed, pair_weight)
    query_rot = rotate(queries, cosine[:, None, :], sine[:, None, :]).astype(jnp.bfloat16)
    key_rot = rotate(keyvals[:, :HEAD_DIM], cosine, sine).astype(jnp.bfloat16)
    value_rows = keyvals[:, HEAD_DIM:].astype(jnp.bfloat16)
    scores = masked_scores(query_rot, key_rot, allowed, scale)
    highest = jnp.max(scores, axis=-1, keepdims=True)
    raised = jnp.exp(scores - highest)
    totals = jnp.sum(raised, axis=-1, keepdims=True)
    probs = (raised / totals).astype(jnp.bfloat16)
    logsum = highest + jnp.log(totals)
    mixed = (
        matmul("hqk,kd->qhd", probs, value_rows)
        .reshape(count_rows, HEADS * HEAD_DIM)
        .astype(jnp.bfloat16)
    )
    branch = matmul("rf,df->rd", mixed, out_weight)
    middle = inputs + branch
    normed_ffn = norm_rows(middle, third_gain).astype(jnp.bfloat16)
    pair_rows = lax.all_gather(normed_ffn, "hid", axis=0, tiled=True)
    gate = matmul("rd,df->rf", pair_rows, gate_full)
    up = matmul("rd,df->rf", pair_rows, up_full)
    sigma = jax.nn.sigmoid(gate)
    activated = gate * sigma
    slope = sigma * (1.0 + gate * (1.0 - sigma))
    hidden = (activated * up).astype(jnp.bfloat16)
    feed = lax.psum_scatter(
        matmul("rf,df->rd", hidden, down_full).astype(jnp.bfloat16),
        "hid",
        scatter_dimension=0,
        tiled=True,
    ).astype(jnp.float32)
    output = jnp.where(valid[:, None], middle + feed, inputs).astype(jnp.bfloat16)
    upstream = cotangent.astype(jnp.float32)
    kept = jnp.where(valid[:, None], upstream, 0.0)
    pair_grad = lax.all_gather(kept.astype(jnp.bfloat16), "hid", axis=0, tiled=True)
    gate_back, up_back, down_back = (
        lax.all_gather(gate_weight, "batch", axis=0, tiled=True),
        lax.all_gather(up_weight, "batch", axis=0, tiled=True),
        lax.all_gather(down_weight, "batch", axis=0, tiled=True),
    )
    (
        gain_back,
        latent_back_weight,
        latent_gain_back,
        query_back,
        pair_back,
        out_back,
        ffn_gain_back,
    ) = (
        lax.all_gather(attention_gain, "batch", axis=0, tiled=True),
        lax.all_gather(query_down, "batch", axis=0, tiled=True),
        lax.all_gather(query_gain, "batch", axis=0, tiled=True),
        lax.all_gather(query_up, "batch", axis=0, tiled=True),
        lax.all_gather(key_value, "batch", axis=0, tiled=True),
        lax.all_gather(output_weight, "batch", axis=0, tiled=True),
        lax.all_gather(feed_gain, "batch", axis=0, tiled=True),
    )
    hidden_grad = matmul("rd,df->rf", pair_grad, down_back)
    gate_grad = (hidden_grad * up * slope).astype(jnp.bfloat16)
    up_grad = (hidden_grad * activated).astype(jnp.bfloat16)
    grad_down = matmul("rd,rf->df", pair_grad, hidden)
    grad_gate = matmul("rd,rf->df", pair_rows, gate_grad)
    grad_up = matmul("rd,rf->df", pair_rows, up_grad)
    ffn_shares = (
        lax.psum_scatter(grad_gate, "batch", scatter_dimension=0, tiled=True),
        lax.psum_scatter(grad_up, "batch", scatter_dimension=0, tiled=True),
        lax.psum_scatter(grad_down, "batch", scatter_dimension=0, tiled=True),
    )
    ffn_grad = lax.psum_scatter(
        matmul("rf,df->rd", gate_grad, gate_back) + matmul("rf,df->rd", up_grad, up_back),
        "hid",
        scatter_dimension=0,
        tiled=True,
    )
    unused_third, third_pull = jax.vjp(norm_rows, middle, ffn_gain_back.astype(jnp.float32))
    middle_norm_grad, feed_gain_grad = third_pull(ffn_grad)
    middle_grad = kept + middle_norm_grad
    branch_grad = middle_grad.astype(jnp.bfloat16)
    grad_out = matmul("rd,rf->df", branch_grad, mixed)
    mixed_grad = (
        matmul("rd,df->rf", branch_grad, out_back)
        .astype(jnp.bfloat16)
        .reshape(count_rows, HEADS, HEAD_DIM)
    )
    scores_back = masked_scores(query_rot, key_rot, allowed, scale)
    probs_back = jnp.exp(scores_back - logsum)
    prob_grad = matmul("qhd,kd->hqk", mixed_grad, value_rows)
    score_grad = (
        probs_back * (prob_grad - jnp.sum(probs_back * prob_grad, axis=-1, keepdims=True))
    ).astype(jnp.bfloat16)
    value_grad = matmul("hqk,qhd->kd", probs, mixed_grad)
    query_rot_grad = matmul("hqk,kd->qhd", score_grad, key_rot) * scale
    key_rot_grad = matmul("hqk,qhd->kd", score_grad, query_rot) * scale
    query_grad = (
        rotate(query_rot_grad, cosine[:, None, :], -sine[:, None, :])
        .reshape(count_rows, HEADS * HEAD_DIM)
        .astype(jnp.bfloat16)
    )
    key_grad = rotate(key_rot_grad, cosine, -sine)
    keyval_grad = jnp.concatenate([key_grad, value_grad], axis=1).astype(jnp.bfloat16)
    grad_query = matmul("rc,rf->cf", latent_normed, query_grad)
    grad_pair = matmul("rd,re->de", normed, keyval_grad)
    latent_normed_grad = matmul("rf,cf->rc", query_grad, query_back)
    unused_second, second_pull = jax.vjp(norm_rows, latent, latent_gain_back.astype(jnp.float32))
    latent_back, latent_gain_grad = second_pull(latent_normed_grad)
    latent_grad = latent_back.astype(jnp.bfloat16)
    grad_latent = matmul("rd,rc->dc", normed, latent_grad)
    normed_grad = matmul("rc,dc->rd", latent_grad, latent_back_weight) + matmul(
        "re,de->rd", keyval_grad, pair_back
    )
    unused_first, first_pull = jax.vjp(norm_rows, inputs, gain_back.astype(jnp.float32))
    input_norm_grad, norm_gain_grad = first_pull(normed_grad)
    grad_tokens = (middle_grad + input_norm_grad + jnp.where(valid[:, None], 0.0, upstream)).astype(
        jnp.bfloat16
    )
    attention_sums = (
        norm_gain_grad,
        grad_latent,
        latent_gain_grad,
        grad_query,
        grad_pair,
        grad_out,
        feed_gain_grad,
    )
    halves = (
        lax.psum_scatter(attention_sums[0], "batch", scatter_dimension=0, tiled=True),
        lax.psum_scatter(attention_sums[1], "batch", scatter_dimension=0, tiled=True),
        lax.psum_scatter(attention_sums[2], "batch", scatter_dimension=0, tiled=True),
        lax.psum_scatter(attention_sums[3], "batch", scatter_dimension=0, tiled=True),
        lax.psum_scatter(attention_sums[4], "batch", scatter_dimension=0, tiled=True),
        lax.psum_scatter(attention_sums[5], "batch", scatter_dimension=0, tiled=True),
        lax.psum_scatter(attention_sums[6], "batch", scatter_dimension=0, tiled=True),
    )
    shares = (
        lax.psum(halves[0].astype(jnp.bfloat16), "hid").astype(jnp.float32),
        lax.psum(halves[1].astype(jnp.bfloat16), "hid").astype(jnp.float32),
        lax.psum(halves[2].astype(jnp.bfloat16), "hid").astype(jnp.float32),
        lax.psum(halves[3].astype(jnp.bfloat16), "hid").astype(jnp.float32),
        lax.psum(halves[4].astype(jnp.bfloat16), "hid").astype(jnp.float32),
        lax.psum(halves[5].astype(jnp.bfloat16), "hid").astype(jnp.float32),
        lax.psum(halves[6].astype(jnp.bfloat16), "hid").astype(jnp.float32),
    )
    return (
        output,
        grad_tokens,
        shares[0],
        shares[1],
        shares[2],
        shares[3],
        shares[4],
        shares[5],
        shares[6],
        ffn_shares[0],
        ffn_shares[1],
        ffn_shares[2],
    )


def solution(mesh):
    placed = (
        P(("batch", "hid"), None),
        P(("batch", "hid"), None),
        P("batch"),
        P("batch", None),
        P("batch"),
        P("batch", None),
        P("batch", None),
        P("batch", None),
        P("batch"),
        P("batch", "hid"),
        P("batch", "hid"),
        P("batch", "hid"),
        P(("batch", "hid"), None),
    )
    return jax.shard_map(
        per_device,
        mesh=mesh,
        in_specs=placed,
        out_specs=(
            P(("batch", "hid"), None),
            P(("batch", "hid"), None),
            P("batch"),
            P("batch", None),
            P("batch"),
            P("batch", None),
            P("batch", None),
            P("batch", None),
            P("batch"),
            P("batch", "hid"),
            P("batch", "hid"),
            P("batch", "hid"),
        ),
        check_vma=False,
    )
```

profile of v0, /device:TPU:0, one launch (start us, length us, event | category | flops | bytes accessed | tf_op | source)
XLA Modules:
  0.0 2199.5 jit_solution(3455538957978560829)
XLA Ops:
  10.6 23.1 %all-gather = bf16[16,1,128]{2,1,0:T(2,128)(2,1)S(1)} all-gather(bf16[1,1,128]{2,1,0:T(2,128)(2,1)} %bitcast.108), channel_id=1, replica_groups=mesh['batch'=16,'hid'=2] {'batch'}, dimensions={0}, use_global_device_ids=true | all-gather | bytes 4352 | tf_op jit(solution)/shard_map/all_gather | solution.py:76
  36.6 30.2 %all-reduce = bf16[1024]{0:T(1024)(128)(2,1)S(1)} all-reduce(bf16[1024]{0:T(1024)(128)(2,1)S(1)} %dynamic-update-slice), channel_id=1, replica_groups=mesh['batch'=16,'hid'=2] {'batch'}, use_global_device_ids=true, to_apply=%add | all-reduce | flops 1024 | bytes 4096
  68.3 17.3 all-gather.1
  90.5 15.6 all-gather.14.cloned.1.call-done
  109.1 72.6 %all-gather.16.cloned.1.call-done = bf16[1024,4096]{1,0:T(8,128)(2,1)} async-done(((bf16[64,4096]{1,0:T(8,128)(2,1)}), bf16[1024,4096]{1,0:T(8,128)(2,1)}) %all-gather.16.cloned.1.call-update) | async-done | bytes 8388624 | tf_op jit(solution)/shard_map/all_gather | solution.py:79
  190.0 118.9 %all-gather.18.cloned.1.call-done = bf16[2048,4096]{1,0:T(8,128)(2,1)} async-done(((bf16[128,4096]{1,0:T(8,128)(2,1)}), bf16[2048,4096]{1,0:T(8,128)(2,1)}) %all-gather.18.cloned.1.call-update) | async-done | bytes 16777232 | tf_op jit(solution)/shard_map/all_gather | solution.py:81
  308.9 11.5 multiply_reduce_fusion.3
  325.1 78.5 %all-gather.22.cloned.1.call-done = bf16[2048,2816]{1,0:T(8,128)(2,1)} async-done(((bf16[128,2816]{1,0:T(8,128)(2,1)}), bf16[2048,2816]{1,0:T(8,128)(2,1)}) %all-gather.22.cloned.1.call-update) | async-done | bytes 11534352 | tf_op jit(solution)/shard_map/all_gather | solution.py:85
  403.6 21.5 all-gather.20.cloned.1.call-done
  434.4 87.3 %all-gather.24.cloned.1.call-done = bf16[2048,2816]{1,0:T(8,128)(2,1)} async-done(((bf16[128,2816]{1,0:T(8,128)(2,1)}), bf16[2048,2816]{1,0:T(8,128)(2,1)}) %all-gather.24.cloned.1.call-update) | async-done | bytes 11534352 | tf_op jit(solution)/shard_map/all_gather | solution.py:86
  530.7 12.7 all-gather.28.cloned.1.call-done
  543.3 96.6 %all-gather.26.cloned.1.call-done = bf16[2048,2816]{1,0:T(8,128)(2,1)} async-done(((bf16[128,2816]{1,0:T(8,128)(2,1)}), bf16[2048,2816]{1,0:T(8,128)(2,1)}) %all-gather.26.cloned.1.call-update) | async-done | bytes 11534352 | tf_op jit(solution)/shard_map/all_gather | solution.py:87
  640.0 11.1 multiply_convert_fusion
  676.7 20.4 reduce-scatter.12.cloned.1.call-done
  699.2 21.2 reduce-scatter.10.cloned.1.call-done
  762.5 13.6 fusion.23
  776.2 33.3 %reduce-scatter.18.cloned.1.call-done = f32[128,512]{1,0:T(8,128)} async-done(((f32[2048,512]{1,0:T(8,128)}), f32[128,512]{1,0:T(8,128)}) %reduce-scatter.18.cloned.1.call-update) | async-done | bytes 262160 | tf_op jit(solution)/shard_map/reduce_scatter | solution.py:228
  811.1 106.8 %reduce-scatter.14.cloned.1.call-done = f32[128,1024]{1,0:T(8,128)} async-done(((f32[2048,1024]{1,0:T(8,128)}), f32[128,1024]{1,0:T(8,128)}) %reduce-scatter.14.cloned.1.call-update) | async-done | bytes 524304 | tf_op jit(solution)/shard_map/reduce_scatter | solution.py:225
  919.7 181.1 %reduce-scatter.16.cloned.1.call-done = f32[64,4096]{1,0:T(8,128)} async-done(((f32[1024,4096]{1,0:T(8,128)}), f32[64,4096]{1,0:T(8,128)}) %reduce-scatter.16.cloned.1.call-update) | async-done | bytes 1048592 | tf_op jit(solution)/shard_map/reduce_scatter | solution.py:227
  1102.8 334.4 %reduce-scatter.20.cloned.1.call-done = f32[128,4096]{1,0:T(8,128)} async-done(((f32[2048,4096]{1,0:T(8,128)}), f32[128,4096]{1,0:T(8,128)}) %reduce-scatter.20.cloned.1.call-update) | async-done | bytes 2097168 | tf_op jit(solution)/shard_map/reduce_scatter | solution.py:229
  1481.0 59.2 %all-reduce.4 = (bf16[2048]{0:T(1024)(128)(2,1)S(1)}, bf16[1024]{0:T(1024)(128)(2,1)S(1)}, bf16[2048]{0:T(1024)(128)(2,1)S(1)}) all-reduce(f32[2048]{0:T(1024)S(1)} %get-tuple-element.14, f32[1024]{0:T(1024)S(1)} %copy-done.29, f32[2048]{0:T(1024)S(1)} %copy-done.26), channel_id=4, replica_groups=mesh['batch'=16,'hid'=2] {'batch'}, use_global_device_ids=true, to_apply=%region_15.16.clone | all-reduce | flops 5120 | bytes 30720
  1553.7 177.6 %reduce-scatter.22.cloned.1.call-done = f32[128,2816]{1,0:T(8,128)} async-done(((f32[2048,2816]{1,0:T(8,128)}), f32[128,2816]{1,0:T(8,128)}) %reduce-scatter.22.cloned.1.call-update) | async-done | bytes 1441808 | tf_op jit(solution)/shard_map/reduce_scatter | solution.py:163
  1731.3 230.5 %reduce-scatter.24.cloned.1.call-done = f32[128,2816]{1,0:T(8,128)} async-done(((f32[2048,2816]{1,0:T(8,128)}), f32[128,2816]{1,0:T(8,128)}) %reduce-scatter.24.cloned.1.call-update) | async-done | bytes 1441808 | tf_op jit(solution)/shard_map/reduce_scatter | solution.py:164
  1961.8 230.7 %reduce-scatter.26.cloned.1.call-done = f32[128,2816]{1,0:T(8,128)} async-done(((f32[2048,2816]{1,0:T(8,128)}), f32[128,2816]{1,0:T(8,128)}) %reduce-scatter.26.cloned.1.call-update) | async-done | bytes 1441808 | tf_op jit(solution)/shard_map/reduce_scatter | solution.py:165
  (199 shorter events, 176.8 us)
Async XLA Ops:
  7.2 80.8 %all-gather.12.cloned.1.call-start = ((), (), s32[]{:S(2)}) async-start(), calls=%async_computation.9 | async-start | bytes 2228224 | tf_op jit(solution)/shard_map/all_gather | solution.py:80
  7.9 98.1 %all-gather.14.cloned.1.call-start = ((), (), s32[]{:S(2)}) async-start(), calls=%async_computation.10 | async-start | bytes 4456448 | tf_op jit(solution)/shard_map/all_gather | solution.py:77
  8.7 173.0 %all-gather.16.cloned.1.call-start = ((), (), s32[]{:S(2)}) async-start(), calls=%async_computation.11 | async-start | bytes 8912896 | tf_op jit(solution)/shard_map/all_gather | solution.py:79
  9.4 299.5 %all-gather.18.cloned.1.call-start = ((), (), s32[]{:S(2)}) async-start(), calls=%async_computation.12 | async-start | bytes 17825792 | tf_op jit(solution)/shard_map/all_gather | solution.py:81
  10.0 393.6 %all-gather.22.cloned.1.call-start = ((), (), s32[]{:S(2)}) async-start(), calls=%async_computation.14 | async-start | bytes 12255232 | tf_op jit(solution)/shard_map/all_gather | solution.py:85
  10.6 414.5 %all-gather.20.cloned.1.call-start = ((), (), s32[]{:S(2)}) async-start(), calls=%async_computation.13 | async-start | bytes 1572864 | tf_op jit(solution)/shard_map/all_gather | solution.py:117
  90.5 97.5 %copy-start.21 = (bf16[128,128]{1,0:T(8,128)(2,1)}, bf16[128,128]{1,0:T(8,128)(2,1)S(1)}, u32[]{:S(2)}) copy-start(bf16[128,128]{1,0:T(8,128)(2,1)S(1)} %get-tuple-element.39) | copy-start | bytes 98308
  90.5 97.5 %copy-start.23 = (bf16[128,128]{1,0:T(8,128)(2,1)}, bf16[128,128]{1,0:T(8,128)(2,1)S(1)}, u32[]{:S(2)}) copy-start(bf16[128,128]{1,0:T(8,128)(2,1)S(1)} %get-tuple-element.40) | copy-start | bytes 98308
  190.0 118.9 %copy-start.8 = (bf16[256,16,128]{2,0,1:T(8,128)(2,1)}, bf16[256,16,128]{2,0,1:T(8,128)(2,1)S(1)}, u32[]{:S(2)}) copy-start(bf16[256,16,128]{2,0,1:T(8,128)(2,1)S(1)} %convolution_convert_fusion.2) | copy-start | bytes 3145732
  321.4 200.3 %all-gather.24.cloned.1.call-start = ((), (), s32[]{:S(2)}) async-start(), calls=%async_computation.15 | async-start | bytes 12255232 | tf_op jit(solution)/shard_map/all_gather | solution.py:86
  322.1 221.2 %all-gather.28.cloned.1.call-start = ((), (), s32[]{:S(2)}) async-start(), calls=%async_computation.18 | async-start | bytes 1572864 | tf_op jit(solution)/shard_map/all_gather | solution.py:133
  322.8 397.5 %copy-start.30 = (pred[128]{0:T(512)(128)(4,1)}, pred[128]{0:T(512)(128)(4,1)S(1)}, u32[]{:S(2)}) copy-start(pred[128]{0:T(512)(128)(4,1)S(1)} %iota_compare_fusion.3) | copy-start | bytes 388
  323.8 316.1 %all-gather.26.cloned.1.call-start = ((), (), s32[]{:S(2)}) async-start(), calls=%async_computation.16 | async-start | bytes 12255232 | tf_op jit(solution)/shard_map/all_gather | solution.py:87
  324.6 372.6 %reduce-scatter.12.cloned.1.call-start = ((), (), s32[]{:S(2)}) async-start(), calls=%async_computation.19 | async-start | bytes 3145728 | tf_op jit(solution)/shard_map/reduce_scatter | solution.py:167
  667.0 53.4 %reduce-scatter.10.cloned.1.call-start = ((), (), s32[]{:S(2)}) async-start(), calls=%async_computation.17 | async-start | bytes 1572864 | tf_op jit(solution)/shard_map/reduce_scatter | solution.py:124
  676.7 132.8 %reduce-scatter.18.cloned.1.call-start = ((), (), s32[]{:S(2)}) async-start(), calls=%async_computation.22 | async-start | bytes 4456448 | tf_op jit(solution)/shard_map/reduce_scatter | solution.py:228
  736.7 181.2 %reduce-scatter.14.cloned.1.call-start = ((), (), s32[]{:S(2)}) async-start(), calls=%async_computation.20 | async-start | bytes 8912896 | tf_op jit(solution)/shard_map/reduce_scatter | solution.py:225
  753.0 347.7 %reduce-scatter.16.cloned.1.call-start = ((), (), s32[]{:S(2)}) async-start(), calls=%async_computation.21 | async-start | bytes 17825792 | tf_op jit(solution)/shard_map/reduce_scatter | solution.py:227
  761.3 675.9 %reduce-scatter.20.cloned.1.call-start = ((), (), s32[]{:S(2)}) async-start(), calls=%async_computation.23 | async-start | bytes 35651584 | tf_op jit(solution)/shard_map/reduce_scatter | solution.py:229
  776.1 772.2 %all-reduce.9.cloned.1.call-start = ((), (), s32[]{:S(2)}) async-start(), calls=%async_computation.27 | async-start | bytes 3932160 | tf_op jit(solution)/shard_map/psum | solution.py:234
  1102.8 337.2 %copy-start.5 = (bf16[256,2048]{1,0:T(8,128)(2,1)S(1)}, bf16[256,2048]{1,0:T(8,128)(2,1)}, u32[]{:S(2)}) copy-start(bf16[256,2048]{1,0:T(8,128)(2,1)} %all-gather.20.cloned.1.call-done) | copy-start | bytes 3145732
  1440.0 291.4 %reduce-scatter.22.cloned.1.call-start = ((), (), s32[]{:S(2)}) async-start(), calls=%async_computation.24 | async-start | bytes 24510464 | tf_op jit(solution)/shard_map/reduce_scatter | solution.py:163
  1451.1 510.7 %reduce-scatter.24.cloned.1.call-start = ((), (), s32[]{:S(2)}) async-start(), calls=%async_computation.25 | async-start | bytes 24510464 | tf_op jit(solution)/shard_map/reduce_scatter | solution.py:164
  1462.2 730.3 %reduce-scatter.26.cloned.1.call-start = ((), (), s32[]{:S(2)}) async-start(), calls=%async_computation.26 | async-start | bytes 24510464 | tf_op jit(solution)/shard_map/reduce_scatter | solution.py:165
  (35 other events, 648.9 us)
Sparse Core Ops, SparseCore 0:
  10.2 44.3 all-gather.11
  56.7 49.2 all-gather.13
  108.2 73.4 all-gather.15
  183.7 125.1 all-gather.17
  311.0 92.4 all-gather.21
  405.5 19.4 all-gather.19
  427.3 94.3 all-gather.23
  523.8 19.4 all-gather.27
  545.6 94.3 all-gather.25
  667.1 29.9 reduce-scatter.11
  700.0 20.3 reduce-scatter.9
  736.8 72.6 reduce-scatter.17
  814.1 103.7 reduce-scatter.13
  922.4 178.2 reduce-scatter.15
  1105.5 331.7 reduce-scatter.19
  1440.3 59.5 all-reduce.8
  1504.4 226.8 reduce-scatter.21
  1735.9 225.9 reduce-scatter.23
  1966.5 225.9 reduce-scatter.25
where the time goes:
time: 2210 us; the launch traced here: 2200 us
  waiting for transfers between devices  1840 us (83%)
  matrix products  161 us (7%)
  blocking collectives  135 us (6%)
  other arithmetic  29.9 us (1%)
    reduce_scatter x1, waiting for transfers between devices, per_device(): lax.psum_scatter(attention_sums[5], 'batch', scatter_dimension=0, tiled=T...  334 us
    reduce_scatter x1, waiting for transfers between devices, per_device(): lax.psum_scatter(grad_down, 'batch', scatter_dimension=0, tiled=True)  231 us
    reduce_scatter x1, waiting for transfers between devices, per_device(): lax.psum_scatter(grad_up, 'batch', scatter_dimension=0, tiled=True)  230 us
    reduce_scatter x1, waiting for transfers between devices, per_device(): lax.psum_scatter(attention_sums[3], 'batch', scatter_dimension=0, tiled=T...  181 us
    reduce_scatter x1, waiting for transfers between devices, per_device(): lax.psum_scatter(grad_gate, 'batch', scatter_dimension=0, tiled=True)  178 us
    dot_general x27, matrix products, matmul(): return jnp.einsum(spec, left, right, preferred_element_type=jnp.float32)  161 us
    all_gather x1, waiting for transfers between devices, per_device(): lax.all_gather(output_weight, 'batch', axis=0, tiled=True)  119 us
    reduce_scatter x1, waiting for transfers between devices, per_device(): lax.psum_scatter(attention_sums[1], 'batch', scatter_dimension=0, tiled=T...  107 us
  transfers between devices with their start and end apart: 19, of which 17 were waited for; matrix products, arithmetic and copies ran while one was open for 7% of the time, Pallas kernels for 0%

commit v1 on v0

--- a/solution.py
+++ b/solution.py
@@ -30,7 +30,8 @@
 
 
 def layout(row_lengths, count_rows):
-    ends = jnp.cumsum(row_lengths)
+    slots = jnp.arange(row_lengths.shape[0], dtype=jnp.int32)
+    ends = jnp.sum(jnp.where(slots[None, :] <= slots[:, None], row_lengths[None, :], 0), axis=1)
     starts = ends - row_lengths
     places = jnp.arange(count_rows, dtype=jnp.int32)
     segment = jnp.sum((places[:, None] >= ends[None, :]).astype(jnp.int32), axis=1)

time: 2210 us -> 2210 us (level)
  no operation moved by 1% of the time
where the time goes in v1:
time: 2210 us; the launch traced here: 2200 us
  waiting for transfers between devices  1840 us (83%)
  matrix products  161 us (7%)
  blocking collectives  135 us (6%)
  other arithmetic  29.9 us (1%)
    reduce_scatter x1, waiting for transfers between devices, per_device(): lax.psum_scatter(attention_sums[5], 'batch', scatter_dimension=0, tiled=T...  334 us
    reduce_scatter x1, waiting for transfers between devices, per_device(): lax.psum_scatter(grad_down, 'batch', scatter_dimension=0, tiled=True)  231 us
    reduce_scatter x1, waiting for transfers between devices, per_device(): lax.psum_scatter(grad_up, 'batch', scatter_dimension=0, tiled=True)  231 us
    reduce_scatter x1, waiting for transfers between devices, per_device(): lax.psum_scatter(attention_sums[3], 'batch', scatter_dimension=0, tiled=T...  181 us
    reduce_scatter x1, waiting for transfers between devices, per_device(): lax.psum_scatter(grad_gate, 'batch', scatter_dimension=0, tiled=True)  178 us
    dot_general x27, matrix products, matmul(): return jnp.einsum(spec, left, right, preferred_element_type=jnp.float32)  161 us
    all_gather x1, waiting for transfers between devices, per_device(): lax.all_gather(output_weight, 'batch', axis=0, tiled=True)  119 us
    reduce_scatter x1, waiting for transfers between devices, per_device(): lax.psum_scatter(attention_sums[1], 'batch', scatter_dimension=0, tiled=T...  107 us
  transfers between devices with their start and end apart: 19, of which 17 were waited for; matrix products, arithmetic and copies ran while one was open for 7% of the time, Pallas kernels for 0%

profile of v1, /device:TPU:0, one launch (start us, length us, event | category | flops | bytes accessed | tf_op | source)
XLA Modules:
  0.0 2199.1 jit_solution(62798269726382352)
XLA Ops:
  10.6 23.1 %all-gather = bf16[16,1,128]{2,1,0:T(2,128)(2,1)S(1)} all-gather(bf16[1,1,128]{2,1,0:T(2,128)(2,1)} %bitcast.104), channel_id=1, replica_groups=mesh['batch'=16,'hid'=2] {'batch'}, dimensions={0}, use_global_device_ids=true | all-gather | bytes 4352 | tf_op jit(solution)/shard_map/all_gather | solution.py:77
  36.6 30.2 %all-reduce = bf16[1024]{0:T(1024)(128)(2,1)S(1)} all-reduce(bf16[1024]{0:T(1024)(128)(2,1)S(1)} %dynamic-update-slice), channel_id=1, replica_groups=mesh['batch'=16,'hid'=2] {'batch'}, use_global_device_ids=true, to_apply=%add | all-reduce | flops 1024 | bytes 4096
  68.2 17.3 all-gather.1
  90.4 15.6 all-gather.14.cloned.1.call-done
  109.1 72.5 %all-gather.16.cloned.1.call-done = bf16[1024,4096]{1,0:T(8,128)(2,1)} async-done(((bf16[64,4096]{1,0:T(8,128)(2,1)}), bf16[1024,4096]{1,0:T(8,128)(2,1)}) %all-gather.16.cloned.1.call-update) | async-done | bytes 8388624 | tf_op jit(solution)/shard_map/all_gather | solution.py:80
  189.9 118.9 %all-gather.18.cloned.1.call-done = bf16[2048,4096]{1,0:T(8,128)(2,1)} async-done(((bf16[128,4096]{1,0:T(8,128)(2,1)}), bf16[2048,4096]{1,0:T(8,128)(2,1)}) %all-gather.18.cloned.1.call-update) | async-done | bytes 16777232 | tf_op jit(solution)/shard_map/all_gather | solution.py:82
  308.9 11.5 multiply_reduce_fusion.3
  325.0 78.5 %all-gather.22.cloned.1.call-done = bf16[2048,2816]{1,0:T(8,128)(2,1)} async-done(((bf16[128,2816]{1,0:T(8,128)(2,1)}), bf16[2048,2816]{1,0:T(8,128)(2,1)}) %all-gather.22.cloned.1.call-update) | async-done | bytes 11534352 | tf_op jit(solution)/shard_map/all_gather | solution.py:86
  403.5 21.5 all-gather.20.cloned.1.call-done
  434.4 87.3 %all-gather.24.cloned.1.call-done = bf16[2048,2816]{1,0:T(8,128)(2,1)} async-done(((bf16[128,2816]{1,0:T(8,128)(2,1)}), bf16[2048,2816]{1,0:T(8,128)(2,1)}) %all-gather.24.cloned.1.call-update) | async-done | bytes 11534352 | tf_op jit(solution)/shard_map/all_gather | solution.py:87
  530.6 12.7 all-gather.28.cloned.1.call-done
  543.3 96.6 %all-gather.26.cloned.1.call-done = bf16[2048,2816]{1,0:T(8,128)(2,1)} async-done(((bf16[128,2816]{1,0:T(8,128)(2,1)}), bf16[2048,2816]{1,0:T(8,128)(2,1)}) %all-gather.26.cloned.1.call-update) | async-done | bytes 11534352 | tf_op jit(solution)/shard_map/all_gather | solution.py:88
  639.9 11.1 multiply_convert_fusion
  676.7 20.4 reduce-scatter.12.cloned.1.call-done
  699.1 21.2 reduce-scatter.10.cloned.1.call-done
  762.5 13.6 fusion.23
  776.1 33.1 %reduce-scatter.18.cloned.1.call-done = f32[128,512]{1,0:T(8,128)} async-done(((f32[2048,512]{1,0:T(8,128)}), f32[128,512]{1,0:T(8,128)}) %reduce-scatter.18.cloned.1.call-update) | async-done | bytes 262160 | tf_op jit(solution)/shard_map/reduce_scatter | solution.py:229
  810.8 106.7 %reduce-scatter.14.cloned.1.call-done = f32[128,1024]{1,0:T(8,128)} async-done(((f32[2048,1024]{1,0:T(8,128)}), f32[128,1024]{1,0:T(8,128)}) %reduce-scatter.14.cloned.1.call-update) | async-done | bytes 524304 | tf_op jit(solution)/shard_map/reduce_scatter | solution.py:226
  919.3 181.1 %reduce-scatter.16.cloned.1.call-done = f32[64,4096]{1,0:T(8,128)} async-done(((f32[1024,4096]{1,0:T(8,128)}), f32[64,4096]{1,0:T(8,128)}) %reduce-scatter.16.cloned.1.call-update) | async-done | bytes 1048592 | tf_op jit(solution)/shard_map/reduce_scatter | solution.py:228
  1102.4 334.4 %reduce-scatter.20.cloned.1.call-done = f32[128,4096]{1,0:T(8,128)} async-done(((f32[2048,4096]{1,0:T(8,128)}), f32[128,4096]{1,0:T(8,128)}) %reduce-scatter.20.cloned.1.call-update) | async-done | bytes 2097168 | tf_op jit(solution)/shard_map/reduce_scatter | solution.py:230
  1480.6 59.3 %all-reduce.4 = (bf16[2048]{0:T(1024)(128)(2,1)S(1)}, bf16[1024]{0:T(1024)(128)(2,1)S(1)}, bf16[2048]{0:T(1024)(128)(2,1)S(1)}) all-reduce(f32[2048]{0:T(1024)S(1)} %get-tuple-element.14, f32[1024]{0:T(1024)S(1)} %copy-done.29, f32[2048]{0:T(1024)S(1)} %copy-done.26), channel_id=4, replica_groups=mesh['batch'=16,'hid'=2] {'batch'}, use_global_device_ids=true, to_apply=%region_15.16.clone | all-reduce | flops 5120 | bytes 30720
  1553.4 177.6 %reduce-scatter.22.cloned.1.call-done = f32[128,2816]{1,0:T(8,128)} async-done(((f32[2048,2816]{1,0:T(8,128)}), f32[128,2816]{1,0:T(8,128)}) %reduce-scatter.22.cloned.1.call-update) | async-done | bytes 1441808 | tf_op jit(solution)/shard_map/reduce_scatter | solution.py:164
  1731.0 230.5 %reduce-scatter.24.cloned.1.call-done = f32[128,2816]{1,0:T(8,128)} async-done(((f32[2048,2816]{1,0:T(8,128)}), f32[128,2816]{1,0:T(8,128)}) %reduce-scatter.24.cloned.1.call-update) | async-done | bytes 1441808 | tf_op jit(solution)/shard_map/reduce_scatter | solution.py:165
  1961.5 230.7 %reduce-scatter.26.cloned.1.call-done = f32[128,2816]{1,0:T(8,128)} async-done(((f32[2048,2816]{1,0:T(8,128)}), f32[128,2816]{1,0:T(8,128)}) %reduce-scatter.26.cloned.1.call-update) | async-done | bytes 1441808 | tf_op jit(solution)/shard_map/reduce_scatter | solution.py:166
  (199 shorter events, 176.8 us)
Async XLA Ops:
  7.2 80.8 %all-gather.12.cloned.1.call-start = ((), (), s32[]{:S(2)}) async-start(), calls=%async_computation.9 | async-start | bytes 2228224 | tf_op jit(solution)/shard_map/all_gather | solution.py:81
  7.9 98.1 %all-gather.14.cloned.1.call-start = ((), (), s32[]{:S(2)}) async-start(), calls=%async_computation.10 | async-start | bytes 4456448 | tf_op jit(solution)/shard_map/all_gather | solution.py:78
  8.7 173.0 %all-gather.16.cloned.1.call-start = ((), (), s32[]{:S(2)}) async-start(), calls=%async_computation.11 | async-start | bytes 8912896 | tf_op jit(solution)/shard_map/all_gather | solution.py:80
  9.4 299.4 %all-gather.18.cloned.1.call-start = ((), (), s32[]{:S(2)}) async-start(), calls=%async_computation.12 | async-start | bytes 17825792 | tf_op jit(solution)/shard_map/all_gather | solution.py:82
  10.0 393.5 %all-gather.22.cloned.1.call-start = ((), (), s32[]{:S(2)}) async-start(), calls=%async_computation.14 | async-start | bytes 12255232 | tf_op jit(solution)/shard_map/all_gather | solution.py:86
  10.6 414.4 %all-gather.20.cloned.1.call-start = ((), (), s32[]{:S(2)}) async-start(), calls=%async_computation.13 | async-start | bytes 1572864 | tf_op jit(solution)/shard_map/all_gather | solution.py:118
  90.4 97.5 %copy-start.21 = (bf16[128,128]{1,0:T(8,128)(2,1)}, bf16[128,128]{1,0:T(8,128)(2,1)S(1)}, u32[]{:S(2)}) copy-start(bf16[128,128]{1,0:T(8,128)(2,1)S(1)} %get-tuple-element.39) | copy-start | bytes 98308
  90.4 97.5 %copy-start.23 = (bf16[128,128]{1,0:T(8,128)(2,1)}, bf16[128,128]{1,0:T(8,128)(2,1)S(1)}, u32[]{:S(2)}) copy-start(bf16[128,128]{1,0:T(8,128)(2,1)S(1)} %get-tuple-element.40) | copy-start | bytes 98308
  189.9 118.9 %copy-start.8 = (bf16[256,16,128]{2,0,1:T(8,128)(2,1)}, bf16[256,16,128]{2,0,1:T(8,128)(2,1)S(1)}, u32[]{:S(2)}) copy-start(bf16[256,16,128]{2,0,1:T(8,128)(2,1)S(1)} %convolution_convert_fusion.2) | copy-start | bytes 3145732
  321.3 200.3 %all-gather.24.cloned.1.call-start = ((), (), s32[]{:S(2)}) async-start(), calls=%async_computation.15 | async-start | bytes 12255232 | tf_op jit(solution)/shard_map/all_gather | solution.py:87
  322.1 221.2 %all-gather.28.cloned.1.call-start = ((), (), s32[]{:S(2)}) async-start(), calls=%async_computation.18 | async-start | bytes 1572864 | tf_op jit(solution)/shard_map/all_gather | solution.py:134
  322.8 397.6 %copy-start.30 = (pred[128]{0:T(512)(128)(4,1)}, pred[128]{0:T(512)(128)(4,1)S(1)}, u32[]{:S(2)}) copy-start(pred[128]{0:T(512)(128)(4,1)S(1)} %iota_compare_fusion.4) | copy-start | bytes 388
  323.8 316.1 %all-gather.26.cloned.1.call-start = ((), (), s32[]{:S(2)}) async-start(), calls=%async_computation.16 | async-start | bytes 12255232 | tf_op jit(solution)/shard_map/all_gather | solution.py:88
  324.5 372.6 %reduce-scatter.12.cloned.1.call-start = ((), (), s32[]{:S(2)}) async-start(), calls=%async_computation.19 | async-start | bytes 3145728 | tf_op jit(solution)/shard_map/reduce_scatter | solution.py:168
  666.9 53.4 %reduce-scatter.10.cloned.1.call-start = ((), (), s32[]{:S(2)}) async-start(), calls=%async_computation.17 | async-start | bytes 1572864 | tf_op jit(solution)/shard_map/reduce_scatter | solution.py:125
  676.6 132.6 %reduce-scatter.18.cloned.1.call-start = ((), (), s32[]{:S(2)}) async-start(), calls=%async_computation.22 | async-start | bytes 4456448 | tf_op jit(solution)/shard_map/reduce_scatter | solution.py:229
  736.6 180.8 %reduce-scatter.14.cloned.1.call-start = ((), (), s32[]{:S(2)}) async-start(), calls=%async_computation.20 | async-start | bytes 8912896 | tf_op jit(solution)/shard_map/reduce_scatter | solution.py:226
  753.0 347.3 %reduce-scatter.16.cloned.1.call-start = ((), (), s32[]{:S(2)}) async-start(), calls=%async_computation.21 | async-start | bytes 17825792 | tf_op jit(solution)/shard_map/reduce_scatter | solution.py:228
  761.3 675.6 %reduce-scatter.20.cloned.1.call-start = ((), (), s32[]{:S(2)}) async-start(), calls=%async_computation.23 | async-start | bytes 35651584 | tf_op jit(solution)/shard_map/reduce_scatter | solution.py:230
  776.1 771.9 %all-reduce.9.cloned.1.call-start = ((), (), s32[]{:S(2)}) async-start(), calls=%async_computation.27 | async-start | bytes 3932160 | tf_op jit(solution)/shard_map/psum | solution.py:235
  1102.4 337.2 %copy-start.5 = (bf16[256,2048]{1,0:T(8,128)(2,1)S(1)}, bf16[256,2048]{1,0:T(8,128)(2,1)}, u32[]{:S(2)}) copy-start(bf16[256,2048]{1,0:T(8,128)(2,1)} %all-gather.20.cloned.1.call-done) | copy-start | bytes 3145732
  1439.5 291.4 %reduce-scatter.22.cloned.1.call-start = ((), (), s32[]{:S(2)}) async-start(), calls=%async_computation.24 | async-start | bytes 24510464 | tf_op jit(solution)/shard_map/reduce_scatter | solution.py:164
  1450.7 510.8 %reduce-scatter.24.cloned.1.call-start = ((), (), s32[]{:S(2)}) async-start(), calls=%async_computation.25 | async-start | bytes 24510464 | tf_op jit(solution)/shard_map/reduce_scatter | solution.py:165
  1461.8 730.4 %reduce-scatter.26.cloned.1.call-start = ((), (), s32[]{:S(2)}) async-start(), calls=%async_computation.26 | async-start | bytes 24510464 | tf_op jit(solution)/shard_map/reduce_scatter | solution.py:166
  (35 other events, 649.0 us)
Sparse Core Ops, SparseCore 0:
  10.2 44.3 all-gather.11
  56.7 49.2 all-gather.13
  108.2 73.3 all-gather.15
  183.7 125.1 all-gather.17
  311.0 92.4 all-gather.21
  405.5 19.4 all-gather.19
  427.3 94.3 all-gather.23
  523.7 19.4 all-gather.27
  545.6 94.3 all-gather.25
  667.0 29.9 reduce-scatter.11
  700.0 20.3 reduce-scatter.9
  736.7 72.4 reduce-scatter.17
  813.8 103.6 reduce-scatter.13
  922.0 178.2 reduce-scatter.15
  1105.0 331.7 reduce-scatter.19
  1439.8 59.6 all-reduce.8
  1504.1 226.8 reduce-scatter.21
  1735.5 225.9 reduce-scatter.23
  1966.2 225.9 reduce-scatter.25

commit v2 on v1

v2 whole, which is shorter than its diff:
```python
import functools

import jax
import jax.numpy as jnp
from jax import lax
from jax.experimental import pallas as pl
from jax.experimental.pallas import tpu as pltpu
from jax.sharding import PartitionSpec as P

HEADS = 16
HEAD_DIM = 256


EPS = 1e-05
ROPE_BASE = 10000.0
NEGATIVE = -1e30

QUAD = 4
PAIR = 2
GROUP = QUAD * PAIR
MESH = pl.DeviceIdType.MESH
BF = jnp.bfloat16
F32 = jnp.float32


def matmul(spec, left, right):
    return jnp.einsum(spec, left, right, preferred_element_type=F32)


def norm_rows(values, gain):
    return values * lax.rsqrt(jnp.mean(values * values, axis=-1, keepdims=True) + EPS) * gain


def rotate(values, cosine, sine):
    half = values.shape[-1] // 2
    first = values[..., :half]
    second = values[..., half:]
    return jnp.concatenate(
        [first * cosine - second * sine, second * cosine + first * sine], axis=-1
    )


def layout(row_lengths, count_rows):
    slots = jnp.arange(row_lengths.shape[0], dtype=jnp.int32)
    ends = jnp.sum(jnp.where(slots[None, :] <= slots[:, None], row_lengths[None, :], 0), axis=1)
    starts = ends - row_lengths
    places = jnp.arange(count_rows, dtype=jnp.int32)
    segment = jnp.sum((places[:, None] >= ends[None, :]).astype(jnp.int32), axis=1)
    begins = jnp.concatenate([starts, ends[-1:]])
    labels = jnp.arange(begins.shape[0], dtype=jnp.int32)
    firsts = jnp.sum(jnp.where(segment[:, None] == labels[None, :], begins[None, :], 0), axis=1)
    position = places - firsts
    valid = places < ends[-1]
    allowed = (segment[:, None] == segment[None, :]) & (places[None, :] <= places[:, None])
    return (position, valid, allowed)


def angles_of(position, head_size):
    half = head_size // 2
    freqs = ROPE_BASE ** (-(jnp.arange(half, dtype=F32) * 2.0) / head_size)
    angle = position.astype(F32)[..., None] * freqs
    return (jnp.cos(angle), jnp.sin(angle))


def place():
    batch = lax.axis_index("batch")
    quad = lax.rem(batch, QUAD)
    return batch - quad, quad, lax.axis_index("hid")


def flip(quad, bits):
    core = lax.rem(quad, 2)
    chip = quad - core
    if bits & 1:
        core = 1 - core
    if bits & 2:
        chip = 2 - chip
    return chip + core


def meet(peers):
    barrier = pltpu.get_barrier_semaphore()
    for peer in peers:
        pl.semaphore_signal(barrier, inc=1, device_id=peer, device_id_type=MESH)
    pl.semaphore_wait(barrier, len(peers))


def gather_kernel(count, put, *refs):
    ins, outs = refs[:count], refs[count : 2 * count]
    local_sem, send_sem, recv_sem = refs[2 * count :]
    base, quad, hid = place()

    def spot(f):
        bits, turn = f
        return (flip(quad, bits), 1 - hid if turn else hid)

    def address(f):
        q, h = spot(f)
        return (base + q, h)

    near = [(2, 1), (2, 0), (0, 1)]
    mate = (1, 0)
    meet([address(f) for f in near + [mate]])

    def mine(f):
        q, h = spot(f)
        return q * PAIR + h

    me = quad * PAIR + hid
    started = []
    for i in range(count):
        for j, f in enumerate(near):
            copy = pltpu.make_async_remote_copy(
                src_ref=ins[i],
                dst_ref=put(outs[i], me),
                send_sem=send_sem.at[i, j],
                recv_sem=recv_sem.at[i, j],
                device_id=address(f),
                device_id_type=MESH,
            )
            copy.start()
            started.append(copy)
        copy = pltpu.make_async_remote_copy(
            src_ref=ins[i],
            dst_ref=put(outs[i], me),
            send_sem=send_sem.at[i, 3],
            recv_sem=recv_sem.at[i, 3],
            device_id=address(mate),
            device_id_type=MESH,
        )
        copy.start()
        started.append(copy)
        copy = pltpu.make_async_copy(ins[i], put(outs[i], me), local_sem.at[i])
        copy.start()
    for i in range(count):
        for j in (1, 2, 0):
            f = near[j]
            where = put(outs[i], mine(f))
            pltpu.make_async_remote_copy(
                src_ref=ins[i],
                dst_ref=where,
                send_sem=send_sem.at[i, j],
                recv_sem=recv_sem.at[i, j],
                device_id=address(f),
                device_id_type=MESH,
            ).wait_recv()
            copy = pltpu.make_async_remote_copy(
                src_ref=where,
                dst_ref=where,
                send_sem=send_sem.at[i, 4 + j],
                recv_sem=recv_sem.at[i, 4 + j],
                device_id=address(mate),
                device_id_type=MESH,
            )
            copy.start()
            started.append(copy)
    for i in range(count):
        pltpu.make_async_copy(ins[i], put(outs[i], me), local_sem.at[i]).wait()
        for j, f in [(3, (1, 0))] + [(4 + j, (near[j][0] ^ 1, near[j][1])) for j in range(3)]:
            where = put(outs[i], mine(f))
            pltpu.make_async_remote_copy(
                src_ref=where,
                dst_ref=where,
                send_sem=send_sem.at[i, j],
                recv_sem=recv_sem.at[i, j],
                device_id=address(mate),
                device_id_type=MESH,
            ).wait_recv()
    for copy in started:
        copy.wait_send()


def gather_layer(arrays, ident, name):
    count = len(arrays)
    moved = sum(a.size * 2 * GROUP for a in arrays)
    return pl.pallas_call(
        functools.partial(gather_kernel, count, lambda ref, i: ref.at[i]),
        out_shape=[jax.ShapeDtypeStruct((GROUP,) + a.shape, a.dtype) for a in arrays],
        in_specs=[pl.BlockSpec(memory_space=pl.ANY)] * count,
        out_specs=[pl.BlockSpec(memory_space=pl.ANY)] * count,
        scratch_shapes=[
            pltpu.SemaphoreType.DMA((count,)),
            pltpu.SemaphoreType.DMA((count, 7)),
            pltpu.SemaphoreType.DMA((count, 7)),
        ],
        compiler_params=pltpu.CompilerParams(collective_id=ident, has_side_effects=True),
        cost_estimate=pl.CostEstimate(flops=0, bytes_accessed=16 * moved, transcendentals=0),
        name=name,
    )(*arrays)


def reduce_kernel(in_ref, out_ref, own, mate_in, sums, far_in, local_sem, send_sem, recv_sem):
    base, quad, hid = place()
    rows = out_ref.shape[0]
    ways = [(2, 1), (2, 0), (0, 1), (0, 0)]
    mate = (base + flip(quad, 1), hid)

    def address(f):
        return (base + flip(quad, f[0]), 1 - hid if f[1] else hid)

    def index(f, other):
        q = flip(quad, f[0] ^ (1 if other else 0))
        return q * PAIR + (1 - hid if f[1] else hid)

    meet([address(f) for f in ways[:3]] + [mate])
    to_mate, locals_, far = [], [], []
    for j, f in enumerate(ways):
        copy = pltpu.make_async_remote_copy(
            src_ref=in_ref.at[index(f, True)],
            dst_ref=mate_in.at[j],
            send_sem=send_sem.at[j],
            recv_sem=recv_sem.at[j],
            device_id=mate,
            device_id_type=MESH,
        )
        copy.start()
        to_mate.append(copy)
        copy = pltpu.make_async_copy(in_ref.at[index(f, False)], own.at[j], local_sem.at[j])
        copy.start()
        locals_.append(copy)
    step = 16
    for j, f in enumerate(ways[:3]):
        locals_[j].wait()
        to_mate[j].wait_recv()

        def add(r, carry, j=j):
            at = pl.ds(pl.multiple_of(r * step, step), step)
            sums[j, at, :] = (
                own[j, at, :].astype(F32) + mate_in[j, at, :].astype(F32)
            ).astype(BF)
            return carry

        lax.fori_loop(0, rows // step, add, 0)
        copy = pltpu.make_async_remote_copy(
            src_ref=sums.at[j],
            dst_ref=far_in.at[j],
            send_sem=send_sem.at[4 + j],
            recv_sem=recv_sem.at[4 + j],
            device_id=address(f),
            device_id_type=MESH,
        )
        copy.start()
        far.append(copy)
    locals_[3].wait()
    to_mate[3].wait_recv()
    for copy in far:
        copy.wait_recv()

    def total(r, carry):
        at = pl.ds(pl.multiple_of(r * step, step), step)
        out_ref[at, :] = (
            own[3, at, :].astype(F32)
            + mate_in[3, at, :].astype(F32)
            + far_in[0, at, :].astype(F32)
            + far_in[1, at, :].astype(F32)
            + far_in[2, at, :].astype(F32)
        )
        return carry

    lax.fori_loop(0, rows // step, total, 0)
    for copy in to_mate + far:
        copy.wait_send()


def reduce_layer(blocks, ident, name):
    rows, columns = blocks.shape[1:]
    return pl.pallas_call(
        reduce_kernel,
        out_shape=jax.ShapeDtypeStruct((rows, columns), F32),
        in_specs=[pl.BlockSpec(memory_space=pl.ANY)],
        out_specs=pl.BlockSpec(memory_space=pltpu.VMEM),
        scratch_shapes=[
            pltpu.VMEM((4, rows, columns), BF),
            pltpu.VMEM((4, rows, columns), BF),
            pltpu.VMEM((3, rows, columns), BF),
            pltpu.VMEM((3, rows, columns), BF),
            pltpu.SemaphoreType.DMA((4,)),
            pltpu.SemaphoreType.DMA((7,)),
            pltpu.SemaphoreType.DMA((7,)),
        ],
        compiler_params=pltpu.CompilerParams(
            collective_id=ident, has_side_effects=True, vmem_limit_bytes=48 * 2**20
        ),
        cost_estimate=pl.CostEstimate(
            flops=0, bytes_accessed=16 * blocks.size * 2, transcendentals=0
        ),
        name=name,
    )(blocks)


def swap_kernel(count, *refs):
    ins, outs = refs[:count], refs[count : 2 * count]
    local_sem, send_sem, recv_sem = refs[2 * count :]
    base, quad, hid = place()
    meet([(base + flip(quad, f), hid) for f in (1, 2, 3)])
    copies = []
    for i in range(count):
        for f in (2, 3, 1):
            copy = pltpu.make_async_remote_copy(
                src_ref=ins[i].at[flip(quad, f)],
                dst_ref=outs[i].at[quad],
                send_sem=send_sem.at[i, f - 1],
                recv_sem=recv_sem.at[i, f - 1],
                device_id=(base + flip(quad, f), hid),
                device_id_type=MESH,
            )
            copy.start()
            copies.append((copy, i, f))
        copy = pltpu.make_async_copy(ins[i].at[quad], outs[i].at[quad], local_sem.at[i])
        copy.start()
    for i in range(count):
        pltpu.make_async_copy(ins[i].at[quad], outs[i].at[quad], local_sem.at[i]).wait()
    for copy, i, f in copies:
        pltpu.make_async_remote_copy(
            src_ref=ins[i].at[flip(quad, f)],
            dst_ref=outs[i].at[flip(quad, f)],
            send_sem=send_sem.at[i, f - 1],
            recv_sem=recv_sem.at[i, f - 1],
            device_id=(base + flip(quad, f), hid),
            device_id_type=MESH,
        ).wait_recv()
    for copy, i, f in copies:
        copy.wait_send()


def swap_quad(arrays, ident, name):
    count = len(arrays)
    moved = sum(a.size * 2 for a in arrays)
    return pl.pallas_call(
        functools.partial(swap_kernel, count),
        out_shape=[jax.ShapeDtypeStruct(a.shape, a.dtype) for a in arrays],
        in_specs=[pl.BlockSpec(memory_space=pl.ANY)] * count,
        out_specs=[pl.BlockSpec(memory_space=pl.ANY)] * count,
        scratch_shapes=[
            pltpu.SemaphoreType.DMA((count,)),
            pltpu.SemaphoreType.DMA((count, 3)),
            pltpu.SemaphoreType.DMA((count, 3)),
        ],
        compiler_params=pltpu.CompilerParams(collective_id=ident, has_side_effects=True),
        cost_estimate=pl.CostEstimate(flops=0, bytes_accessed=32 * moved, transcendentals=0),
        name=name,
    )(*arrays)


def hops(layers, forward, first):
    pairs = []
    for z in range(layers - 1):
        if z < first:
            continue
        a, b = (z, z + 1) if forward else (layers - 1 - z, layers - 2 - z)
        pairs += [(a * QUAD + q, b * QUAD + q) for q in range(QUAD)]
    return pairs


def tail_hops(layers, forward, count):
    pairs = []
    for z in range(count):
        a, b = (z, z + 1) if forward else (layers - 1 - z, layers - 2 - z)
        pairs += [(a * QUAD + q, b * QUAD + q) for q in range(QUAD)]
    return pairs


def gather_chain(unit, layers):
    up, down = [unit], [unit]
    for k in range(1, layers):
        up.append(lax.ppermute(up[-1], "batch", hops(layers, True, k - 1)))
        down.append(lax.ppermute(down[-1], "batch", hops(layers, False, k - 1)))
    return [unit] + [down[k] + up[layers - k] for k in range(1, layers)]


def reduce_chain(slots, layers):
    totals = slots[0].astype(F32)
    for forward in (True, False):
        arrived = None
        for offset in range(layers - 1, 0, -1):
            slot = slots[offset] if forward else slots[layers - offset]
            if arrived is not None:
                slot = (slot.astype(F32) + arrived.astype(F32)).astype(BF)
            arrived = lax.ppermute(slot, "batch", tail_hops(layers, forward, layers - offset))
        if arrived is not None:
            totals = totals + arrived.astype(F32)
    return totals


def turn(values, start):
    return lax.dynamic_slice_in_dim(
        jnp.concatenate([values, values], axis=-1), start, values.shape[-1], axis=-1
    )


def per_device(
    layers,
    tokens,
    lengths,
    attention_gain,
    query_down,
    query_gain,
    query_up,
    key_value,
    output_weight,
    feed_gain,
    gate_weight,
    up_weight,
    down_weight,
    cotangent,
):
    count_rows, model = tokens.shape
    part, rank = query_down.shape
    rank_part = query_up.shape[0]
    half = part // PAIR
    pair_columns = key_value.shape[1]
    wide = rank + pair_columns
    all_rows = GROUP * count_rows
    heads = HEADS // GROUP
    head_columns = heads * HEAD_DIM
    units = gate_weight.shape[1] // QUAD
    scale = HEAD_DIM ** (-0.5)
    base, quad, hid = place()
    layer = base // QUAD
    me = quad * PAIR + hid
    span = QUAD * part
    rank_span = QUAD * rank_part

    first_pack = jnp.concatenate(
        [
            lax.dynamic_slice_in_dim(
                jnp.concatenate([query_down, key_value], axis=1), hid * half, half, axis=0
            ),
            jnp.pad(
                jnp.concatenate(
                    [attention_gain, query_gain, feed_gain, lengths[0].astype(BF)]
                )[None],
                ((0, 15), (0, wide - 2 * part - rank_part - lengths.shape[1])),
            ),
        ],
        axis=0,
    )
    first_slots = jnp.stack(gather_chain(first_pack, layers))
    own_heads = [
        lax.dynamic_slice_in_dim(
            jnp.concatenate([output_weight, query_up], axis=0).reshape(
                part + rank_part, QUAD, PAIR, head_columns
            ),
            hid,
            1,
            axis=2,
        )[:, :, 0]
        .transpose(1, 0, 2)
    ][0]
    feed_pack = jnp.concatenate(
        [w.reshape(part, QUAD, units) for w in (gate_weight, up_weight, down_weight)], axis=2
    ).transpose(1, 0, 2)
    head_unit, feed_unit = swap_quad([own_heads, feed_pack], 1, "swap_weights")
    head_slots = gather_chain(head_unit, layers)
    out_slice = jnp.stack([s[:, :part] for s in head_slots]).reshape(model, head_columns)
    query_slice = jnp.stack([s[:, part:] for s in head_slots]).reshape(rank, head_columns)
    feed_slots = gather_chain(feed_unit, layers)
    feed_all = jnp.stack(feed_slots).reshape(model, 3 * units)
    gate_up = feed_all[:, : 2 * units]
    down = feed_all[:, 2 * units :]

    [first_all] = gather_layer([first_slots], 2, "gather_first")
    first_all = first_all.transpose(1, 0, 2, 3)
    first_weight = first_all[:, :, :half].reshape(model, wide)
    small = first_all[:, :, half, :]
    first_gain = small[:, ::PAIR, :part].reshape(model).astype(F32)
    second_gain = small[:, ::PAIR, part : part + rank_part].reshape(rank).astype(F32)
    third_gain = (
        small[:, ::PAIR, part + rank_part : 2 * part + rank_part].reshape(model).astype(F32)
    )
    begin = 2 * part + rank_part
    all_lengths = small[0, :, begin : begin + lengths.shape[1]].astype(jnp.int32)

    inputs = turn(tokens, layer * span).astype(F32)
    upstream = turn(cotangent, layer * span).astype(F32)
    position, valid, allowed_own = layout(lengths[0], count_rows)
    cosine, sine = angles_of(position, HEAD_DIM)
    normed = norm_rows(inputs, first_gain).astype(BF)
    first = matmul("rd,de->re", normed, first_weight)
    latent = turn(first[:, :rank], layer * rank_span)
    keyvals = first[:, rank:]
    latent_normed = norm_rows(latent, second_gain).astype(BF)
    key_rot = rotate(keyvals[:, :HEAD_DIM], cosine, sine).astype(BF)
    value_rows = keyvals[:, HEAD_DIM:].astype(BF)
    [rows_all] = gather_layer(
        [jnp.concatenate([latent_normed, key_rot, value_rows], axis=1)], 3, "gather_latent"
    )
    latent_all = rows_all[:, :, :rank].reshape(all_rows, rank)
    key_all = rows_all[:, :, rank : rank + HEAD_DIM]
    value_all = rows_all[:, :, rank + HEAD_DIM :]

    positions, valids, allowed = jax.vmap(lambda one: layout(one, count_rows))(all_lengths)
    cosines, sines = angles_of(positions, HEAD_DIM)
    queries = matmul("rc,cf->rf", latent_all, query_slice).reshape(
        GROUP, count_rows, heads, HEAD_DIM
    )
    query_rot = rotate(queries, cosines[:, :, None, :], sines[:, :, None, :]).astype(BF)

    def masked_scores():
        raw = matmul("gqhd,gkd->ghqk", query_rot, key_all) * scale
        return jnp.where(allowed[:, None], raw, NEGATIVE)

    scores = masked_scores()
    highest = jnp.max(scores, axis=-1, keepdims=True)
    raised = jnp.exp(scores - highest)
    totals = jnp.sum(raised, axis=-1, keepdims=True)
    probs = (raised / totals).astype(BF)
    logsum = highest + jnp.log(totals)
    mixed = (
        matmul("ghqk,gkd->gqhd", probs, value_all).reshape(all_rows, head_columns).astype(BF)
    )
    branch_terms = matmul("rf,df->rd", mixed, out_slice).astype(BF)
    branch = reduce_layer(branch_terms.reshape(GROUP, count_rows, model), 4, "reduce_branch")
    middle = inputs + branch
    normed_ffn = norm_rows(middle, third_gain).astype(BF)
    kept = jnp.where(valid[:, None], upstream, 0.0)
    feed_rows, grad_rows, normed_rows = gather_layer(
        [normed_ffn, kept.astype(BF), normed], 5, "gather_feed"
    )
    feed_rows = feed_rows.reshape(all_rows, model)
    grad_rows = grad_rows.reshape(all_rows, model)
    normed_rows = normed_rows.reshape(all_rows, model)

    both = matmul("rd,df->rf", feed_rows, gate_up)
    gate, up = both[:, :units], both[:, units:]
    hidden_grad = matmul("rd,df->rf", grad_rows, down)
    sigma = jax.nn.sigmoid(gate)
    activated = gate * sigma
    slope = sigma * (1.0 + gate * (1.0 - sigma))
    hidden = (activated * up).astype(BF)
    both_grad = jnp.concatenate([hidden_grad * up * slope, hidden_grad * activated], axis=1).astype(
        BF
    )
    feed_terms = matmul("rf,df->rd", hidden, down).astype(BF)
    ffn_terms = matmul("rf,df->rd", both_grad, gate_up).astype(BF)
    sums = reduce_layer(
        jnp.concatenate([ffn_terms, feed_terms], axis=1).reshape(GROUP, count_rows, 2 * model),
        6,
        "reduce_feed",
    )
    ffn_grad, feed = sums[:, :model], sums[:, model:]
    grad_both = matmul("rd,rf->df", feed_rows, both_grad).astype(BF)
    grad_down = matmul("rd,rf->df", grad_rows, hidden).astype(BF)
    feed_grads = jnp.concatenate([grad_both, grad_down], axis=1).reshape(
        layers, QUAD, part, 3 * units
    )
    feed_sum = reduce_chain([feed_grads[k] for k in range(layers)], layers).astype(BF)

    output = turn(
        jnp.where(valid[:, None], middle + feed, inputs).astype(BF),
        lax.rem(model - layer * span, model),
    )
    unused_third, third_pull = jax.vjp(norm_rows, middle, third_gain)
    middle_norm_grad, feed_gain_grad = third_pull(ffn_grad)
    middle_grad = kept + middle_norm_grad
    [branch_rows] = gather_layer([middle_grad.astype(BF)], 7, "gather_branch")
    branch_rows = branch_rows.reshape(all_rows, model)

    grad_out = matmul("rd,rf->df", branch_rows, mixed).astype(BF)
    mixed_grad = (
        matmul("rd,df->rf", branch_rows, out_slice)
        .astype(BF)
        .reshape(GROUP, count_rows, heads, HEAD_DIM)
    )
    probs_back = jnp.exp(masked_scores() - logsum)
    prob_grad = matmul("gqhd,gkd->ghqk", mixed_grad, value_all)
    score_grad = (
        probs_back * (prob_grad - jnp.sum(probs_back * prob_grad, axis=-1, keepdims=True))
    ).astype(BF)
    value_terms = matmul("ghqk,gqhd->gkd", probs, mixed_grad)
    query_rot_grad = matmul("ghqk,gkd->gqhd", score_grad, key_all) * scale
    key_terms = matmul("ghqk,gqhd->gkd", score_grad, query_rot) * scale
    query_grad = (
        rotate(query_rot_grad, cosines[:, :, None, :], -sines[:, :, None, :])
        .reshape(all_rows, head_columns)
        .astype(BF)
    )
    grad_query = matmul("rc,rf->cf", latent_all, query_grad).astype(BF)
    latent_terms = matmul("rf,cf->rc", query_grad, query_slice)
    head_grads = [
        jnp.concatenate(
            [
                grad_out.reshape(layers, QUAD, part, head_columns)[k],
                grad_query.reshape(layers, QUAD, rank_part, head_columns)[k],
            ],
            axis=1,
        )
        for k in range(layers)
    ]
    head_sum = reduce_chain(head_grads, layers).astype(BF)
    back = reduce_layer(
        jnp.concatenate(
            [
                latent_terms.reshape(GROUP, count_rows, rank),
                key_terms,
                value_terms,
            ],
            axis=2,
        ).astype(BF),
        8,
        "reduce_latent",
    )

    latent_normed_grad = back[:, :rank]
    keyval_grad = jnp.concatenate(
        [rotate(back[:, rank : rank + HEAD_DIM], cosine, -sine), back[:, rank + HEAD_DIM :]], axis=1
    ).astype(BF)
    unused_second, second_pull = jax.vjp(norm_rows, latent, second_gain)
    latent_back, latent_gain_grad = second_pull(latent_normed_grad)
    latent_grad = turn(latent_back.astype(BF), lax.rem(rank - layer * rank_span, rank))
    first_grad = jnp.concatenate([latent_grad, keyval_grad], axis=1)
    normed_grad = matmul("re,de->rd", first_grad, first_weight)
    unused_first, first_pull = jax.vjp(norm_rows, inputs, first_gain)
    input_norm_grad, norm_gain_grad = first_pull(normed_grad)
    grad_tokens = turn(
        (middle_grad + input_norm_grad + jnp.where(valid[:, None], 0.0, upstream)).astype(BF),
        lax.rem(model - layer * span, model),
    )
    gains = jnp.concatenate([norm_gain_grad, feed_gain_grad, latent_gain_grad])
    gains = jnp.pad(gains.reshape(-1, rank), ((0, 16 - gains.size // rank), (0, wide - rank)))
    [grad_all] = gather_layer(
        [jnp.concatenate([first_grad, gains.astype(BF)], axis=0)], 9, "gather_last"
    )
    gain_sums = jnp.sum(grad_all[:, count_rows:, :rank].astype(F32), axis=0)
    lines = model // rank
    norm_sums = gain_sums[:lines].reshape(layers, span)
    feed_sums = gain_sums[lines : 2 * lines].reshape(layers, span)
    latent_sums = gain_sums[2 * lines].reshape(layers, rank_span)
    columns = wide // QUAD
    grad_slice = lax.dynamic_slice_in_dim(
        grad_all[:, :count_rows].reshape(all_rows, QUAD, columns), quad, 1, axis=1
    )[:, 0]
    half_rows = lax.dynamic_slice_in_dim(
        normed_rows.reshape(all_rows, layers * QUAD, PAIR, half), hid, 1, axis=2
    ).reshape(all_rows, model // PAIR)
    grad_first = matmul("rd,re->de", half_rows, grad_slice).astype(BF)
    small_sums = jnp.concatenate([norm_sums, feed_sums, latent_sums], axis=1)
    small_width = -(-small_sums.shape[1] // columns) * columns
    small_sums = jnp.pad(
        small_sums, ((0, 0), (0, small_width - small_sums.shape[1]))
    ).reshape(layers, -1, columns)
    small_sums = jnp.pad(small_sums, ((0, 0), (0, -small_sums.shape[1] % 16), (0, 0))).astype(BF)
    last_sum = reduce_chain(
        [
            jnp.concatenate(
                [grad_first.reshape(layers, QUAD * half, columns)[k], small_sums[k]], axis=0
            )
            for k in range(layers)
        ],
        layers,
    )
    first_sum = last_sum[: QUAD * half].reshape(QUAD, half, columns).astype(BF)
    small_sum = last_sum[QUAD * half :].reshape(-1)

    feed_own, head_own, first_own = swap_quad([feed_sum, head_sum, first_sum], 10, "swap_sums")
    feed_own = feed_own.transpose(1, 0, 2).astype(F32)
    grad_gate, grad_up, grad_down = (
        feed_own[:, :, i * units : (i + 1) * units].reshape(part, QUAD * units) for i in range(3)
    )
    head_half = head_own.transpose(1, 0, 2)
    first_half = first_own.transpose(1, 0, 2).reshape(half, wide)
    other_way = [(0, 1), (1, 0)]
    head_other = lax.ppermute(head_half, "hid", other_way)
    first_other = lax.ppermute(first_half, "hid", other_way)

    def sides(own, other, axis):
        low = jnp.where(hid == 0, own, other)
        high = jnp.where(hid == 0, other, own)
        return low, high

    low, high = sides(head_half, head_other, 2)
    head_full = (
        jnp.stack([low, high], axis=2).reshape(part + rank_part, HEADS * HEAD_DIM).astype(F32)
    )
    low, high = sides(first_half, first_other, 0)
    first_full = jnp.concatenate([low, high], axis=0).astype(F32)
    return (
        output,
        grad_tokens,
        lax.dynamic_slice_in_dim(small_sum, quad * part, part),
        first_full[:, :rank],
        lax.dynamic_slice_in_dim(small_sum, 2 * span + quad * rank_part, rank_part),
        head_full[part:],
        first_full[:, rank:],
        head_full[:part],
        lax.dynamic_slice_in_dim(small_sum, span + quad * part, part),
        grad_gate,
        grad_up,
        grad_down,
    )


def solution(mesh):
    placed = (
        P(("batch", "hid"), None),
        P(("batch", "hid"), None),
        P("batch"),
        P("batch", None),
        P("batch"),
        P("batch", None),
        P("batch", None),
        P("batch", None),
        P("batch"),
        P("batch", "hid"),
        P("batch", "hid"),
        P("batch", "hid"),
        P(("batch", "hid"), None),
    )
    return jax.shard_map(
        functools.partial(per_device, mesh.shape["batch"] // QUAD),
        mesh=mesh,
        in_specs=placed,
        out_specs=(
            P(("batch", "hid"), None),
            P(("batch", "hid"), None),
            P("batch"),
            P("batch", None),
            P("batch"),
            P("batch", None),
            P("batch", None),
            P("batch", None),
            P("batch"),
            P("batch", "hid"),
            P("batch", "hid"),
            P("batch", "hid"),
        ),
        check_vma=False,
    )
```

time: 2210 us -> 1010 us (0.46)
  waiting for transfers between devices: 1840 us -> 215 us
  Pallas kernels: 0 us -> 381 us
  blocking collectives: 135 us -> 0 us
  local copies, waits for them, and re-layouts: 10.2 us -> 134 us
  starting transfers between devices: 1.87 us -> 86.1 us
  matrix products: 161 us -> 81.2 us
  other arithmetic: 29.9 us -> 96.1 us
    reduce_scatter x9 -> x0, waiting for transfers between devices: 1340 us -> none  [the longest x1 334 us: per_device(): lax.psum_scatter(attention_sums[5], 'batch', scatter_dimension=0, tiled=T...]
    all_gather x9 -> x0, waiting for transfers between devices: 504 us -> none  [the longest x1 119 us: per_device(): lax.all_gather(output_weight, 'batch', axis=0, tiled=True)]
    pallas_call x0 -> x10, Pallas kernels: none -> 381 us  [the longest x5 203 us: gather_layer(): pl.pallas_call(functools.partial(gather_kernel, count, lambda ref, i: ref...]
    ppermute x0 -> x38, waiting for transfers between devices: none -> 215 us  [the longest x9 115 us: gather_chain(): down.append(lax.ppermute(down[-1], 'batch', hops(layers, False, k - 1)))]
    unnamed x2 -> x0, blocking collectives: 89.5 us -> none
    ppermute x0 -> x38, starting transfers between devices: none -> 86.1 us  [the longest x18 48.8 us: reduce_chain(): lax.ppermute(slot, 'batch', tail_hops(layers, forward, layers - offset))]
    dot_general x27 -> x21, matrix products: 161 us -> 81.2 us  [matmul(): return jnp.einsum(spec, left, right, preferred_element_type=F32)]
    all_gather x2 -> x0, blocking collectives: 40.4 us -> none  [the longest x1 23.1 us: per_device(): lax.all_gather(attention_gain, 'batch', axis=0, tiled=True)]
  transfers between devices with their start and end apart: 19 -> 38, of which waited for: 17 -> 8; matrix products, arithmetic and copies ran while one was open for 7% -> 18% of each run, Pallas kernels for 0% -> 24%
where the time goes in v2:
time: 1010 us; the launch traced here: 997 us
  Pallas kernels  381 us (38%)
  waiting for transfers between devices  215 us (21%)
  local copies, waits for them, and re-layouts  134 us (13%)
  other arithmetic  96.1 us (10%)
  starting transfers between devices  86.1 us (9%)
  matrix products  81.2 us (8%)
    pallas_call x5, Pallas kernels, gather_layer(): pl.pallas_call(functools.partial(gather_kernel, count, lambda ref, i: ref...  203 us
    ppermute x9, waiting for transfers between devices, gather_chain(): down.append(lax.ppermute(down[-1], 'batch', hops(layers, False, k - 1)))  115 us
    pallas_call x3, Pallas kernels, reduce_layer(): pl.pallas_call(reduce_kernel, out_shape=jax.ShapeDtypeStruct((rows, colum...  104 us
    ppermute x18, waiting for transfers between devices, reduce_chain(): lax.ppermute(slot, 'batch', tail_hops(layers, forward, layers - offset))  95.8 us
    dot_general x21, matrix products, matmul(): return jnp.einsum(spec, left, right, preferred_element_type=F32)  81.2 us
    pallas_call x2, Pallas kernels, swap_quad(): pl.pallas_call(functools.partial(swap_kernel, count), out_shape=[jax.Shap...  73.2 us
    ppermute x18, starting transfers between devices, reduce_chain(): lax.ppermute(slot, 'batch', tail_hops(layers, forward, layers - offset))  48.8 us
    ppermute x9, starting transfers between devices, gather_chain(): up.append(lax.ppermute(up[-1], 'batch', hops(layers, True, k - 1)))  23.5 us
  transfers between devices with their start and end apart: 38, of which 8 were waited for; matrix products, arithmetic and copies ran while one was open for 18% of the time, Pallas kernels for 24%

profile of v2, /device:TPU:0, one launch (start us, length us, event | category | flops | bytes accessed | tf_op | source)
XLA Modules:
  0.0 996.7 jit_solution(9660047735334189763)
XLA Ops:
  25.6 35.8 %swap_weights.1 = (bf16[4,192,512]{2,1,0:T(8,128)(2,1)}, bf16[4,128,2112]{2,1,0:T(8,128)(2,1)}) custom-call(bf16[4,192,512]{2,1,0:T(8,128)(2,1)} %bitcast.255, bf16[4,128,2112]{2,1,0:T(8,128)(2,1)} %bitcast.240), custom_call_target="tpu_custom_call" | custom-call | bytes 94371840 | tf_op jit(solution)/shard_map/swap_weights/pallas_call | solution.py:329
  84.3 7.6 collective-permute-done.4
  94.5 52.8 %collective-permute-done.5 = bf16[80,1536]{1,0:T(8,128)(2,1)S(1)} collective-permute-done((bf16[80,1536]{1,0:T(8,128)(2,1)S(1)}, bf16[80,1536]{1,0:T(8,128)(2,1)S(1)}, u32[]{:S(2)}, u32[]{:S(2)}) %collective-permute-start.5) | collective-permute-done | bytes 245792 | tf_op jit(solution)/shard_map/ppermute | solution.py:367
  151.0 50.8 %gather_first.1 = bf16[8,4,80,1536]{3,2,1,0:T(8,128)(2,1)} custom-call(bf16[4,80,1536]{2,1,0:T(8,128)(2,1)} %pad_maximum_fusion.13.refs_0_), custom_call_target="tpu_custom_call" | custom-call | bytes 125829120 | tf_op jit(solution)/shard_map/gather_first/pallas_call | solution.py:176
  226.8 17.2 %collective-permute-done.10 = bf16[4,192,512]{2,1,0:T(8,128)(2,1)S(1)} collective-permute-done((bf16[4,192,512]{2,1,0:T(8,128)(2,1)}, bf16[4,192,512]{2,1,0:T(8,128)(2,1)S(1)}, u32[]{:S(2)}, u32[]{:S(2)}) %collective-permute-start.10) | collective-permute-done | bytes 786464 | tf_op jit(solution)/shard_map/ppermute | solution.py:367
  245.6 23.3 %gather_latent.1 = bf16[8,128,1536]{2,1,0:T(8,128)(2,1)} custom-call(bf16[128,1536]{1,0:T(8,128)(2,1)} %pad_maximum_fusion.19.refs_0_), custom_call_target="tpu_custom_call" | custom-call | bytes 50331648 | tf_op jit(solution)/shard_map/gather_latent/pallas_call | solution.py:176
  290.8 37.2 %collective-permute-done.16 = bf16[4,128,2112]{1,2,0:T(8,128)(2,1)} collective-permute-done((bf16[4,128,2112]{1,2,0:T(8,128)(2,1)}, bf16[4,128,2112]{1,2,0:T(8,128)(2,1)}, u32[]{:S(2)}, u32[]{:S(2)}) %collective-permute-start.16) | collective-permute-done | bytes 2162720 | tf_op jit(solution)/shard_map/ppermute | solution.py:367
  332.0 28.5 %reduce_branch.1 = f32[128,2048]{1,0:T(8,128)S(1)} custom-call(bf16[8,128,2048]{2,1,0:T(8,128)(2,1)S(1)} %bitcast.222), custom_call_target="tpu_custom_call" | custom-call | bytes 67108864 | tf_op jit(solution)/shard_map/reduce_branch/pallas_call | solution.py:267
  361.8 74.6 %gather_feed.1 = (bf16[8,128,2048]{2,1,0:T(8,128)(2,1)}, bf16[8,128,2048]{2,1,0:T(8,128)(2,1)}, bf16[8,128,2048]{2,1,0:T(8,128)(2,1)}) custom-call(bf16[128,2048]{1,0:T(8,128)(2,1)} %multiply_convert_fusion.4.refs_0_, bf16[128,2048]{1,0:T(8,128)(2,1)} %get-tuple-element.82.refs_1_, bf16[128,2048]{1,0:T(8,128)(2,1)} %copy-done.14), custom_call_target="tpu_custom_call" | custom-call | bytes 201326592 | tf_op jit(solution)/shard_map/gather_feed/pallas_call | solution.py:176
  443.1 7.3 reshape_reshape.3
  477.6 8.2 fusion.2
  485.8 7.3 multiply_convert_fusion.2
  493.1 10.4 %convolution_convert_fusion = bf16[2048,1408]{0,1:T(8,128)(2,1)} fusion(bf16[1024,2048]{1,0:T(8,128)(2,1)S(1)} %bitcast.294, bf16[1024,704]{0,1:T(8,128)(2,1)} %get-tuple-element.93, bf16[1024,704]{0,1:T(8,128)(2,1)} %get-tuple-element.92), kind=kOutput, calls=%fused_computation.8 | convolution fusion | flops 5914230784 | bytes 12845056 | tf_op jit(solution)/shard_map/rd,rf->df/dot_general | solution.py:27
  503.5 8.4 fusion.6
  521.6 7.9 pad_maximum_fusion.1
  529.6 52.9 %reduce_feed.1 = f32[128,4096]{1,0:T(8,128)S(1)} custom-call(bf16[8,128,4096]{2,1,0:T(8,128)(2,1)} %bitcast.227), custom_call_target="tpu_custom_call" | custom-call | bytes 134217728 | tf_op jit(solution)/shard_map/reduce_feed/pallas_call | solution.py:267
  584.7 29.8 %gather_branch.1 = bf16[8,128,2048]{2,1,0:T(8,128)(2,1)} custom-call(bf16[128,2048]{1,0:T(8,128)(2,1)} %fusion.118.refs_0_), custom_call_target="tpu_custom_call" | custom-call | bytes 67108864 | tf_op jit(solution)/shard_map/gather_branch/pallas_call | solution.py:176
  638.6 23.0 %reduce_latent.1 = f32[128,1536]{1,0:T(8,128)S(1)} custom-call(bf16[8,128,1536]{2,1,0:T(8,128)(2,1)S(1)} %pad_maximum_fusion.2.in_ref), custom_call_target="tpu_custom_call" | custom-call | bytes 50331648 | tf_op jit(solution)/shard_map/reduce_latent/pallas_call | solution.py:267
  666.9 7.7 fusion.15
  705.4 24.9 %gather_last.1 = bf16[8,144,1536]{2,1,0:T(8,128)(2,1)} custom-call(bf16[144,1536]{1,0:T(8,128)(2,1)} %fusion.67.refs_0_), custom_call_target="tpu_custom_call" | custom-call | bytes 56623104 | tf_op jit(solution)/shard_map/gather_last/pallas_call | solution.py:176
  773.0 24.2 %collective-permute-done.25 = bf16[4,128,2112]{1,2,0:T(8,128)(2,1)} collective-permute-done((bf16[4,128,2112]{1,2,0:T(8,128)(2,1)}, bf16[4,128,2112]{1,2,0:T(8,128)(2,1)}, u32[]{:S(2)}, u32[]{:S(2)}) %collective-permute-start.25) | collective-permute-done | bytes 2162720 | tf_op jit(solution)/shard_map/ppermute | solution.py:379
  818.6 50.3 %collective-permute-done.19 = bf16[272,384]{1,0:T(8,128)(2,1)S(1)} collective-permute-done((bf16[272,384]{1,0:T(8,128)(2,1)S(1)}, bf16[272,384]{1,0:T(8,128)(2,1)S(1)}, u32[]{:S(2)}, u32[]{:S(2)}) %collective-permute-start.19) | collective-permute-done | bytes 208928 | tf_op jit(solution)/shard_map/ppermute | solution.py:379
  886.4 21.2 %collective-permute-done.23 = bf16[272,384]{1,0:T(8,128)(2,1)S(1)} collective-permute-done((bf16[272,384]{1,0:T(8,128)(2,1)S(1)}, bf16[272,384]{1,0:T(8,128)(2,1)S(1)}, u32[]{:S(2)}, u32[]{:S(2)}) %collective-permute-start.23) | collective-permute-done | bytes 208928 | tf_op jit(solution)/shard_map/ppermute | solution.py:379
  924.5 37.5 %swap_sums.1 = (bf16[4,128,2112]{2,1,0:T(8,128)(2,1)}, bf16[4,192,512]{2,1,0:T(8,128)(2,1)}, bf16[4,64,384]{2,1,0:T(8,128)(2,1)}) custom-call(bf16[4,128,2112]{2,1,0:T(8,128)(2,1)} %add_convert_fusion.refs_0_, bf16[4,192,512]{2,1,0:T(8,128)(2,1)} %add_convert_fusion.3.refs_1_, bf16[4,64,384]{2,1,0:T(8,128)(2,1)} %bitcast.275), custom_call_target="tpu_custom_call" | custom-call | bytes 100663296 | tf_op jit(solution)/shard_map/swap_sums/pallas_call | solution.py:329
  (451 shorter events, 344.8 us)
Async XLA Ops:
  3.8 77.6 %collective-permute-start = (bf16[80,1536]{1,0:T(8,128)(2,1)}, bf16[80,1536]{1,0:T(8,128)(2,1)}, u32[]{:S(2)}, u32[]{:S(2)}) collective-permute-start(bf16[80,1536]{1,0:T(8,128)(2,1)} %get-tuple-element.131), channel_id=1, source_target_pairs={{24,16},{26,18},{28,20},{30,22},{16,8},{18,10},{20,12},{22,14},{8,... | collective-permute-start | bytes 737288 | tf_op jit(solution)/shard_map/ppermute | solution.py:367
  5.1 77.6 %collective-permute-start.1 = (bf16[80,1536]{1,0:T(8,128)(2,1)}, bf16[80,1536]{1,0:T(8,128)(2,1)}, u32[]{:S(2)}, u32[]{:S(2)}) collective-permute-start(bf16[80,1536]{1,0:T(8,128)(2,1)} %get-tuple-element.131), channel_id=1, source_target_pairs={{0,8},{2,10},{4,12},{6,14},{8,16},{10,18},{12,20},{14,22},{16,24},... | collective-permute-start | bytes 737288 | tf_op jit(solution)/shard_map/ppermute | solution.py:366
  61.4 160.0 %collective-permute-start.7 = (bf16[4,192,512]{2,1,0:T(8,128)(2,1)}, bf16[4,192,512]{2,1,0:T(8,128)(2,1)}, u32[]{:S(2)}, u32[]{:S(2)}) collective-permute-start(bf16[4,192,512]{2,1,0:T(8,128)(2,1)} %get-tuple-element.20), channel_id=1, source_target_pairs={{0,8},{2,10},{4,12},{6,14},{8,16},{10,18},{12,20},{14,22},{16,24},... | collective-permute-start | bytes 2359304 | tf_op jit(solution)/shard_map/ppermute | solution.py:366
  65.0 157.1 %collective-permute-start.6 = (bf16[4,192,512]{2,1,0:T(8,128)(2,1)}, bf16[4,192,512]{2,1,0:T(8,128)(2,1)}, u32[]{:S(2)}, u32[]{:S(2)}) collective-permute-start(bf16[4,192,512]{2,1,0:T(8,128)(2,1)} %get-tuple-element.20), channel_id=1, source_target_pairs={{24,16},{26,18},{28,20},{30,22},{16,8},{18,10},{20,12},{22,14},{8,... | collective-permute-start | bytes 2359304 | tf_op jit(solution)/shard_map/ppermute | solution.py:367
  70.6 201.7 %collective-permute-start.13 = (bf16[4,128,2112]{1,2,0:T(8,128)(2,1)}, bf16[4,128,2112]{1,2,0:T(8,128)(2,1)}, u32[]{:S(2)}, u32[]{:S(2)}) collective-permute-start(bf16[4,128,2112]{1,2,0:T(8,128)(2,1)} %copy.210), channel_id=1, source_target_pairs={{0,8},{2,10},{4,12},{6,14},{8,16},{10,18},{12,20},{14,22},{16,24},... | collective-permute-start | bytes 6488072 | tf_op jit(solution)/shard_map/ppermute | solution.py:366
  91.8 182.4 %collective-permute-start.12 = (bf16[4,128,2112]{1,2,0:T(8,128)(2,1)}, bf16[4,128,2112]{1,2,0:T(8,128)(2,1)}, u32[]{:S(2)}, u32[]{:S(2)}) collective-permute-start(bf16[4,128,2112]{1,2,0:T(8,128)(2,1)} %copy.210), channel_id=1, source_target_pairs={{24,16},{26,18},{28,20},{30,22},{16,8},{18,10},{20,12},{22,14},{8,... | collective-permute-start | bytes 6488072 | tf_op jit(solution)/shard_map/ppermute | solution.py:367
  93.1 54.2 %collective-permute-start.5 = (bf16[80,1536]{1,0:T(8,128)(2,1)S(1)}, bf16[80,1536]{1,0:T(8,128)(2,1)S(1)}, u32[]{:S(2)}, u32[]{:S(2)}) collective-permute-start(bf16[80,1536]{1,0:T(8,128)(2,1)S(1)} %collective-permute-done.4), channel_id=1, source_target_pairs={{8,0},{10,2},{12,4},{14,6},{9,1},{11,3},{13,5},{15,7}} | collective-permute-start | bytes 737288 | tf_op jit(solution)/shard_map/ppermute | solution.py:367
  225.3 50.3 %collective-permute-start.9 = (bf16[4,192,512]{2,1,0:T(8,128)(2,1)S(1)}, bf16[4,192,512]{2,1,0:T(8,128)(2,1)}, u32[]{:S(2)}, u32[]{:S(2)}) collective-permute-start(bf16[4,192,512]{2,1,0:T(8,128)(2,1)S(1)} %collective-permute-done.8), channel_id=1, source_target_pairs={{16,24},{18,26},{20,28},{22,30},{17,25},{19,27},{21,29},{23,31}} | collective-permute-start | bytes 2359304 | tf_op jit(solution)/shard_map/ppermute | solution.py:366
  274.3 53.7 %collective-permute-start.16 = (bf16[4,128,2112]{1,2,0:T(8,128)(2,1)}, bf16[4,128,2112]{1,2,0:T(8,128)(2,1)}, u32[]{:S(2)}, u32[]{:S(2)}) collective-permute-start(bf16[4,128,2112]{1,2,0:T(8,128)(2,1)} %collective-permute-done.12), channel_id=1, source_target_pairs={{16,8},{18,10},{20,12},{22,14},{8,0},{10,2},{12,4},{14,6},{17,9},{... | collective-permute-start | bytes 6488072 | tf_op jit(solution)/shard_map/ppermute | solution.py:367
  288.8 170.3 %collective-permute-start.15 = (bf16[4,128,2112]{1,2,0:T(8,128)(2,1)}, bf16[4,128,2112]{1,2,0:T(8,128)(2,1)}, u32[]{:S(2)}, u32[]{:S(2)}) collective-permute-start(bf16[4,128,2112]{1,2,0:T(8,128)(2,1)} %collective-permute-done.14), channel_id=1, source_target_pairs={{16,24},{18,26},{20,28},{22,30},{17,25},{19,27},{21,29},{23,31}} | collective-permute-start | bytes 6488072 | tf_op jit(solution)/shard_map/ppermute | solution.py:366
  328.0 136.7 %collective-permute-start.17 = (bf16[4,128,2112]{1,2,0:T(8,128)(2,1)}, bf16[4,128,2112]{1,2,0:T(8,128)(2,1)}, u32[]{:S(2)}, u32[]{:S(2)}) collective-permute-start(bf16[4,128,2112]{1,2,0:T(8,128)(2,1)} %collective-permute-done.16), channel_id=1, source_target_pairs={{8,0},{10,2},{12,4},{14,6},{9,1},{11,3},{13,5},{15,7}} | collective-permute-start | bytes 6488072 | tf_op jit(solution)/shard_map/ppermute | solution.py:367
  678.4 63.1 %collective-permute-start.24 = (bf16[4,128,2112]{1,2,0:T(8,128)(2,1)}, bf16[4,128,2112]{1,2,0:T(8,128)(2,1)}, u32[]{:S(2)}, u32[]{:S(2)}) collective-permute-start(bf16[4,128,2112]{1,2,0:T(8,128)(2,1)} %bitcast.215), channel_id=1, source_target_pairs={{0,8},{2,10},{4,12},{6,14},{1,9},{3,11},{5,13},{7,15}} | collective-permute-start | bytes 6488072 | tf_op jit(solution)/shard_map/ppermute | solution.py:379
  685.1 56.3 %collective-permute-start.27 = (bf16[4,128,2112]{1,2,0:T(8,128)(2,1)}, bf16[4,128,2112]{1,2,0:T(8,128)(2,1)}, u32[]{:S(2)}, u32[]{:S(2)}) collective-permute-start(bf16[4,128,2112]{1,2,0:T(8,128)(2,1)} %bitcast.216), channel_id=1, source_target_pairs={{24,16},{26,18},{28,20},{30,22},{25,17},{27,19},{29,21},{31,23}} | collective-permute-start | bytes 6488072 | tf_op jit(solution)/shard_map/ppermute | solution.py:379
  700.0 69.1 %collective-permute-start.33 = (bf16[4,192,512]{2,1,0:T(8,128)(2,1)}, bf16[4,192,512]{2,1,0:T(8,128)(2,1)}, u32[]{:S(2)}, u32[]{:S(2)}) collective-permute-start(bf16[4,192,512]{2,1,0:T(8,128)(2,1)} %pad_maximum_fusion.14), channel_id=1, source_target_pairs={{24,16},{26,18},{28,20},{30,22},{25,17},{27,19},{29,21},{31,23}} | collective-permute-start | bytes 2359304 | tf_op jit(solution)/shard_map/ppermute | solution.py:379
  702.4 67.4 %collective-permute-start.30 = (bf16[4,192,512]{2,1,0:T(8,128)(2,1)}, bf16[4,192,512]{2,1,0:T(8,128)(2,1)}, u32[]{:S(2)}, u32[]{:S(2)}) collective-permute-start(bf16[4,192,512]{2,1,0:T(8,128)(2,1)} %pad_maximum_fusion.16), channel_id=1, source_target_pairs={{0,8},{2,10},{4,12},{6,14},{1,9},{3,11},{5,13},{7,15}} | collective-permute-start | bytes 2359304 | tf_op jit(solution)/shard_map/ppermute | solution.py:379
  748.1 49.1 %collective-permute-start.25 = (bf16[4,128,2112]{1,2,0:T(8,128)(2,1)}, bf16[4,128,2112]{1,2,0:T(8,128)(2,1)}, u32[]{:S(2)}, u32[]{:S(2)}) collective-permute-start(bf16[4,128,2112]{1,2,0:T(8,128)(2,1)} %get-tuple-element.98), channel_id=1, source_target_pairs={{0,8},{2,10},{4,12},{6,14},{8,16},{10,18},{12,20},{14,22},{1,9},{3... | collective-permute-start | bytes 6488072 | tf_op jit(solution)/shard_map/ppermute | solution.py:379
  754.7 45.6 %collective-permute-start.28 = (bf16[4,128,2112]{1,2,0:T(8,128)(2,1)}, bf16[4,128,2112]{1,2,0:T(8,128)(2,1)}, u32[]{:S(2)}, u32[]{:S(2)}) collective-permute-start(bf16[4,128,2112]{1,2,0:T(8,128)(2,1)} %get-tuple-element.99), channel_id=1, source_target_pairs={{24,16},{26,18},{28,20},{30,22},{16,8},{18,10},{20,12},{22,14},{25... | collective-permute-start | bytes 6488072 | tf_op jit(solution)/shard_map/ppermute | solution.py:379
  757.4 52.9 %collective-permute-start.18 = (bf16[272,384]{1,0:T(8,128)(2,1)}, bf16[272,384]{1,0:T(8,128)(2,1)}, u32[]{:S(2)}, u32[]{:S(2)}) collective-permute-start(bf16[272,384]{1,0:T(8,128)(2,1)} %pad_maximum_fusion.22), channel_id=1, source_target_pairs={{0,8},{2,10},{4,12},{6,14},{1,9},{3,11},{5,13},{7,15}} | collective-permute-start | bytes 626696 | tf_op jit(solution)/shard_map/ppermute | solution.py:379
  769.0 42.7 %collective-permute-start.21 = (bf16[272,384]{1,0:T(8,128)(2,1)S(1)}, bf16[272,384]{1,0:T(8,128)(2,1)S(1)}, u32[]{:S(2)}, u32[]{:S(2)}) collective-permute-start(bf16[272,384]{1,0:T(8,128)(2,1)S(1)} %pad_maximum_fusion.20), channel_id=1, source_target_pairs={{24,16},{26,18},{28,20},{30,22},{25,17},{27,19},{29,21},{31,23}} | collective-permute-start | bytes 626696 | tf_op jit(solution)/shard_map/ppermute | solution.py:379
  771.6 98.1 %collective-permute-start.31 = (bf16[4,192,512]{2,1,0:T(8,128)(2,1)S(1)}, bf16[4,192,512]{2,1,0:T(8,128)(2,1)S(1)}, u32[]{:S(2)}, u32[]{:S(2)}) collective-permute-start(bf16[4,192,512]{2,1,0:T(8,128)(2,1)S(1)} %get-tuple-element.120), channel_id=1, source_target_pairs={{0,8},{2,10},{4,12},{6,14},{8,16},{10,18},{12,20},{14,22},{1,9},{3... | collective-permute-start | bytes 2359304 | tf_op jit(solution)/shard_map/ppermute | solution.py:379
  797.2 78.8 %collective-permute-start.34 = (bf16[4,192,512]{2,1,0:T(8,128)(2,1)S(1)}, bf16[4,192,512]{2,1,0:T(8,128)(2,1)S(1)}, u32[]{:S(2)}, u32[]{:S(2)}) collective-permute-start(bf16[4,192,512]{2,1,0:T(8,128)(2,1)S(1)} %get-tuple-element.121), channel_id=1, source_target_pairs={{24,16},{26,18},{28,20},{30,22},{16,8},{18,10},{20,12},{22,14},{25... | collective-permute-start | bytes 2359304 | tf_op jit(solution)/shard_map/ppermute | solution.py:379
  800.2 112.0 %collective-permute-start.26 = (bf16[4,128,2112]{1,2,0:T(8,128)(2,1)S(1)}, bf16[4,128,2112]{1,2,0:T(8,128)(2,1)}, u32[]{:S(2)}, u32[]{:S(2)}) collective-permute-start(bf16[4,128,2112]{1,2,0:T(8,128)(2,1)S(1)} %add_convert_fusion.2), channel_id=1, source_target_pairs={{0,8},{2,10},{4,12},{6,14},{8,16},{10,18},{12,20},{14,22},{16,24},... | collective-permute-start | bytes 6488072 | tf_op jit(solution)/shard_map/ppermute | solution.py:379
  810.3 105.1 %collective-permute-start.29 = (bf16[4,128,2112]{1,2,0:T(8,128)(2,1)}, bf16[4,128,2112]{1,2,0:T(8,128)(2,1)}, u32[]{:S(2)}, u32[]{:S(2)}) collective-permute-start(bf16[4,128,2112]{1,2,0:T(8,128)(2,1)} %add_convert_fusion.1), channel_id=1, source_target_pairs={{24,16},{26,18},{28,20},{30,22},{16,8},{18,10},{20,12},{22,14},{8,... | collective-permute-start | bytes 6488072 | tf_op jit(solution)/shard_map/ppermute | solution.py:379
  812.8 56.1 %collective-permute-start.19 = (bf16[272,384]{1,0:T(8,128)(2,1)S(1)}, bf16[272,384]{1,0:T(8,128)(2,1)S(1)}, u32[]{:S(2)}, u32[]{:S(2)}) collective-permute-start(bf16[272,384]{1,0:T(8,128)(2,1)S(1)} %get-tuple-element.128), channel_id=1, source_target_pairs={{0,8},{2,10},{4,12},{6,14},{8,16},{10,18},{12,20},{14,22},{1,9},{3... | collective-permute-start | bytes 626696 | tf_op jit(solution)/shard_map/ppermute | solution.py:379
  (107 other events, 2547.3 us)

commit v3 on v2

v3 whole, which is shorter than its diff:
```python
import functools

import jax
import jax.numpy as jnp
from jax import lax
from jax.experimental import pallas as pl
from jax.experimental.pallas import tpu as pltpu
from jax.sharding import PartitionSpec as P

HEADS = 16
HEAD_DIM = 256


EPS = 1e-05
ROPE_BASE = 10000.0
NEGATIVE = -1e30

QUAD = 4
PAIR = 2
GROUP = QUAD * PAIR
EXTRA = 32
MESH = pl.DeviceIdType.MESH
BF = jnp.bfloat16
F32 = jnp.float32


def matmul(spec, left, right):
    return jnp.einsum(spec, left, right, preferred_element_type=F32)


def norm_rows(values, gain):
    return values * lax.rsqrt(jnp.mean(values * values, axis=-1, keepdims=True) + EPS) * gain


def rotate(values, cosine, sine):
    half = values.shape[-1] // 2
    first = values[..., :half]
    second = values[..., half:]
    return jnp.concatenate(
        [first * cosine - second * sine, second * cosine + first * sine], axis=-1
    )


def layout(row_lengths, count_rows):
    slots = jnp.arange(row_lengths.shape[0], dtype=jnp.int32)
    ends = jnp.sum(jnp.where(slots[None, :] <= slots[:, None], row_lengths[None, :], 0), axis=1)
    starts = ends - row_lengths
    places = jnp.arange(count_rows, dtype=jnp.int32)
    segment = jnp.sum((places[:, None] >= ends[None, :]).astype(jnp.int32), axis=1)
    begins = jnp.concatenate([starts, ends[-1:]])
    labels = jnp.arange(begins.shape[0], dtype=jnp.int32)
    firsts = jnp.sum(jnp.where(segment[:, None] == labels[None, :], begins[None, :], 0), axis=1)
    position = places - firsts
    valid = places < ends[-1]
    allowed = (segment[:, None] == segment[None, :]) & (places[None, :] <= places[:, None])
    return (position, valid, allowed)


def angles_of(position, head_size):
    half = head_size // 2
    freqs = ROPE_BASE ** (-(jnp.arange(half, dtype=F32) * 2.0) / head_size)
    angle = position.astype(F32)[..., None] * freqs
    return (jnp.cos(angle), jnp.sin(angle))


def place():
    batch = lax.axis_index("batch")
    quad = lax.rem(batch, QUAD)
    return batch - quad, quad, lax.axis_index("hid")


def flip(quad, bits):
    core = lax.rem(quad, 2)
    chip = quad - core
    if bits & 1:
        core = 1 - core
    if bits & 2:
        chip = 2 - chip
    return chip + core


def after(value, *others):
    return lax.optimization_barrier((value, *others))[0]


def meet(peers):
    barrier = pltpu.get_barrier_semaphore()
    for peer in peers:
        pl.semaphore_signal(barrier, inc=1, device_id=peer, device_id_type=MESH)
    pl.semaphore_wait(barrier, len(peers))


def ways_of(base, quad, hid):
    def spot(bits, turn):
        return (flip(quad, bits), 1 - hid if turn else hid)

    def address(f):
        q, h = spot(*f)
        return (base + q, h)

    def index(f):
        q, h = spot(*f)
        return q * PAIR + h

    return address, index


ACROSS, ALONG, CORNER, MATE, SELF = (2, 0), (0, 1), (2, 1), (1, 0), (0, 0)


def gather_kernel(count, cuts, puts, *refs):
    ins, outs = refs[:count], refs[count : 2 * count]
    local_sem, send_sem, recv_sem = refs[2 * count :]
    base, quad, hid = place()
    address, index = ways_of(base, quad, hid)
    meet([address(f) for f in (ACROSS, ALONG, MATE)])

    def part(ref, i, h):
        cut, size = cuts[i]
        return ref.at[pl.ds(0, cut)] if h == 0 else ref.at[pl.ds(cut, size - cut)]

    def spot(i, f):
        return puts[i](outs[i], index(f))

    def copy(i, j, source, target, f):
        return pltpu.make_async_remote_copy(
            src_ref=source,
            dst_ref=target,
            send_sem=send_sem.at[i, j],
            recv_sem=recv_sem.at[i, j],
            device_id=address(f),
            device_id_type=MESH,
        )

    started = []

    def start(one):
        one.start()
        started.append(one)

    for i in range(count):
        for j, f, h in ((0, ACROSS, 0), (3, ALONG, 1), (1, ACROSS, 1), (2, ALONG, 0)):
            start(copy(i, j, part(ins[i], i, h), part(spot(i, SELF), i, h), f))
        start(copy(i, 6, ins[i], spot(i, SELF), MATE))
        pltpu.make_async_copy(ins[i], spot(i, SELF), local_sem.at[i]).start()

    def arrived(i, j, where, f):
        copy(i, j, where, where, f).wait_recv()

    for i in range(count):
        where = part(spot(i, ACROSS), i, 0)
        arrived(i, 0, where, ACROSS)
        start(copy(i, 4, where, where, ALONG))
        where = part(spot(i, ALONG), i, 1)
        arrived(i, 3, where, ALONG)
        start(copy(i, 5, where, where, ACROSS))
        arrived(i, 1, part(spot(i, ACROSS), i, 1), ACROSS)
        where = spot(i, ACROSS)
        start(copy(i, 7, where, where, MATE))
        arrived(i, 2, part(spot(i, ALONG), i, 0), ALONG)
        where = spot(i, ALONG)
        start(copy(i, 8, where, where, MATE))
    for i in range(count):
        where = part(spot(i, CORNER), i, 0)
        arrived(i, 4, where, ALONG)
        start(copy(i, 9, where, where, MATE))
        where = part(spot(i, CORNER), i, 1)
        arrived(i, 5, where, ACROSS)
        start(copy(i, 10, where, where, MATE))
    for i in range(count):
        pltpu.make_async_copy(ins[i], spot(i, SELF), local_sem.at[i]).wait()
        arrived(i, 6, spot(i, MATE), MATE)
        arrived(i, 7, spot(i, (ACROSS[0] ^ 1, ACROSS[1])), MATE)
        arrived(i, 8, spot(i, (ALONG[0] ^ 1, ALONG[1])), MATE)
        corner = spot(i, (CORNER[0] ^ 1, CORNER[1]))
        arrived(i, 9, part(corner, i, 0), MATE)
        arrived(i, 10, part(corner, i, 1), MATE)
    for one in started:
        one.wait_send()


def stacked(ref, place):
    return ref.at[place]


def inside(ref, place):
    return ref.at[:, place]


def gather_layer(arrays, ident, name, puts=None):
    count = len(arrays)
    puts = puts or [stacked] * count
    shapes = [
        (GROUP,) + a.shape if p is stacked else (a.shape[0], GROUP) + a.shape[1:]
        for a, p in zip(arrays, puts)
    ]
    cuts = [
        (a.shape[0] // 2 if a.ndim > 2 else a.shape[0] // 32 * 16, a.shape[0]) for a in arrays
    ]
    moved = sum(a.size * 2 * GROUP for a in arrays)
    return pl.pallas_call(
        functools.partial(gather_kernel, count, cuts, puts),
        out_shape=[jax.ShapeDtypeStruct(s, a.dtype) for s, a in zip(shapes, arrays)],
        in_specs=[pl.BlockSpec(memory_space=pl.ANY)] * count,
        out_specs=[pl.BlockSpec(memory_space=pl.ANY)] * count,
        scratch_shapes=[
            pltpu.SemaphoreType.DMA((count,)),
            pltpu.SemaphoreType.DMA((count, 11)),
            pltpu.SemaphoreType.DMA((count, 11)),
        ],
        compiler_params=pltpu.CompilerParams(collective_id=ident, has_side_effects=True),
        cost_estimate=pl.CostEstimate(flops=0, bytes_accessed=16 * moved, transcendentals=0),
        name=name,
    )(*arrays)


def reduce_kernel(in_ref, out_ref, own, mate_in, sums, relay, far_in, local_sem, send_sem, recv_sem):
    base, quad, hid = place()
    address, index = ways_of(base, quad, hid)
    rows = out_ref.shape[0]
    half = rows // 2
    step = 16
    ways = [CORNER, ACROSS, ALONG, SELF]
    meet([address(f) for f in (ACROSS, ALONG, MATE)])
    started = []

    def copy(j, source, target, f):
        return pltpu.make_async_remote_copy(
            src_ref=source,
            dst_ref=target,
            send_sem=send_sem.at[j],
            recv_sem=recv_sem.at[j],
            device_id=address(f),
            device_id_type=MESH,
        )

    def start(one):
        one.start()
        started.append(one)
        return one

    to_mate, local = [], []
    for j, f in enumerate(ways):
        to_mate.append(start(copy(j, in_ref.at[index((f[0] ^ 1, f[1]))], mate_in.at[j], MATE)))
        local.append(pltpu.make_async_copy(in_ref.at[index(f)], own.at[j], local_sem.at[j]))
        local[-1].start()

    def ready(j):
        local[j].wait()
        to_mate[j].wait_recv()

    def add(j, first, count, more=None):
        def body(r, carry):
            at = pl.ds(pl.multiple_of(first + r * step, step), step)
            value = own[j, at, :].astype(F32) + mate_in[j, at, :].astype(F32)
            if more is not None:
                value += more[pl.ds(pl.multiple_of(r * step, step), step), :].astype(F32)
            sums[j, at, :] = value.astype(BF)
            return carry

        lax.fori_loop(0, count // step, body, 0)

    low, high = pl.ds(0, half), pl.ds(half, half)
    ready(0)
    add(0, 0, half)
    by_across = start(copy(4, sums.at[0, low], relay.at[0], ACROSS))
    add(0, half, half)
    by_along = start(copy(5, sums.at[0, high], relay.at[1], ALONG))
    ready(1)
    add(1, 0, half)
    across_low = start(copy(6, sums.at[1, low], far_in.at[0, low], ACROSS))
    ready(2)
    add(2, half, half)
    along_high = start(copy(7, sums.at[2, high], far_in.at[1, high], ALONG))
    by_across.wait_recv()
    add(2, 0, half, relay.at[0])
    along_low = start(copy(8, sums.at[2, low], far_in.at[1, low], ALONG))
    by_along.wait_recv()
    add(1, half, half, relay.at[1])
    across_high = start(copy(9, sums.at[1, high], far_in.at[0, high], ACROSS))
    ready(3)
    for one in (across_low, along_high, along_low, across_high):
        one.wait_recv()

    def total(r, carry):
        at = pl.ds(pl.multiple_of(r * step, step), step)
        out_ref[at, :] = (
            own[3, at, :].astype(F32)
            + mate_in[3, at, :].astype(F32)
            + far_in[0, at, :].astype(F32)
            + far_in[1, at, :].astype(F32)
        )
        return carry

    lax.fori_loop(0, rows // step, total, 0)
    for one in started:
        one.wait_send()


def reduce_layer(blocks, ident, name):
    rows, columns = blocks.shape[1:]
    return pl.pallas_call(
        reduce_kernel,
        out_shape=jax.ShapeDtypeStruct((rows, columns), F32),
        in_specs=[pl.BlockSpec(memory_space=pl.ANY)],
        out_specs=pl.BlockSpec(memory_space=pltpu.VMEM),
        scratch_shapes=[
            pltpu.VMEM((4, rows, columns), BF),
            pltpu.VMEM((4, rows, columns), BF),
            pltpu.VMEM((3, rows, columns), BF),
            pltpu.VMEM((2, rows // 2, columns), BF),
            pltpu.VMEM((2, rows, columns), BF),
            pltpu.SemaphoreType.DMA((4,)),
            pltpu.SemaphoreType.DMA((10,)),
            pltpu.SemaphoreType.DMA((10,)),
        ],
        compiler_params=pltpu.CompilerParams(
            collective_id=ident, has_side_effects=True, vmem_limit_bytes=40 * 2**20
        ),
        cost_estimate=pl.CostEstimate(
            flops=0, bytes_accessed=16 * blocks.size * 2, transcendentals=0
        ),
        name=name,
    )(blocks)


def swap_kernel(count, takes, puts, flips, *refs):
    ins, outs = refs[:count], refs[count : 2 * count]
    local_sem, send_sem, recv_sem = refs[2 * count :]
    base, quad, hid = place()
    address, index = ways_of(base, quad, hid)
    meet([address(f) for f in flips])

    def copy(i, j, f, owner):
        return pltpu.make_async_remote_copy(
            src_ref=takes[i](ins[i], index(f)),
            dst_ref=puts[i](outs[i], owner),
            send_sem=send_sem.at[i, j],
            recv_sem=recv_sem.at[i, j],
            device_id=address(f),
            device_id_type=MESH,
        )

    me = index(SELF)
    for i in range(count):
        for j, f in enumerate(flips):
            copy(i, j, f, me).start()
        pltpu.make_async_copy(takes[i](ins[i], me), puts[i](outs[i], me), local_sem.at[i]).start()
    for i in range(count):
        pltpu.make_async_copy(takes[i](ins[i], me), puts[i](outs[i], me), local_sem.at[i]).wait()
        for j, f in enumerate(flips):
            copy(i, j, f, index(f)).wait_recv()
    for i in range(count):
        for j, f in enumerate(flips):
            copy(i, j, f, me).wait_send()


QUAD_FLIPS = ((3, 0), (2, 0), (1, 0))
ALL_FLIPS = ((3, 1), (2, 1), (3, 0), (2, 0), (1, 1), (0, 1), (1, 0))


def swap(arrays, takes, puts, shapes, flips, ident, name):
    count = len(arrays)
    moved = sum(a.size * 2 for a in arrays)
    return pl.pallas_call(
        functools.partial(swap_kernel, count, takes, puts, flips),
        out_shape=[jax.ShapeDtypeStruct(s, a.dtype) for s, a in zip(shapes, arrays)],
        in_specs=[pl.BlockSpec(memory_space=pl.ANY)] * count,
        out_specs=[pl.BlockSpec(memory_space=pl.ANY)] * count,
        scratch_shapes=[
            pltpu.SemaphoreType.DMA((count,)),
            pltpu.SemaphoreType.DMA((count, len(flips))),
            pltpu.SemaphoreType.DMA((count, len(flips))),
        ],
        compiler_params=pltpu.CompilerParams(collective_id=ident, has_side_effects=True),
        cost_estimate=pl.CostEstimate(flops=0, bytes_accessed=32 * moved, transcendentals=0),
        name=name,
    )(*arrays)


def columns_of(width):
    return lambda ref, i: ref.at[:, pl.ds(pl.multiple_of(i * width, width), width)]


def quad_of(ref, i):
    return ref.at[i // PAIR]


def layer_groups(layers):
    return [[z * QUAD + q for z in range(layers)] for q in range(QUAD)]


def gather_layers(unit, layers):
    return lax.all_gather(
        unit, "batch", axis=0, tiled=True, axis_index_groups=layer_groups(layers)
    )


def reduce_layers(blocks, layers):
    return lax.psum_scatter(
        blocks,
        "batch",
        scatter_dimension=0,
        tiled=True,
        axis_index_groups=layer_groups(layers),
    )


def per_device(
    layers,
    tokens,
    lengths,
    attention_gain,
    query_down,
    query_gain,
    query_up,
    key_value,
    output_weight,
    feed_gain,
    gate_weight,
    up_weight,
    down_weight,
    cotangent,
):
    count_rows, model = tokens.shape
    part, rank = query_down.shape
    rank_part = query_up.shape[0]
    half = part // PAIR
    wide = rank + key_value.shape[1]
    all_rows = GROUP * count_rows
    heads = HEADS // GROUP
    head_columns = heads * HEAD_DIM
    units = gate_weight.shape[1] // QUAD
    cut = -(-units // 256) * 128
    chunks = [(0, cut), (cut, units)]
    scale = HEAD_DIM ** (-0.5)
    base, quad, hid = place()
    layer = base // QUAD
    me = quad * PAIR + hid
    span = QUAD * part
    rank_span = QUAD * rank_part

    first_pack = jnp.concatenate(
        [
            lax.dynamic_slice_in_dim(
                jnp.concatenate([query_down, key_value], axis=1), hid * half, half, axis=0
            ),
            jnp.pad(
                jnp.concatenate([attention_gain, query_gain, feed_gain, lengths[0].astype(BF)])[None],
                ((0, EXTRA - 1), (0, wide - 2 * part - rank_part - lengths.shape[1])),
            ),
        ],
        axis=0,
    )
    first_slots = gather_layers(first_pack, layers).reshape(layers, half + EXTRA, wide)
    out_unit, query_unit = swap(
        [output_weight, query_up],
        [columns_of(head_columns)] * 2,
        [quad_of] * 2,
        [(QUAD, part, head_columns), (QUAD, rank_part, head_columns)],
        QUAD_FLIPS,
        1,
        "swap_heads",
    )
    head_all = gather_layers(
        jnp.concatenate(
            [query_unit.reshape(rank_span, head_columns), out_unit.reshape(span, head_columns)]
        ),
        layers,
    ).reshape(layers, rank_span + span, head_columns)
    query_slice = head_all[:, :rank_span].reshape(rank, head_columns)
    out_slice = head_all[:, rank_span:].reshape(model, head_columns)
    packs = [
        jnp.concatenate(
            [
                w.reshape(part, QUAD, units)[:, :, low:high]
                for w in (gate_weight, up_weight, down_weight)
            ],
            axis=2,
        ).transpose(1, 0, 2)
        for low, high in chunks
    ]
    feed_units = swap(
        packs, [quad_of] * 2, [quad_of] * 2, [p.shape for p in packs], QUAD_FLIPS, 2, "swap_feed"
    )

    small_width = -(-(2 * part + rank_part + lengths.shape[1]) // 128) * 128
    first_weight, small = gather_layer(
        [first_slots[:, :half], first_slots[:, half : half + 16, :small_width]],
        3,
        "gather_first",
        [inside, stacked],
    )
    feed_weights = [
        gather_layers(feed_units[0].reshape(span, -1), layers),
        gather_layers(after(feed_units[1], first_weight).reshape(span, -1), layers),
    ]
    first_weight = first_weight.reshape(model, wide)
    small = small[:, :, 0].transpose(1, 0, 2)
    first_gain = small[:, ::PAIR, :part].reshape(model).astype(F32)
    second_gain = small[:, ::PAIR, part : part + rank_part].reshape(rank).astype(F32)
    third_gain = (
        small[:, ::PAIR, part + rank_part : 2 * part + rank_part].reshape(model).astype(F32)
    )
    begin = 2 * part + rank_part
    all_lengths = small[:, :, begin : begin + lengths.shape[1]].astype(jnp.int32)
    all_lengths = lax.dynamic_index_in_dim(all_lengths, layer, 0, keepdims=False)

    inputs = tokens.astype(F32)
    upstream = cotangent.astype(F32)
    position, valid, allowed_own = layout(lengths[0], count_rows)
    cosine, sine = angles_of(position, HEAD_DIM)
    normed = norm_rows(inputs, first_gain).astype(BF)
    first = matmul("rd,de->re", normed, first_weight)
    latent = first[:, :rank]
    keyvals = first[:, rank:]
    latent_normed = norm_rows(latent, second_gain).astype(BF)
    key_rot = rotate(keyvals[:, :HEAD_DIM], cosine, sine).astype(BF)
    value_rows = keyvals[:, HEAD_DIM:].astype(BF)
    [rows_all] = gather_layer(
        [jnp.concatenate([latent_normed, key_rot, value_rows], axis=1)], 4, "gather_latent"
    )
    latent_all = rows_all[:, :, :rank].reshape(all_rows, rank)
    key_all = rows_all[:, :, rank : rank + HEAD_DIM]
    value_all = rows_all[:, :, rank + HEAD_DIM :]

    positions, valids, allowed = jax.vmap(lambda one: layout(one, count_rows))(all_lengths)
    cosines, sines = angles_of(positions, HEAD_DIM)
    queries = matmul("rc,cf->rf", latent_all, query_slice).reshape(
        GROUP, count_rows, heads, HEAD_DIM
    )
    query_rot = rotate(queries, cosines[:, :, None, :], sines[:, :, None, :]).astype(BF)

    def masked_scores():
        raw = matmul("gqhd,gkd->ghqk", query_rot, key_all) * scale
        return jnp.where(allowed[:, None], raw, NEGATIVE)

    scores = masked_scores()
    highest = jnp.max(scores, axis=-1, keepdims=True)
    raised = jnp.exp(scores - highest)
    totals = jnp.sum(raised, axis=-1, keepdims=True)
    probs = (raised / totals).astype(BF)
    logsum = highest + jnp.log(totals)
    mixed = matmul("ghqk,gkd->gqhd", probs, value_all).reshape(all_rows, head_columns).astype(BF)
    branch_terms = matmul("rf,df->rd", mixed, out_slice).astype(BF)
    branch = reduce_layer(branch_terms.reshape(GROUP, count_rows, model), 5, "reduce_branch")
    middle = inputs + branch
    normed_ffn = norm_rows(middle, third_gain).astype(BF)
    kept = jnp.where(valid[:, None], upstream, 0.0)
    feed_rows, grad_rows = gather_layer([normed_ffn, kept.astype(BF)], 6, "gather_feed")
    feed_rows = feed_rows.reshape(all_rows, model)
    grad_rows = grad_rows.reshape(all_rows, model)

    feed_terms = jnp.zeros((all_rows, model), F32)
    ffn_terms = jnp.zeros((all_rows, model), F32)
    feed_sums = []
    for weights, (low, high) in zip(feed_weights, chunks):
        width = high - low
        gate_up, down = weights[:, : 2 * width], weights[:, 2 * width :]
        both = matmul("rd,df->rf", feed_rows, gate_up)
        gate, up = both[:, :width], both[:, width:]
        hidden_grad = matmul("rd,df->rf", grad_rows, down)
        sigma = jax.nn.sigmoid(gate)
        activated = gate * sigma
        slope = sigma * (1.0 + gate * (1.0 - sigma))
        hidden = (activated * up).astype(BF)
        both_grad = jnp.concatenate(
            [hidden_grad * up * slope, hidden_grad * activated], axis=1
        ).astype(BF)
        grad_both = matmul("rd,rf->df", feed_rows, both_grad).astype(BF)
        grad_down = matmul("rd,rf->df", grad_rows, hidden).astype(BF)
        grad_pack = jnp.concatenate([grad_both, grad_down], axis=1)
        feed_sums.append(reduce_layers(grad_pack, layers))
        feed_rows = after(feed_rows, grad_pack)
        both_grad = after(both_grad, grad_pack)
        ffn_terms = ffn_terms + matmul("rf,df->rd", both_grad, gate_up)
        feed_terms = feed_terms + matmul("rf,df->rd", hidden, down)
    ffn_grad = reduce_layer(
        ffn_terms.astype(BF).reshape(GROUP, count_rows, model), 7, "reduce_ffn_grad"
    )
    unused_third, third_pull = jax.vjp(norm_rows, middle, third_gain)
    middle_norm_grad, feed_gain_grad = third_pull(ffn_grad)
    middle_grad = kept + middle_norm_grad
    [branch_rows] = gather_layer([middle_grad.astype(BF)], 8, "gather_branch")
    branch_rows = branch_rows.reshape(all_rows, model)

    grad_out = matmul("rd,rf->df", branch_rows, mixed).astype(BF)
    mixed_grad = (
        matmul("rd,df->rf", branch_rows, out_slice)
        .astype(BF)
        .reshape(GROUP, count_rows, heads, HEAD_DIM)
    )
    probs_back = jnp.exp(masked_scores() - logsum)
    prob_grad = matmul("gqhd,gkd->ghqk", mixed_grad, value_all)
    score_grad = (
        probs_back * (prob_grad - jnp.sum(probs_back * prob_grad, axis=-1, keepdims=True))
    ).astype(BF)
    value_terms = matmul("ghqk,gqhd->gkd", probs, mixed_grad)
    query_rot_grad = matmul("ghqk,gkd->gqhd", score_grad, key_all) * scale
    key_terms = matmul("ghqk,gqhd->gkd", score_grad, query_rot) * scale
    query_grad = (
        rotate(query_rot_grad, cosines[:, :, None, :], -sines[:, :, None, :])
        .reshape(all_rows, head_columns)
        .astype(BF)
    )
    grad_query = matmul("rc,rf->cf", latent_all, query_grad).astype(BF)
    latent_terms = matmul("rf,cf->rc", query_grad, query_slice)
    head_pack = jnp.concatenate(
        [
            grad_query.reshape(layers, rank_span, head_columns),
            grad_out.reshape(layers, span, head_columns),
        ],
        axis=1,
    ).reshape(rank + model, head_columns)
    head_sum = reduce_layers(after(head_pack, *feed_sums), layers)
    query_sum, out_sum = head_sum[:rank_span], head_sum[rank_span:]
    back = reduce_layer(
        jnp.concatenate(
            [latent_terms.reshape(GROUP, count_rows, rank), key_terms, value_terms], axis=2
        ).astype(BF),
        9,
        "reduce_latent",
    )

    latent_normed_grad = back[:, :rank]
    keyval_grad = jnp.concatenate(
        [rotate(back[:, rank : rank + HEAD_DIM], cosine, -sine), back[:, rank + HEAD_DIM :]], axis=1
    ).astype(BF)
    unused_second, second_pull = jax.vjp(norm_rows, latent, second_gain)
    latent_back, latent_gain_grad = second_pull(latent_normed_grad)
    first_grad = jnp.concatenate([latent_back.astype(BF), keyval_grad], axis=1)
    normed_grad = matmul("re,de->rd", first_grad, first_weight)
    unused_first, first_pull = jax.vjp(norm_rows, inputs, first_gain)
    input_norm_grad, norm_gain_grad = first_pull(normed_grad)
    grad_tokens = (
        middle_grad + input_norm_grad + jnp.where(valid[:, None], 0.0, upstream)
    ).astype(BF)
    gains = jnp.concatenate([norm_gain_grad, feed_gain_grad, latent_gain_grad])
    gains = jnp.pad(gains.reshape(-1, rank), ((0, 16 - gains.size // rank), (0, wide - rank)))
    grad_all, normed_rows = gather_layer(
        [jnp.concatenate([first_grad, gains.astype(BF)], axis=0), normed], 10, "gather_last"
    )
    normed_rows = normed_rows.reshape(all_rows, model)
    gain_sums = jnp.sum(grad_all[:, count_rows:, :rank].astype(F32), axis=0)
    lines = model // rank
    columns = wide // QUAD
    grad_slice = lax.dynamic_slice_in_dim(
        grad_all[:, :count_rows].reshape(all_rows, wide), quad * columns, columns, axis=1
    )
    half_rows = lax.dynamic_index_in_dim(
        normed_rows.reshape(all_rows, layers * QUAD, PAIR, half), hid, 2, keepdims=False
    ).reshape(all_rows, model // PAIR)
    grad_first = matmul("rd,re->de", half_rows, grad_slice).astype(BF)
    small_sums = jnp.concatenate(
        [
            gain_sums[:lines].reshape(layers, span),
            gain_sums[lines : 2 * lines].reshape(layers, span),
            gain_sums[2 * lines].reshape(layers, rank_span),
        ],
        axis=1,
    )
    flat = 16 * columns
    small_sums = jnp.pad(small_sums, ((0, 0), (0, flat - small_sums.shape[1])))
    last_sum = reduce_layers(
        jnp.concatenate(
            [
                grad_first.reshape(layers, QUAD * half, columns),
                small_sums.reshape(layers, 16, columns).astype(BF),
            ],
            axis=1,
        ).reshape(layers * (QUAD * half + 16), columns),
        layers,
    )
    first_sum = last_sum[: QUAD * half].reshape(QUAD, half, columns)
    small_sum = last_sum[QUAD * half :].astype(F32).reshape(-1)

    feed_terms, grad_all = lax.optimization_barrier((feed_terms, grad_all))
    feed = reduce_layer(
        feed_terms.astype(BF).reshape(GROUP, count_rows, model), 11, "reduce_feed"
    )
    output = jnp.where(valid[:, None], middle + feed, inputs).astype(BF)

    feed_sums = [f.reshape(QUAD, part, -1) for f in feed_sums]
    feed_own = swap(
        feed_sums,
        [quad_of] * 2,
        [quad_of] * 2,
        [f.shape for f in feed_sums],
        QUAD_FLIPS,
        12,
        "swap_feed_sums",
    )
    out_own, query_own, first_own = swap(
        [
            out_sum.reshape(QUAD, part, head_columns),
            query_sum.reshape(QUAD, rank_part, head_columns),
            first_sum,
        ],
        [quad_of] * 3,
        [
            columns_of(head_columns),
            columns_of(head_columns),
            lambda ref, i: ref.at[
                pl.ds(pl.multiple_of(lax.rem(i, PAIR) * half, half), half),
                pl.ds(pl.multiple_of(i // PAIR * columns, columns), columns),
            ],
        ],
        [(part, HEADS * HEAD_DIM), (rank_part, HEADS * HEAD_DIM), (part, wide)],
        ALL_FLIPS,
        13,
        "swap_sums",
    )
    grads = []
    for i in range(3):
        pieces = [
            f[:, :, i * (high - low) : (i + 1) * (high - low)]
            for f, (low, high) in zip(feed_own, chunks)
        ]
        grads.append(
            jnp.concatenate(pieces, axis=2)
            .transpose(1, 0, 2)
            .reshape(part, QUAD * units)
            .astype(F32)
        )
    return (
        output,
        grad_tokens,
        lax.dynamic_slice_in_dim(small_sum, quad * part, part),
        first_own[:, :rank].astype(F32),
        lax.dynamic_slice_in_dim(small_sum, 2 * span + quad * rank_part, rank_part),
        query_own.astype(F32),
        first_own[:, rank:].astype(F32),
        out_own.astype(F32),
        lax.dynamic_slice_in_dim(small_sum, span + quad * part, part),
        *grads,
    )


def solution(mesh):
    placed = (
        P(("batch", "hid"), None),
        P(("batch", "hid"), None),
        P("batch"),
        P("batch", None),
        P("batch"),
        P("batch", None),
        P("batch", None),
        P("batch", None),
        P("batch"),
        P("batch", "hid"),
        P("batch", "hid"),
        P("batch", "hid"),
        P(("batch", "hid"), None),
    )
    return jax.shard_map(
        functools.partial(per_device, mesh.shape["batch"] // QUAD),
        mesh=mesh,
        in_specs=placed,
        out_specs=(
            P(("batch", "hid"), None),
            P(("batch", "hid"), None),
            P("batch"),
            P("batch", None),
            P("batch"),
            P("batch", None),
            P("batch", None),
            P("batch", None),
            P("batch"),
            P("batch", "hid"),
            P("batch", "hid"),
            P("batch", "hid"),
        ),
        check_vma=False,
    )
```

time: 1010 us -> 609 us (0.60)
  waiting for transfers between devices: 215 us -> 51.1 us
  starting transfers between devices: 86.1 us -> 0.55 us
  local copies, waits for them, and re-layouts: 134 us -> 72.4 us
  Pallas kernels: 381 us -> 326 us
  other arithmetic: 96.1 us -> 48.1 us
  between operations: 3.03 us -> 16.1 us
    ppermute x38 -> x0, waiting for transfers between devices: 215 us -> none  [the longest x9 115 us: gather_chain(): down.append(lax.ppermute(down[-1], 'batch', hops(layers, False, k - 1)))]
    ppermute x38 -> x0, starting transfers between devices: 86.1 us -> none  [the longest x18 48.8 us: reduce_chain(): lax.ppermute(slot, 'batch', tail_hops(layers, forward, layers - offset))]
    all_gather x0 -> x4, waiting for transfers between devices: none -> 51 us  [gather_layers(): lax.all_gather(unit, 'batch', axis=0, tiled=True, axis_index_groups=layer...]
    pallas_call x7 -> x9, Pallas kernels: 277 us -> 241 us  [the longest x5 149 us: gather_layer(): pl.pallas_call(functools.partial(gather_kernel, count, cuts, puts), out_s...]
    convert_element_type x20 -> x11, other arithmetic: 39.9 us -> 13.9 us  [the longest x1 2.76 us: per_device(): out_own.astype(F32)]
    pallas_call x3 -> x4, Pallas kernels: 104 us -> 84.8 us  [reduce_layer(): pl.pallas_call(reduce_kernel, out_shape=jax.ShapeDtypeStruct((rows, colum...]
    add x7 -> x0, other arithmetic: 13.6 us -> none  [the longest x6 13.5 us: gather_chain(): return [unit] + [down[k] + up[layers - k] for k in range(1, layers)]]
    reshape x10 -> x3, local copies, waits for them, and re-layouts: 11.9 us -> 0.03 us  [the longest x1 0.01 us: per_device(): gain_sums[:lines].reshape(layers, span)]
  transfers between devices with their start and end apart: 38 -> 8, of which waited for: 8 -> 1; matrix products, arithmetic and copies ran while one was open for 18% -> 28% of each run, Pallas kernels for 24% -> 50%
where the time goes in v3:
time: 609 us; the launch traced here: 602 us
  Pallas kernels  326 us (54%)
  matrix products  87.7 us (14%)
  local copies, waits for them, and re-layouts  72.4 us (12%)
  waiting for transfers between devices  51.1 us (8%)
  other arithmetic  48.1 us (8%)
  between operations  16.1 us (3%)
    pallas_call x5, Pallas kernels, gather_layer(): pl.pallas_call(functools.partial(gather_kernel, count, cuts, puts), out_s...  149 us
    pallas_call x4, Pallas kernels, swap(): pl.pallas_call(functools.partial(swap_kernel, count, takes, puts, flips),...  92.9 us
    dot_general x27, matrix products, matmul(): return jnp.einsum(spec, left, right, preferred_element_type=F32)  87.7 us
    pallas_call x4, Pallas kernels, reduce_layer(): pl.pallas_call(reduce_kernel, out_shape=jax.ShapeDtypeStruct((rows, colum...  84.8 us
    all_gather x4, waiting for transfers between devices, gather_layers(): lax.all_gather(unit, 'batch', axis=0, tiled=True, axis_index_groups=layer...  51 us
    unnamed x145, local copies, waits for them, and re-layouts  15.1 us
  transfers between devices with their start and end apart: 8, of which 1 were waited for; matrix products, arithmetic and copies ran while one was open for 28% of the time, Pallas kernels for 50%

profile of v3, /device:TPU:0, one launch (start us, length us, event | category | flops | bytes accessed | tf_op | source)
XLA Modules:
  0.0 602.3 jit_solution(12816648705610463617)
XLA Ops:
  10.5 13.2 %swap_heads.1 = (bf16[4,128,512]{2,1,0:T(8,128)(2,1)}, bf16[4,64,512]{2,1,0:T(8,128)(2,1)}) custom-call(bf16[128,4096]{1,0:T(8,128)(2,1)} %refs_0_.1, bf16[64,4096]{1,0:T(8,128)(2,1)} %refs_1_.1), custom_call_target="tpu_custom_call" | custom-call | bytes 50331648 | tf_op jit(solution)/shard_map/swap_heads/pallas_call | solution.py:365
  32.1 27.3 %swap_feed.1 = (bf16[4,128,1152]{2,1,0:T(8,128)(2,1)}, bf16[4,128,960]{2,1,0:T(8,128)(2,1)}) custom-call(bf16[4,128,1152]{2,1,0:T(8,128)(2,1)} %maximum_bitcast_fusion.refs_0_, bf16[4,128,960]{2,1,0:T(8,128)(2,1)} %maximum_bitcast_fusion.1.refs_1_), custom_call_target="tpu_custom_call" | custom-call | bytes 69206016 | tf_op jit(solution)/shard_map/swap_feed/pallas_call | solution.py:365
  65.6 32.9 %gather_first.1 = (bf16[4,8,64,1536]{3,2,1,0:T(8,128)(2,1)}, bf16[8,4,16,384]{3,2,1,0:T(8,128)(2,1)}) custom-call(bf16[4,64,1536]{2,1,0:T(8,128)(2,1)} %slice.243.refs_0_, bf16[4,16,384]{2,1,0:T(8,128)(2,1)} %slice.244.refs_1_), custom_call_target="tpu_custom_call" | custom-call | bytes 106954752 | tf_op jit(solution)/shard_map/gather_first/pallas_call | solution.py:201
  100.2 4.0 fusion.105
  105.6 17.9 %gather_latent.1 = bf16[8,128,1536]{2,1,0:T(8,128)(2,1)} custom-call(bf16[128,1536]{1,0:T(8,128)(2,1)} %pad_maximum_fusion.12.refs_0_), custom_call_target="tpu_custom_call" | custom-call | bytes 50331648 | tf_op jit(solution)/shard_map/gather_latent/pallas_call | solution.py:201
  144.6 22.4 %reduce_branch.1 = f32[128,2048]{1,0:T(8,128)S(1)} custom-call(bf16[8,128,2048]{2,1,0:T(8,128)(2,1)S(1)} %bitcast.173), custom_call_target="tpu_custom_call" | custom-call | bytes 67108864 | tf_op jit(solution)/shard_map/reduce_branch/pallas_call | solution.py:302
  168.4 38.9 %gather_feed.1 = (bf16[8,128,2048]{2,1,0:T(8,128)(2,1)}, bf16[8,128,2048]{2,1,0:T(8,128)(2,1)}) custom-call(bf16[128,2048]{1,0:T(8,128)(2,1)} %get-tuple-element.119.refs_0_, bf16[128,2048]{1,0:T(8,128)(2,1)} %get-tuple-element.118.refs_1_), custom_call_target="tpu_custom_call" | custom-call | bytes 134217728 | tf_op jit(solution)/shard_map/gather_feed/pallas_call | solution.py:201
  207.4 7.0 %fusion.2 = f32[1024,768]{0,1:T(8,128)S(1)} fusion(bf16[1024,2048]{1,0:T(8,128)(2,1)} %bitcast.232, bf16[2048,1152]{1,0:T(8,128)(2,1)} %all-gather.9.cloned.1.call-done), kind=kOutput, calls=%fused_computation.13 | convolution fusion | flops 3221225472 | bytes 10485760 | tf_op jit(solution)/shard_map/rd,df->rf/dot_general | solution.py:28
  214.4 3.9 multiply_convert_fusion.1
  221.1 4.3 convolution_convert_fusion.1
  227.9 50.9 %all-gather.11.cloned.1.call-done = bf16[2048,960]{1,0:T(8,128)(2,1)} async-done(((bf16[512,960]{1,0:T(8,128)(2,1)}), bf16[2048,960]{1,0:T(8,128)(2,1)}) %all-gather.11.cloned.1.call-update) | async-done | bytes 3932176 | tf_op jit(solution)/shard_map/all_gather | solution.py:394
  278.9 5.7 fusion.5
  299.8 6.5 %fusion = f32[1024,2048]{1,0:T(8,128)S(1)} fusion(bf16[1024,768]{0,1:T(8,128)(2,1)} %pad_maximum_fusion.4, bf16[2048,1152]{1,0:T(8,128)(2,1)} %all-gather.9.cloned.1.call-done), kind=kOutput, calls=%fused_computation.11 | convolution fusion | flops 3221225472 | bytes 13107200 | tf_op jit(solution)/shard_map/rf,df->rd/dot_general | solution.py:28
  310.1 22.2 %reduce_ffn_grad.1 = f32[128,2048]{1,0:T(8,128)S(1)} custom-call(bf16[8,128,2048]{2,1,0:T(8,128)(2,1)S(1)} %bitcast.172), custom_call_target="tpu_custom_call" | custom-call | bytes 67108864 | tf_op jit(solution)/shard_map/reduce_ffn_grad/pallas_call | solution.py:302
  334.6 22.4 %gather_branch.1 = bf16[8,128,2048]{2,1,0:T(8,128)(2,1)} custom-call(bf16[128,2048]{1,0:T(8,128)(2,1)} %fusion.99.refs_0_), custom_call_target="tpu_custom_call" | custom-call | bytes 67108864 | tf_op jit(solution)/shard_map/gather_branch/pallas_call | solution.py:201
  357.0 6.3 %convolution_convert_fusion.9 = bf16[1024,512]{1,0:T(8,128)(2,1)} fusion(bf16[1024,2048]{1,0:T(8,128)(2,1)} %bitcast.183, bf16[2048,512]{1,0:T(8,128)(2,1)} %bitcast.199), kind=kOutput, calls=%fused_computation.42 | convolution fusion | flops 2148007936 | bytes 7340032 | tf_op jit(solution)/shard_map/rd,df->rf/dot_general | solution.py:28
  379.8 17.9 %reduce_latent.1 = f32[128,1536]{1,0:T(8,128)S(1)} custom-call(bf16[8,128,1536]{2,1,0:T(8,128)(2,1)S(1)} %pad_maximum_fusion.2.in_ref), custom_call_target="tpu_custom_call" | custom-call | bytes 50331648 | tf_op jit(solution)/shard_map/reduce_latent/pallas_call | solution.py:302
  404.6 36.4 %gather_last.1 = (bf16[8,144,1536]{2,1,0:T(8,128)(2,1)}, bf16[8,128,2048]{2,1,0:T(8,128)(2,1)}) custom-call(bf16[144,1536]{1,0:T(8,128)(2,1)} %fusion.57.refs_0_, bf16[128,2048]{1,0:T(8,128)(2,1)} %copy-done.4), custom_call_target="tpu_custom_call" | custom-call | bytes 123731968 | tf_op jit(solution)/shard_map/gather_last/pallas_call | solution.py:201
  441.0 6.7 %copy.96 = bf16[8,128,2048]{1,0,2:T(8,128)(2,1)} copy(bf16[8,128,2048]{2,1,0:T(8,128)(2,1)} %get-tuple-element.47) | data formatting | bytes 8388608 | tf_op jit(solution)/shard_map/gather_last/pallas_call | solution.py:201
  447.7 7.5 %reshape_reshape.3 = bf16[1024,16,2,64]{0,3,2,1:T(8,128)(2,1)} reshape(bf16[8,128,2048]{1,0,2:T(8,128)(2,1)} %copy.96) | data formatting | bytes 8388608 | tf_op jit(solution)/shard_map/reshape;reshape | solution.py:651
  455.2 3.9 slice.226
  487.8 22.4 %reduce_feed.1 = f32[128,2048]{1,0:T(8,128)S(1)} custom-call(bf16[8,128,2048]{2,1,0:T(8,128)(2,1)S(1)} %bitcast.171), custom_call_target="tpu_custom_call" | custom-call | bytes 67108864 | tf_op jit(solution)/shard_map/reduce_feed/pallas_call | solution.py:302
  519.9 27.4 %swap_feed_sums.1 = (bf16[4,128,1152]{2,1,0:T(8,128)(2,1)}, bf16[4,128,960]{2,1,0:T(8,128)(2,1)}) custom-call(bf16[4,128,1152]{2,1,0:T(8,128)(2,1)} %bitcast.182, bf16[4,128,960]{2,1,0:T(8,128)(2,1)} %bitcast.187), custom_call_target="tpu_custom_call" | custom-call | bytes 69206016 | tf_op jit(solution)/shard_map/swap_feed_sums/pallas_call | solution.py:365
  562.7 24.9 %swap_sums.1 = (bf16[128,4096]{1,0:T(8,128)(2,1)}, bf16[64,4096]{1,0:T(8,128)(2,1)}, bf16[128,1536]{1,0:T(8,128)(2,1)}) custom-call(bf16[4,128,512]{2,1,0:T(8,128)(2,1)} %bitcast.203, bf16[4,64,512]{2,1,0:T(8,128)(2,1)} %bitcast.211, bf16[4,64,384]{2,1,0:T(8,128)(2,1)} %bitcast.214), custom_call_target="tpu_custom_call" | custom-call | bytes 31457280 | tf_op jit(solution)/shard_map/swap_sums/pallas_call | solution.py:365
  (311 shorter events, 153.3 us)
Async XLA Ops:
  7.2 54.9 %all-gather.5.cloned.1.call-start = ((), (), s32[]{:S(2)}) async-start(), calls=%async_computation.4 | async-start | bytes 1474560 | tf_op jit(solution)/shard_map/all_gather | solution.py:394
  10.4 117.4 %all-gather.7.cloned.1.call-start = ((), (), s32[]{:S(2)}) async-start(), calls=%async_computation.5 | async-start | bytes 3932160 | tf_op jit(solution)/shard_map/all_gather | solution.py:394
  25.9 181.5 %all-gather.9.cloned.1.call-start = ((), (), s32[]{:S(2)}) async-start(), calls=%async_computation.6 | async-start | bytes 5898240 | tf_op jit(solution)/shard_map/all_gather | solution.py:394
  30.9 28.6 %copy-start.62 = (s32[1,4]{1,0:T(1,128)S(1)}, s32[1,4]{1,0:T(1,128)}, u32[]{:S(2)}) copy-start(s32[1,4]{1,0:T(1,128)} %param.14) | copy-start | bytes 52
  30.9 30.9 %copy-start = (bf16[128,2048]{1,0:T(8,128)(2,1)S(1)}, bf16[128,2048]{1,0:T(8,128)(2,1)}, u32[]{:S(2)}) copy-start(bf16[128,2048]{1,0:T(8,128)(2,1)} %param.13) | copy-start | bytes 1572868
  59.4 219.5 %all-gather.11.cloned.1.call-start = ((), (), s32[]{:S(2)}) async-start(), calls=%async_computation.7 | async-start | bytes 5242880 | tf_op jit(solution)/shard_map/all_gather | solution.py:394
  60.2 64.3 %copy-start.47 = (f32[128]{0:T(128)}, f32[128]{0:T(128)S(1)}, u32[]{:S(2)}) copy-start(f32[128]{0:T(128)S(1)} %multiply_power_fusion) | copy-start | bytes 1540
  61.6 271.6 %copy-start.45 = (pred[128]{0:T(512)(128)(4,1)}, pred[128]{0:T(512)(128)(4,1)S(1)}, u32[]{:S(2)}) copy-start(pred[128]{0:T(512)(128)(4,1)S(1)} %iota_compare_fusion.9) | copy-start | bytes 388
  62.0 37.6 %copy-start.56 = (f32[128]{0:T(128)}, f32[128]{0:T(128)S(1)}, u32[]{:S(2)}) copy-start(f32[128]{0:T(128)S(1)} %fusion.33) | copy-start | bytes 1540
  62.0 42.2 %copy-start.49 = (f32[128]{0:T(128)}, f32[128]{0:T(128)S(1)}, u32[]{:S(2)}) copy-start(f32[128]{0:T(128)S(1)} %fusion.92) | copy-start | bytes 1540
  62.0 42.3 %copy-start.52 = (f32[128]{0:T(128)}, f32[128]{0:T(128)S(1)}, u32[]{:S(2)}) copy-start(f32[128]{0:T(128)S(1)} %subtract_convert_fusion.3) | copy-start | bytes 1540
  100.0 297.7 %copy-start.40 = (f32[1024]{0:T(1024)}, f32[1024]{0:T(1024)S(1)}, u32[]{:S(2)}) copy-start(f32[1024]{0:T(1024)S(1)} %reshape.370) | copy-start | bytes 12292
  104.4 293.3 %copy-start.44 = (f32[128]{0:T(128)}, f32[128]{0:T(128)S(1)}, u32[]{:S(2)}) copy-start(f32[128]{0:T(128)S(1)} %fusion.93) | copy-start | bytes 1540
  127.5 351.3 %reduce-scatter.9.cloned.1.call-start = ((), (), s32[]{:S(2)}) async-start(), calls=%async_computation.10 | async-start | bytes 4915200 | tf_op jit(solution)/shard_map/reduce_scatter | solution.py:400
  144.6 22.6 %copy-start.5 = (bf16[128,2048]{1,0:T(8,128)(2,1)S(1)}, bf16[128,2048]{1,0:T(8,128)(2,1)}, u32[]{:S(2)}) copy-start(bf16[128,2048]{1,0:T(8,128)(2,1)} %param.25) | copy-start | bytes 1572868
  167.3 166.0 %copy-start.42 = (f32[128]{0:T(128)}, f32[128]{0:T(128)S(1)}, u32[]{:S(2)}) copy-start(f32[128]{0:T(128)S(1)} %fusion.94) | copy-start | bytes 1540
  297.2 181.6 %reduce-scatter.7.cloned.1.call-start = ((), (), s32[]{:S(2)}) async-start(), calls=%async_computation.9 | async-start | bytes 5898240 | tf_op jit(solution)/shard_map/reduce_scatter | solution.py:400
  299.7 212.7 %reduce-scatter.5.cloned.1.call-start = ((), (), s32[]{:S(2)}) async-start(), calls=%async_computation.8 | async-start | bytes 1044480 | tf_op jit(solution)/shard_map/reduce_scatter | solution.py:400
  333.3 23.7 %copy-start.54 = (f32[128]{0:T(128)}, f32[128]{0:T(128)S(1)}, u32[]{:S(2)}) copy-start(f32[128]{0:T(128)S(1)} %multiply_multiply_fusion.2) | copy-start | bytes 1540
  465.5 93.7 %reduce-scatter.11.cloned.1.call-start = ((), (), s32[]{:S(2)}) async-start(), calls=%async_computation.11 | async-start | bytes 3932160 | tf_op jit(solution)/shard_map/reduce_scatter | solution.py:400
  487.7 22.5 %copy-start.7 = (bf16[128,2048]{1,0:T(8,128)(2,1)S(1)}, bf16[128,2048]{1,0:T(8,128)(2,1)}, u32[]{:S(2)}) copy-start(bf16[128,2048]{1,0:T(8,128)(2,1)} %param.25) | copy-start | bytes 1572868
  487.7 22.5 %copy-start.23 = (f32[128,2048]{1,0:T(8,128)S(1)}, f32[128,2048]{1,0:T(8,128)}, u32[]{:S(2)}) copy-start(f32[128,2048]{1,0:T(8,128)} %get-tuple-element.117) | copy-start | bytes 3145732
  487.8 22.5 %copy-start.43 = (f32[128]{0:T(128)S(1)}, f32[128]{0:T(128)}, u32[]{:S(2)}) copy-start(f32[128]{0:T(128)} %copy-done.42) | copy-start | bytes 1540
  487.8 22.5 %copy-start.46 = (pred[128]{0:T(512)(128)(4,1)S(1)}, pred[128]{0:T(512)(128)(4,1)}, u32[]{:S(2)}) copy-start(pred[128]{0:T(512)(128)(4,1)} %copy-done.45) | copy-start | bytes 388
  (50 other events, 337.0 us)
Sparse Core Ops, SparseCore 0:
  10.5 33.1 all-gather.4
  45.9 62.6 all-gather.6
  110.1 88.0 all-gather.8
  199.6 79.2 all-gather.10
  297.3 71.1 reduce-scatter.8
  370.7 85.5 reduce-scatter.6
  465.6 21.2 reduce-scatter.4
  489.3 59.3 reduce-scatter.10

commit v4 on v3

--- a/solution.py
+++ b/solution.py
@@ -553,7 +553,8 @@
 
     feed_terms = jnp.zeros((all_rows, model), F32)
     ffn_terms = jnp.zeros((all_rows, model), F32)
-    feed_sums = []
+    grad_packs = []
+    normed_rows = []
     for weights, (low, high) in zip(feed_weights, chunks):
         width = high - low
         gate_up, down = weights[:, : 2 * width], weights[:, 2 * width :]
@@ -570,8 +571,10 @@
         grad_both = matmul("rd,rf->df", feed_rows, both_grad).astype(BF)
         grad_down = matmul("rd,rf->df", grad_rows, hidden).astype(BF)
         grad_pack = jnp.concatenate([grad_both, grad_down], axis=1)
-        feed_sums.append(reduce_layers(grad_pack, layers))
-        feed_rows = after(feed_rows, grad_pack)
+        grad_packs.append(grad_pack)
+        if not normed_rows:
+            normed_rows = gather_layer([after(normed, grad_pack)], 15, "gather_normed")
+        feed_rows = after(feed_rows, grad_pack, normed_rows[0])
         both_grad = after(both_grad, grad_pack)
         ffn_terms = ffn_terms + matmul("rf,df->rd", both_grad, gate_up)
         feed_terms = feed_terms + matmul("rf,df->rd", hidden, down)
@@ -582,9 +585,9 @@
     middle_norm_grad, feed_gain_grad = third_pull(ffn_grad)
     middle_grad = kept + middle_norm_grad
     [branch_rows] = gather_layer([middle_grad.astype(BF)], 8, "gather_branch")
+    feed_sums = [reduce_layers(grad_packs[0], layers)]
     branch_rows = branch_rows.reshape(all_rows, model)
 
-    grad_out = matmul("rd,rf->df", branch_rows, mixed).astype(BF)
     mixed_grad = (
         matmul("rd,df->rf", branch_rows, out_slice)
         .astype(BF)
@@ -603,8 +606,15 @@
         .reshape(all_rows, head_columns)
         .astype(BF)
     )
-    grad_query = matmul("rc,rf->cf", latent_all, query_grad).astype(BF)
     latent_terms = matmul("rf,cf->rc", query_grad, query_slice)
+    back_terms = jnp.concatenate(
+        [latent_terms.reshape(GROUP, count_rows, rank), key_terms, value_terms], axis=2
+    ).astype(BF)
+    second_pack = after(grad_packs[1], feed_sums[0], back_terms)
+    feed_sums.append(reduce_layers(second_pack, layers))
+    back = reduce_layer(after(back_terms, second_pack), 9, "reduce_latent")
+    grad_query = matmul("rc,rf->cf", latent_all, after(query_grad, back)).astype(BF)
+    grad_out = matmul("rd,rf->df", after(branch_rows, back), mixed).astype(BF)
     head_pack = jnp.concatenate(
         [
             grad_query.reshape(layers, rank_span, head_columns),
@@ -612,15 +622,6 @@
         ],
         axis=1,
     ).reshape(rank + model, head_columns)
-    head_sum = reduce_layers(after(head_pack, *feed_sums), layers)
-    query_sum, out_sum = head_sum[:rank_span], head_sum[rank_span:]
-    back = reduce_layer(
-        jnp.concatenate(
-            [latent_terms.reshape(GROUP, count_rows, rank), key_terms, value_terms], axis=2
-        ).astype(BF),
-        9,
-        "reduce_latent",
-    )
 
     latent_normed_grad = back[:, :rank]
     keyval_grad = jnp.concatenate(
@@ -635,22 +636,32 @@
     grad_tokens = (
         middle_grad + input_norm_grad + jnp.where(valid[:, None], 0.0, upstream)
     ).astype(BF)
+    first_grad = after(first_grad, head_pack)
     gains = jnp.concatenate([norm_gain_grad, feed_gain_grad, latent_gain_grad])
     gains = jnp.pad(gains.reshape(-1, rank), ((0, 16 - gains.size // rank), (0, wide - rank)))
-    grad_all, normed_rows = gather_layer(
-        [jnp.concatenate([first_grad, gains.astype(BF)], axis=0), normed], 10, "gather_last"
-    )
-    normed_rows = normed_rows.reshape(all_rows, model)
+    [grad_all] = gather_layer(
+        [jnp.concatenate([first_grad, gains.astype(BF)], axis=0)], 10, "gather_last"
+    )
+    feed_terms = feed_terms.astype(BF)
+    feed = reduce_layer(
+        feed_terms.reshape(GROUP, count_rows, model), 11, "reduce_feed"
+    )
+    output = jnp.where(valid[:, None], middle + feed, inputs).astype(BF)
+
+    head_pack = after(head_pack, grad_all, feed_terms)
+    head_sum = reduce_layers(after(head_pack, *feed_sums), layers)
+    query_sum, out_sum = head_sum[:rank_span], head_sum[rank_span:]
+    normed_rows = normed_rows[0].reshape(all_rows, model)
     gain_sums = jnp.sum(grad_all[:, count_rows:, :rank].astype(F32), axis=0)
     lines = model // rank
     columns = wide // QUAD
     grad_slice = lax.dynamic_slice_in_dim(
         grad_all[:, :count_rows].reshape(all_rows, wide), quad * columns, columns, axis=1
     )
-    half_rows = lax.dynamic_index_in_dim(
-        normed_rows.reshape(all_rows, layers * QUAD, PAIR, half), hid, 2, keepdims=False
-    ).reshape(all_rows, model // PAIR)
-    grad_first = matmul("rd,re->de", half_rows, grad_slice).astype(BF)
+    grad_first = matmul("rd,re->de", normed_rows, grad_slice).astype(BF)
+    grad_first = lax.dynamic_index_in_dim(
+        grad_first.reshape(layers * QUAD, PAIR, half, columns), hid, 1, keepdims=False
+    )
     small_sums = jnp.concatenate(
         [
             gain_sums[:lines].reshape(layers, span),
@@ -661,61 +672,65 @@
     )
     flat = 16 * columns
     small_sums = jnp.pad(small_sums, ((0, 0), (0, flat - small_sums.shape[1])))
-    last_sum = reduce_layers(
-        jnp.concatenate(
-            [
-                grad_first.reshape(layers, QUAD * half, columns),
-                small_sums.reshape(layers, 16, columns).astype(BF),
-            ],
-            axis=1,
-        ).reshape(layers * (QUAD * half + 16), columns),
-        layers,
-    )
+    feed_sums = [f.reshape(QUAD, part, -1) for f in feed_sums]
+    quads = [[z * QUAD + q for q in range(QUAD)] for z in range(layers)]
+    feed_own = lax.all_to_all(
+        jnp.concatenate(feed_sums, axis=2), "batch", 0, 0, axis_index_groups=quads, tiled=True
+    )
+    last_pack = jnp.concatenate(
+        [
+            grad_first.reshape(layers, QUAD * half, columns),
+            small_sums.reshape(layers, 16, columns).astype(BF),
+        ],
+        axis=1,
+    ).reshape(layers * (QUAD * half + 16), columns)
+    last_sum = reduce_layers(after(after(last_pack, feed, feed_own), head_sum), layers)
     first_sum = last_sum[: QUAD * half].reshape(QUAD, half, columns)
     small_sum = last_sum[QUAD * half :].astype(F32).reshape(-1)
 
-    feed_terms, grad_all = lax.optimization_barrier((feed_terms, grad_all))
-    feed = reduce_layer(
-        feed_terms.astype(BF).reshape(GROUP, count_rows, model), 11, "reduce_feed"
-    )
-    output = jnp.where(valid[:, None], middle + feed, inputs).astype(BF)
-
-    feed_sums = [f.reshape(QUAD, part, -1) for f in feed_sums]
-    feed_own = swap(
-        feed_sums,
-        [quad_of] * 2,
-        [quad_of] * 2,
-        [f.shape for f in feed_sums],
-        QUAD_FLIPS,
-        12,
-        "swap_feed_sums",
-    )
-    out_own, query_own, first_own = swap(
+    groups = [[z * GROUP + i for i in range(GROUP)] for z in range(layers)]
+    head_own = lax.all_to_all(
+        jnp.repeat(
+            jnp.concatenate(
+                [
+                    query_sum.reshape(QUAD, rank_part, head_columns),
+                    out_sum.reshape(QUAD, part, head_columns),
+                ],
+                axis=1,
+            ),
+            PAIR,
+            axis=0,
+        ),
+        ("batch", "hid"),
+        0,
+        0,
+        axis_index_groups=groups,
+        tiled=True,
+    )
+    head_own = head_own.transpose(1, 0, 2).reshape(rank_part + part, HEADS * HEAD_DIM)
+    query_own, out_own = head_own[:rank_part], head_own[rank_part:]
+    [first_own] = swap(
+        [first_sum],
+        [quad_of],
         [
-            out_sum.reshape(QUAD, part, head_columns),
-            query_sum.reshape(QUAD, rank_part, head_columns),
-            first_sum,
-        ],
-        [quad_of] * 3,
-        [
-            columns_of(head_columns),
-            columns_of(head_columns),
             lambda ref, i: ref.at[
                 pl.ds(pl.multiple_of(lax.rem(i, PAIR) * half, half), half),
                 pl.ds(pl.multiple_of(i // PAIR * columns, columns), columns),
             ],
         ],
-        [(part, HEADS * HEAD_DIM), (rank_part, HEADS * HEAD_DIM), (part, wide)],
+        [(part, wide)],
         ALL_FLIPS,
-        13,
-        "swap_sums",
+        14,
+        "swap_last_sums",
     )
     grads = []
     for i in range(3):
-        pieces = [
-            f[:, :, i * (high - low) : (i + 1) * (high - low)]
-            for f, (low, high) in zip(feed_own, chunks)
-        ]
+        pieces = []
+        begin = 0
+        for low, high in chunks:
+            width = high - low
+            pieces.append(feed_own[:, :, begin + i * width : begin + (i + 1) * width])
+            begin += 3 * width
         grads.append(
             jnp.concatenate(pieces, axis=2)
             .transpose(1, 0, 2)

time: 609 us -> 577 us (0.947)
  Pallas kernels: 326 us -> 288 us
  matrix products: 87.7 us -> 103 us
  local copies, waits for them, and re-layouts: 72.4 us -> 61 us
  starting transfers between devices: 0.55 us -> 9.5 us
    pallas_call x4 -> x3, Pallas kernels: 92.9 us -> 49.2 us  [swap(): pl.pallas_call(functools.partial(swap_kernel, count, takes, puts, flips),...]
    all_gather x4, waiting for transfers between devices: 51 us -> 17.5 us  [gather_layers(): lax.all_gather(unit, 'batch', axis=0, tiled=True, axis_index_groups=layer...]
    all_to_all x0 -> x2, waiting for transfers between devices: none -> 29.1 us  [the longest x1 20.1 us: per_device(): lax.all_to_all(jnp.concatenate(feed_sums, axis=2), 'batch', 0, 0, axis_in...]
    dot_general x27, matrix products: 87.7 us -> 103 us  [matmul(): return jnp.einsum(spec, left, right, preferred_element_type=F32)]
    unnamed x145 -> x138, local copies, waits for them, and re-layouts: 15.1 us -> 25.7 us
    all_to_all x0 -> x2, starting transfers between devices: none -> 8.74 us  [the longest x1 4.46 us: per_device(): lax.all_to_all(jnp.concatenate(feed_sums, axis=2), 'batch', 0, 0, axis_in...]
    another operation x1 -> x0, local copies, waits for them, and re-layouts: 7.5 us -> none  [per_device(): normed_rows.reshape(all_rows, layers * QUAD, PAIR, half)]
    pallas_call x1 -> x0, local copies, waits for them, and re-layouts: 6.71 us -> none  [gather_layer(): pl.pallas_call(functools.partial(gather_kernel, count, cuts, puts), out_s...]
  transfers between devices with their start and end apart: 8 -> 10, of which waited for: 1 -> 3; matrix products, arithmetic and copies ran while one was open for 28% -> 33% of each run, Pallas kernels for 50% -> 49%
where the time goes in v4:
time: 577 us; the launch traced here: 570 us
  Pallas kernels  288 us (50%)
  matrix products  103 us (18%)
  local copies, waits for them, and re-layouts  61 us (11%)
  waiting for transfers between devices  46.7 us (8%)
  other arithmetic  46.3 us (8%)
  between operations  15.8 us (3%)
  starting transfers between devices  9.5 us (2%)
    pallas_call x6, Pallas kernels, gather_layer(): pl.pallas_call(functools.partial(gather_kernel, count, cuts, puts), out_s...  154 us
    dot_general x27, matrix products, matmul(): return jnp.einsum(spec, left, right, preferred_element_type=F32)  103 us
    pallas_call x4, Pallas kernels, reduce_layer(): pl.pallas_call(reduce_kernel, out_shape=jax.ShapeDtypeStruct((rows, colum...  85 us
    pallas_call x3, Pallas kernels, swap(): pl.pallas_call(functools.partial(swap_kernel, count, takes, puts, flips),...  49.2 us
    unnamed x138, local copies, waits for them, and re-layouts  25.7 us
    all_to_all x1, waiting for transfers between devices, per_device(): lax.all_to_all(jnp.concatenate(feed_sums, axis=2), 'batch', 0, 0, axis_in...  20.1 us
    all_gather x4, waiting for transfers between devices, gather_layers(): lax.all_gather(unit, 'batch', axis=0, tiled=True, axis_index_groups=layer...  17.5 us
  transfers between devices with their start and end apart: 10, of which 3 were waited for; matrix products, arithmetic and copies ran while one was open for 33% of the time, Pallas kernels for 49%

profile of v4, /device:TPU:0, one launch (start us, length us, event | category | flops | bytes accessed | tf_op | source)
XLA Modules:
  0.0 569.8 jit_solution(10031754032266097638)
XLA Ops:
  10.4 13.2 %swap_heads.1 = (bf16[4,128,512]{2,1,0:T(8,128)(2,1)}, bf16[4,64,512]{2,1,0:T(8,128)(2,1)}) custom-call(bf16[128,4096]{1,0:T(8,128)(2,1)} %refs_0_.1, bf16[64,4096]{1,0:T(8,128)(2,1)} %refs_1_.1), custom_call_target="tpu_custom_call" | custom-call | bytes 50331648 | tf_op jit(solution)/shard_map/swap_heads/pallas_call | solution.py:365
  32.0 27.3 %swap_feed.1 = (bf16[4,128,1152]{2,1,0:T(8,128)(2,1)}, bf16[4,128,960]{2,1,0:T(8,128)(2,1)}) custom-call(bf16[4,128,1152]{2,1,0:T(8,128)(2,1)} %maximum_bitcast_fusion.refs_0_, bf16[4,128,960]{2,1,0:T(8,128)(2,1)} %maximum_bitcast_fusion.1.refs_1_), custom_call_target="tpu_custom_call" | custom-call | bytes 69206016 | tf_op jit(solution)/shard_map/swap_feed/pallas_call | solution.py:365
  65.5 32.9 %gather_first.1 = (bf16[4,8,64,1536]{3,2,1,0:T(8,128)(2,1)}, bf16[8,4,16,384]{3,2,1,0:T(8,128)(2,1)}) custom-call(bf16[4,64,1536]{2,1,0:T(8,128)(2,1)} %slice.253.refs_0_, bf16[4,16,384]{2,1,0:T(8,128)(2,1)} %slice.254.refs_1_), custom_call_target="tpu_custom_call" | custom-call | bytes 106954752 | tf_op jit(solution)/shard_map/gather_first/pallas_call | solution.py:201
  105.5 17.9 %gather_latent.1 = bf16[8,128,1536]{2,1,0:T(8,128)(2,1)} custom-call(bf16[128,1536]{1,0:T(8,128)(2,1)} %pad_maximum_fusion.13.refs_0_), custom_call_target="tpu_custom_call" | custom-call | bytes 50331648 | tf_op jit(solution)/shard_map/gather_latent/pallas_call | solution.py:201
  144.1 22.4 %reduce_branch.1 = f32[128,2048]{1,0:T(8,128)S(1)} custom-call(bf16[8,128,2048]{2,1,0:T(8,128)(2,1)S(1)} %bitcast.188), custom_call_target="tpu_custom_call" | custom-call | bytes 67108864 | tf_op jit(solution)/shard_map/reduce_branch/pallas_call | solution.py:302
  167.9 38.9 %gather_feed.1 = (bf16[8,128,2048]{2,1,0:T(8,128)(2,1)}, bf16[8,128,2048]{2,1,0:T(8,128)(2,1)}) custom-call(bf16[128,2048]{1,0:T(8,128)(2,1)} %get-tuple-element.157.refs_0_, bf16[128,2048]{1,0:T(8,128)(2,1)} %get-tuple-element.156.refs_1_), custom_call_target="tpu_custom_call" | custom-call | bytes 134217728 | tf_op jit(solution)/shard_map/gather_feed/pallas_call | solution.py:201
  206.9 6.8 %fusion.2 = f32[1024,768]{0,1:T(8,128)S(1)} fusion(bf16[1024,2048]{1,0:T(8,128)(2,1)} %bitcast.251, bf16[2048,1152]{1,0:T(8,128)(2,1)} %all-gather.9.cloned.1.call-done), kind=kOutput, calls=%fused_computation.14 | convolution fusion | flops 3221225472 | bytes 10485760 | tf_op jit(solution)/shard_map/rd,df->rf/dot_general | solution.py:28
  229.8 22.4 %gather_normed.1 = bf16[8,128,2048]{2,1,0:T(8,128)(2,1)} custom-call(bf16[128,2048]{1,0:T(8,128)(2,1)} %copy-done.9), custom_call_target="tpu_custom_call" | custom-call | bytes 67108864 | tf_op jit(solution)/shard_map/gather_normed/pallas_call | solution.py:201
  252.2 9.2 %fusion = f32[1024,2048]{1,0:T(8,128)} fusion(bf16[1024,768]{0,1:T(8,128)(2,1)} %pad_maximum_fusion.5, bf16[2048,1152]{1,0:T(8,128)(2,1)} %all-gather.9.cloned.1.call-done), kind=kOutput, calls=%fused_computation.12 | convolution fusion | flops 3221225472 | bytes 13107200 | tf_op jit(solution)/shard_map/rf,df->rd/dot_general | solution.py:28
  261.4 17.4 %all-gather.11.cloned.1.call-done = bf16[2048,960]{1,0:T(8,128)(2,1)} async-done(((bf16[512,960]{1,0:T(8,128)(2,1)}), bf16[2048,960]{1,0:T(8,128)(2,1)}) %all-gather.11.cloned.1.call-update) | async-done | bytes 3932176 | tf_op jit(solution)/shard_map/all_gather | solution.py:394
  278.8 6.1 %fusion.5 = f32[1024,640]{0,1:T(8,128)S(1)} fusion(bf16[1024,2048]{1,0:T(8,128)(2,1)} %bitcast.252, bf16[2048,960]{1,0:T(8,128)(2,1)} %all-gather.11.cloned.1.call-done), kind=kOutput, calls=%fused_computation.24 | convolution fusion | flops 2684354560 | bytes 9437184 | tf_op jit(solution)/shard_map/rd,df->rf/dot_general | solution.py:28
  298.4 8.1 %add_convert_fusion = bf16[1024,2048]{1,0:T(8,128)(2,1)S(1)} fusion(f32[1024,2048]{1,0:T(8,128)} %fusion, bf16[1024,640]{0,1:T(8,128)(2,1)} %pad_maximum_fusion.6, bf16[2048,960]{1,0:T(8,128)(2,1)} %all-gather.11.cloned.1.call-done), kind=kOutput, calls=%fused_computation | convolution fusion | flops 2688548864 | bytes 16515072 | tf_op jit(solution)/shard_map/rf,df->rd/dot_general | solution.py:28
  306.5 22.5 %reduce_ffn_grad.1 = f32[128,2048]{1,0:T(8,128)S(1)} custom-call(bf16[8,128,2048]{2,1,0:T(8,128)(2,1)S(1)} %bitcast.187), custom_call_target="tpu_custom_call" | custom-call | bytes 67108864 | tf_op jit(solution)/shard_map/reduce_ffn_grad/pallas_call | solution.py:302
  331.3 22.5 %gather_branch.1 = bf16[8,128,2048]{2,1,0:T(8,128)(2,1)} custom-call(bf16[128,2048]{1,0:T(8,128)(2,1)} %fusion.89.refs_0_), custom_call_target="tpu_custom_call" | custom-call | bytes 67108864 | tf_op jit(solution)/shard_map/gather_branch/pallas_call | solution.py:201
  353.8 6.2 %convolution_convert_fusion.10 = bf16[1024,512]{1,0:T(8,128)(2,1)} fusion(bf16[1024,2048]{1,0:T(8,128)(2,1)} %bitcast.201, bf16[2048,512]{1,0:T(8,128)(2,1)} %bitcast.220), kind=kOutput, calls=%fused_computation.43 | convolution fusion | flops 2148007936 | bytes 7340032 | tf_op jit(solution)/shard_map/rd,df->rf/dot_general | solution.py:28
  377.6 7.1 %fusion.15 = f32[1024,2048]{1,0:T(8,128)} fusion(bf16[1024,384]{0,1:T(8,128)(2,1)S(1)} %copy-done.28, bf16[2048,1152]{1,0:T(8,128)(2,1)} %all-gather.9.cloned.1.call-done), kind=kOutput, calls=%fused_computation.49 | convolution fusion | flops 1610612736 | bytes 10747904 | tf_op jit(solution)/shard_map/rf,df->rd/dot_general | solution.py:28
  388.9 8.4 %add_convert_fusion.1 = bf16[1024,2048]{1,0:T(8,128)(2,1)} fusion(f32[1024,2048]{1,0:T(8,128)} %fusion.15, bf16[1024,320]{0,1:T(8,128)(2,1)S(1)} %copy-done.32, bf16[2048,960]{1,0:T(8,128)(2,1)} %all-gather.11.cloned.1.call-done), kind=kOutput, calls=%fused_computation.1 | convolution fusion | flops 1346371584 | bytes 14811136 | tf_op jit(solution)/shard_map/rf,df->rd/dot_general | solution.py:28
  397.3 17.9 %reduce_latent.1 = f32[128,1536]{1,0:T(8,128)S(1)} custom-call(bf16[8,128,1536]{2,1,0:T(8,128)(2,1)S(1)} %copy-done.1), custom_call_target="tpu_custom_call" | custom-call | bytes 50331648 | tf_op jit(solution)/shard_map/reduce_latent/pallas_call | solution.py:302
  424.1 6.0 %fusion.29 = (bf16[2048]{0:T(1024)(128)(2,1)S(1)}, f32[128]{0:T(128)S(1)}, f32[128,2048]{1,0:T(8,128)}) fusion(bf16[128,2048]{1,0:T(8,128)(2,1)S(1)} %copy-done.2, f32[128]{0:T(128)} %copy-done.48, f32[2048]{0:T(1024)S(1)} %convert.103, bf16[2048,1536]{1,0:T(8,128)(2,1)} %bitcast.190, bf16[128,256]{1,0:T(8,128)(2,1)S(1)} %slice.381, ...), kind=kOutput, calls=%fused_computation.76 | convolution fusion | flops 808712064 | bytes 8270848 | tf_op jit(solution)/shard_map/re,de->rd/dot_general | solution.py:28
  430.9 19.3 %gather_last.1 = bf16[8,144,1536]{2,1,0:T(8,128)(2,1)} custom-call(bf16[144,1536]{1,0:T(8,128)(2,1)} %fusion.55.refs_0_), custom_call_target="tpu_custom_call" | custom-call | bytes 56623104 | tf_op jit(solution)/shard_map/gather_last/pallas_call | solution.py:201
  452.4 22.3 %reduce_feed.1 = f32[128,2048]{1,0:T(8,128)S(1)} custom-call(bf16[8,128,2048]{2,1,0:T(8,128)(2,1)S(1)} %bitcast.186), custom_call_target="tpu_custom_call" | custom-call | bytes 67108864 | tf_op jit(solution)/shard_map/reduce_feed/pallas_call | solution.py:302
  491.0 20.1 %all-to-all-done = bf16[4,128,2112]{1,2,0:T(8,128)(2,1)} async-done(((bf16[4,128,2112]{1,2,0:T(8,128)(2,1)}), bf16[4,128,2112]{1,2,0:T(8,128)(2,1)}, u32[]{:S(2)}, u32[]{:S(2)}) %all-to-all-start) | async-done | bytes 2162720 | tf_op jit(solution)/shard_map/all_to_all | solution.py:677
  529.2 8.9 %all-to-all-done.1 = bf16[8,192,512]{2,1,0:T(8,128)(2,1)} async-done(((bf16[8,192,512]{2,1,0:T(8,128)(2,1)}), bf16[8,192,512]{2,1,0:T(8,128)(2,1)}, u32[]{:S(2)}, u32[]{:S(2)}) %all-to-all-start.1) | async-done | bytes 1572896 | tf_op jit(solution)/shard_map/all_to_all | solution.py:692
  548.8 8.6 %swap_last_sums.1 = bf16[128,1536]{1,0:T(8,128)(2,1)} custom-call(bf16[4,64,384]{2,1,0:T(8,128)(2,1)} %bitcast.232), custom_call_target="tpu_custom_call" | custom-call | bytes 6291456 | tf_op jit(solution)/shard_map/swap_last_sums/pallas_call | solution.py:365
  (310 shorter events, 161.5 us)
Async XLA Ops:
  7.2 54.8 %all-gather.5.cloned.1.call-start = ((), (), s32[]{:S(2)}) async-start(), calls=%async_computation.6 | async-start | bytes 1474560 | tf_op jit(solution)/shard_map/all_gather | solution.py:394
  10.4 117.3 %all-gather.7.cloned.1.call-start = ((), (), s32[]{:S(2)}) async-start(), calls=%async_computation.7 | async-start | bytes 3932160 | tf_op jit(solution)/shard_map/all_gather | solution.py:394
  25.8 181.1 %all-gather.9.cloned.1.call-start = ((), (), s32[]{:S(2)}) async-start(), calls=%async_computation.8 | async-start | bytes 5898240 | tf_op jit(solution)/shard_map/all_gather | solution.py:394
  30.9 28.6 %copy-start.60 = (s32[1,4]{1,0:T(1,128)S(1)}, s32[1,4]{1,0:T(1,128)}, u32[]{:S(2)}) copy-start(s32[1,4]{1,0:T(1,128)} %param.14) | copy-start | bytes 52
  30.9 30.9 %copy-start.2 = (bf16[128,2048]{1,0:T(8,128)(2,1)S(1)}, bf16[128,2048]{1,0:T(8,128)(2,1)}, u32[]{:S(2)}) copy-start(bf16[128,2048]{1,0:T(8,128)(2,1)} %param.13) | copy-start | bytes 1572868
  59.3 219.5 %all-gather.11.cloned.1.call-start = ((), (), s32[]{:S(2)}) async-start(), calls=%async_computation.9 | async-start | bytes 5242880 | tf_op jit(solution)/shard_map/all_gather | solution.py:394
  60.1 64.3 %copy-start.46 = (f32[128]{0:T(128)}, f32[128]{0:T(128)S(1)}, u32[]{:S(2)}) copy-start(f32[128]{0:T(128)S(1)} %multiply_power_fusion) | copy-start | bytes 1540
  60.8 269.1 %copy-start.44 = (pred[128]{0:T(512)(128)(4,1)}, pred[128]{0:T(512)(128)(4,1)S(1)}, u32[]{:S(2)}) copy-start(pred[128]{0:T(512)(128)(4,1)S(1)} %iota_compare_fusion.9) | copy-start | bytes 388
  61.9 42.2 %copy-start.54 = (f32[128]{0:T(128)}, f32[128]{0:T(128)S(1)}, u32[]{:S(2)}) copy-start(f32[128]{0:T(128)S(1)} %fusion.33) | copy-start | bytes 1540
  62.0 42.2 %copy-start.48 = (f32[128]{0:T(128)}, f32[128]{0:T(128)S(1)}, u32[]{:S(2)}) copy-start(f32[128]{0:T(128)S(1)} %fusion.82) | copy-start | bytes 1540
  62.0 42.3 %copy-start.50 = (f32[128]{0:T(128)}, f32[128]{0:T(128)S(1)}, u32[]{:S(2)}) copy-start(f32[128]{0:T(128)S(1)} %subtract_convert_fusion.2) | copy-start | bytes 1540
  99.7 315.5 %copy-start.36 = (f32[1024]{0:T(1024)}, f32[1024]{0:T(1024)S(1)}, u32[]{:S(2)}) copy-start(f32[1024]{0:T(1024)S(1)} %reshape.379) | copy-start | bytes 12292
  104.3 310.9 %copy-start.42 = (f32[128]{0:T(128)}, f32[128]{0:T(128)S(1)}, u32[]{:S(2)}) copy-start(f32[128]{0:T(128)S(1)} %fusion.83) | copy-start | bytes 1540
  127.5 248.9 %reduce-scatter.5.cloned.1.call-start = ((), (), s32[]{:S(2)}) async-start(), calls=%async_computation.10 | async-start | bytes 5898240 | tf_op jit(solution)/shard_map/reduce_scatter | solution.py:400
  144.1 22.6 %copy-start.10 = (bf16[128,2048]{1,0:T(8,128)(2,1)S(1)}, bf16[128,2048]{1,0:T(8,128)(2,1)}, u32[]{:S(2)}) copy-start(bf16[128,2048]{1,0:T(8,128)(2,1)} %param.25) | copy-start | bytes 1572868
  166.7 163.2 %copy-start.39 = (f32[128]{0:T(128)}, f32[128]{0:T(128)S(1)}, u32[]{:S(2)}) copy-start(f32[128]{0:T(128)S(1)} %fusion.84) | copy-start | bytes 1540
  227.3 222.9 %reduce-scatter.7.cloned.1.call-start = ((), (), s32[]{:S(2)}) async-start(), calls=%async_computation.11 | async-start | bytes 4915200 | tf_op jit(solution)/shard_map/reduce_scatter | solution.py:400
  330.1 23.8 %copy-start.52 = (f32[128]{0:T(128)}, f32[128]{0:T(128)S(1)}, u32[]{:S(2)}) copy-start(f32[128]{0:T(128)S(1)} %multiply_multiply_fusion.2) | copy-start | bytes 1540
  376.4 134.7 %reduce-scatter.9.cloned.1.call-start = ((), (), s32[]{:S(2)}) async-start(), calls=%async_computation.12 | async-start | bytes 3932160 | tf_op jit(solution)/shard_map/reduce_scatter | solution.py:400
  397.3 18.7 %slice-start = ((bf16[8,128,1536]{2,1,0:T(8,128)(2,1)}), bf16[8,128,1024]{2,1,0:T(8,128)(2,1)S(1)}, s32[]{:S(2)}) async-start(bf16[8,128,1536]{2,1,0:T(8,128)(2,1)} %gather_latent.1), calls=%async_computation.14 | async-start | bytes 4194304 | tf_op jit(solution)/shard_map/slice | solution.py:523
  452.4 22.3 %copy-start.3 = (bf16[8,144,1536]{2,1,0:T(8,128)(2,1)S(1)}, bf16[8,144,1536]{2,1,0:T(8,128)(2,1)}, u32[]{:S(2)}) copy-start(bf16[8,144,1536]{2,1,0:T(8,128)(2,1)} %gather_last.1) | copy-start | bytes 10616836
  480.2 30.9 %all-to-all-start = ((bf16[4,128,2112]{1,2,0:T(8,128)(2,1)}), bf16[4,128,2112]{1,2,0:T(8,128)(2,1)}, u32[]{:S(2)}, u32[]{:S(2)}) async-start(bf16[4,128,2112]{1,2,0:T(8,128)(2,1)} %pad_maximum_fusion.4), calls=%async_computation.2 | async-start | bytes 4325376 | tf_op jit(solution)/shard_map/all_to_all | solution.py:677
  484.6 62.5 %reduce-scatter.11.cloned.1.call-start = ((), (), s32[]{:S(2)}) async-start(), calls=%async_computation.13 | async-start | bytes 1044480 | tf_op jit(solution)/shard_map/reduce_scatter | solution.py:400
  513.6 24.5 %all-to-all-start.1 = ((bf16[8,192,512]{2,1,0:T(8,128)(2,1)}), bf16[8,192,512]{2,1,0:T(8,128)(2,1)}, u32[]{:S(2)}, u32[]{:S(2)}) async-start(bf16[8,192,512]{2,1,0:T(8,128)(2,1)} %bitcast.194), calls=%async_computation.5 | async-start | bytes 3145728 | tf_op jit(solution)/shard_map/all_to_all | solution.py:692
  (49 other events, 159.0 us)
Sparse Core Ops, SparseCore 0:
  10.5 33.1 all-gather.4
  45.8 62.6 all-gather.6
  110.0 88.0 all-gather.8
  199.5 79.2 all-gather.10
  280.9 83.7 reduce-scatter.4
  376.5 70.1 reduce-scatter.6
  450.4 59.2 reduce-scatter.8
  511.9 24.0 reduce-scatter.10

commit v5 on v4

--- a/solution.py
+++ b/solution.py
@@ -18,7 +18,7 @@
 QUAD = 4
 PAIR = 2
 GROUP = QUAD * PAIR
-EXTRA = 32
+EXTRA = 24
 MESH = pl.DeviceIdType.MESH
 BF = jnp.bfloat16
 F32 = jnp.float32
@@ -376,6 +376,36 @@
         cost_estimate=pl.CostEstimate(flops=0, bytes_accessed=32 * moved, transcendentals=0),
         name=name,
     )(*arrays)
+
+
+def spread_kernel(blocks_ref, first_ref, second_ref):
+    count = first_ref.shape[0]
+    columns = blocks_ref.shape[2]
+    for i in range(blocks_ref.shape[0]):
+        at = pl.ds(i * columns, columns)
+        first_ref[:, at] = blocks_ref[i, :count, :].astype(F32)
+        second_ref[:, at] = blocks_ref[i, count:, :].astype(F32)
+
+
+def spread(blocks, count):
+    n, rows, columns = blocks.shape
+    return pl.pallas_call(
+        spread_kernel,
+        grid=(n // 2,),
+        in_specs=[pl.BlockSpec((2, rows, columns), lambda i: (i, 0, 0))],
+        out_specs=[
+            pl.BlockSpec((count, 2 * columns), lambda i: (0, i)),
+            pl.BlockSpec((rows - count, 2 * columns), lambda i: (0, i)),
+        ],
+        out_shape=[
+            jax.ShapeDtypeStruct((count, n * columns), F32),
+            jax.ShapeDtypeStruct((rows - count, n * columns), F32),
+        ],
+        cost_estimate=pl.CostEstimate(
+            flops=0, bytes_accessed=6 * blocks.size, transcendentals=0
+        ),
+        name="spread_heads",
+    )(blocks)
 
 
 def columns_of(width):
@@ -517,12 +547,10 @@
     latent_normed = norm_rows(latent, second_gain).astype(BF)
     key_rot = rotate(keyvals[:, :HEAD_DIM], cosine, sine).astype(BF)
     value_rows = keyvals[:, HEAD_DIM:].astype(BF)
-    [rows_all] = gather_layer(
-        [jnp.concatenate([latent_normed, key_rot, value_rows], axis=1)], 4, "gather_latent"
-    )
-    latent_all = rows_all[:, :, :rank].reshape(all_rows, rank)
-    key_all = rows_all[:, :, rank : rank + HEAD_DIM]
-    value_all = rows_all[:, :, rank + HEAD_DIM :]
+    latent_all, key_all, value_all = gather_layer(
+        [latent_normed, key_rot, value_rows], 4, "gather_latent"
+    )
+    latent_all = latent_all.reshape(all_rows, rank)
 
     positions, valids, allowed = jax.vmap(lambda one: layout(one, count_rows))(all_lengths)
     cosines, sines = angles_of(positions, HEAD_DIM)
@@ -551,7 +579,7 @@
     feed_rows = feed_rows.reshape(all_rows, model)
     grad_rows = grad_rows.reshape(all_rows, model)
 
-    feed_terms = jnp.zeros((all_rows, model), F32)
+    hiddens = []
     ffn_terms = jnp.zeros((all_rows, model), F32)
     grad_packs = []
     normed_rows = []
@@ -577,7 +605,7 @@
         feed_rows = after(feed_rows, grad_pack, normed_rows[0])
         both_grad = after(both_grad, grad_pack)
         ffn_terms = ffn_terms + matmul("rf,df->rd", both_grad, gate_up)
-        feed_terms = feed_terms + matmul("rf,df->rd", hidden, down)
+        hiddens.append((hidden, down))
     ffn_grad = reduce_layer(
         ffn_terms.astype(BF).reshape(GROUP, count_rows, model), 7, "reduce_ffn_grad"
     )
@@ -610,7 +638,7 @@
     back_terms = jnp.concatenate(
         [latent_terms.reshape(GROUP, count_rows, rank), key_terms, value_terms], axis=2
     ).astype(BF)
-    second_pack = after(grad_packs[1], feed_sums[0], back_terms)
+    second_pack = after(grad_packs[1], feed_sums[0], score_grad)
     feed_sums.append(reduce_layers(second_pack, layers))
     back = reduce_layer(after(back_terms, second_pack), 9, "reduce_latent")
     grad_query = matmul("rc,rf->cf", latent_all, after(query_grad, back)).astype(BF)
@@ -636,27 +664,35 @@
     grad_tokens = (
         middle_grad + input_norm_grad + jnp.where(valid[:, None], 0.0, upstream)
     ).astype(BF)
-    first_grad = after(first_grad, head_pack)
+    quads = [[z * QUAD + q for q in range(QUAD)] for z in range(layers)]
+
+    def swap_quads(sums):
+        return lax.all_to_all(
+            sums.reshape(QUAD, part, -1), "batch", 0, 0, axis_index_groups=quads, tiled=True
+        )
+
+    feed_own = [swap_quads(after(feed_sums[0], back))]
+    first_grad = after(first_grad, head_pack, feed_own[0])
     gains = jnp.concatenate([norm_gain_grad, feed_gain_grad, latent_gain_grad])
-    gains = jnp.pad(gains.reshape(-1, rank), ((0, 16 - gains.size // rank), (0, wide - rank)))
-    [grad_all] = gather_layer(
-        [jnp.concatenate([first_grad, gains.astype(BF)], axis=0)], 10, "gather_last"
-    )
-    feed_terms = feed_terms.astype(BF)
+    gains = jnp.pad(gains.reshape(-1, rank), ((0, 32 - gains.size // rank), (0, 0)))
+    grad_all, gains_all = gather_layer([first_grad, gains.astype(BF)], 10, "gather_last")
+    feed_terms = sum(
+        matmul("rf,df->rd", after(hidden, grad_all), down) for hidden, down in hiddens
+    ).astype(BF)
     feed = reduce_layer(
         feed_terms.reshape(GROUP, count_rows, model), 11, "reduce_feed"
     )
     output = jnp.where(valid[:, None], middle + feed, inputs).astype(BF)
 
-    head_pack = after(head_pack, grad_all, feed_terms)
+    head_pack = after(head_pack, grad_all)
     head_sum = reduce_layers(after(head_pack, *feed_sums), layers)
     query_sum, out_sum = head_sum[:rank_span], head_sum[rank_span:]
     normed_rows = normed_rows[0].reshape(all_rows, model)
-    gain_sums = jnp.sum(grad_all[:, count_rows:, :rank].astype(F32), axis=0)
+    gain_sums = jnp.sum(gains_all.astype(F32), axis=0)
     lines = model // rank
     columns = wide // QUAD
     grad_slice = lax.dynamic_slice_in_dim(
-        grad_all[:, :count_rows].reshape(all_rows, wide), quad * columns, columns, axis=1
+        grad_all.reshape(all_rows, wide), quad * columns, columns, axis=1
     )
     grad_first = matmul("rd,re->de", normed_rows, grad_slice).astype(BF)
     grad_first = lax.dynamic_index_in_dim(
@@ -672,11 +708,7 @@
     )
     flat = 16 * columns
     small_sums = jnp.pad(small_sums, ((0, 0), (0, flat - small_sums.shape[1])))
-    feed_sums = [f.reshape(QUAD, part, -1) for f in feed_sums]
-    quads = [[z * QUAD + q for q in range(QUAD)] for z in range(layers)]
-    feed_own = lax.all_to_all(
-        jnp.concatenate(feed_sums, axis=2), "batch", 0, 0, axis_index_groups=quads, tiled=True
-    )
+    feed_own.append(swap_quads(feed_sums[1]))
     last_pack = jnp.concatenate(
         [
             grad_first.reshape(layers, QUAD * half, columns),
@@ -684,10 +716,24 @@
         ],
         axis=1,
     ).reshape(layers * (QUAD * half + 16), columns)
-    last_sum = reduce_layers(after(after(last_pack, feed, feed_own), head_sum), layers)
+    last_pack = after(after(last_pack, feed, feed_own[1]), head_sum)
+    last_sum = reduce_layers(last_pack, layers)
     first_sum = last_sum[: QUAD * half].reshape(QUAD, half, columns)
     small_sum = last_sum[QUAD * half :].astype(F32).reshape(-1)
 
+    grads = []
+    for i in range(3):
+        pieces = [
+            f[:, :, i * (high - low) : (i + 1) * (high - low)]
+            for f, (low, high) in zip(feed_own, chunks)
+        ]
+        grads.append(
+            jnp.concatenate(pieces, axis=2)
+            .transpose(1, 0, 2)
+            .reshape(part, QUAD * units)
+            .astype(F32)
+        )
+    query_sum = after(query_sum, *grads)
     groups = [[z * GROUP + i for i in range(GROUP)] for z in range(layers)]
     head_own = lax.all_to_all(
         jnp.repeat(
@@ -707,8 +753,6 @@
         axis_index_groups=groups,
         tiled=True,
     )
-    head_own = head_own.transpose(1, 0, 2).reshape(rank_part + part, HEADS * HEAD_DIM)
-    query_own, out_own = head_own[:rank_part], head_own[rank_part:]
     [first_own] = swap(
         [first_sum],
         [quad_of],
@@ -723,29 +767,16 @@
         14,
         "swap_last_sums",
     )
-    grads = []
-    for i in range(3):
-        pieces = []
-        begin = 0
-        for low, high in chunks:
-            width = high - low
-            pieces.append(feed_own[:, :, begin + i * width : begin + (i + 1) * width])
-            begin += 3 * width
-        grads.append(
-            jnp.concatenate(pieces, axis=2)
-            .transpose(1, 0, 2)
-            .reshape(part, QUAD * units)
-            .astype(F32)
-        )
+    query_own, out_own = spread(after(head_own, first_own), rank_part)
     return (
         output,
         grad_tokens,
         lax.dynamic_slice_in_dim(small_sum, quad * part, part),
         first_own[:, :rank].astype(F32),
         lax.dynamic_slice_in_dim(small_sum, 2 * span + quad * rank_part, rank_part),
-        query_own.astype(F32),
+        query_own,
         first_own[:, rank:].astype(F32),
-        out_own.astype(F32),
+        out_own,
         lax.dynamic_slice_in_dim(small_sum, span + quad * part, part),
         *grads,
     )

time: 577 us -> 562 us (0.974)
  local copies, waits for them, and re-layouts: 61 us -> 48.9 us
  waiting for transfers between devices: 46.7 us -> 36.5 us
    reduce_scatter x4, waiting for transfers between devices: 0.03 us -> 13.4 us  [reduce_layers(): lax.psum_scatter(blocks, 'batch', scatter_dimension=0, tiled=True, axis_i...]
    all_to_all x1 -> x2, waiting for transfers between devices: 20.1 us -> 7.64 us  [swap_quads(): lax.all_to_all(sums.reshape(QUAD, part, -1), 'batch', 0, 0, axis_index_gr...]
    all_to_all x1, waiting for transfers between devices: 8.95 us -> 0.01 us  [per_device(): lax.all_to_all(jnp.repeat(jnp.concatenate([query_sum.reshape(QUAD, rank_p...]
    unnamed x138 -> x142, local copies, waits for them, and re-layouts: 25.7 us -> 18.9 us
  transfers between devices with their start and end apart: 10 -> 11, of which waited for: 3 -> 4; matrix products, arithmetic and copies ran while one was open for 33% -> 33% of each run, Pallas kernels for 49% -> 52%
where the time goes in v5:
time: 562 us; the launch traced here: 556 us
  Pallas kernels  293 us (52%)
  matrix products  98 us (17%)
  other arithmetic  49.5 us (9%)
  local copies, waits for them, and re-layouts  48.9 us (9%)
  waiting for transfers between devices  36.5 us (6%)
  between operations  15.7 us (3%)
  starting transfers between devices  13.9 us (2%)
    pallas_call x6, Pallas kernels, gather_layer(): pl.pallas_call(functools.partial(gather_kernel, count, cuts, puts), out_s...  155 us
    dot_general x27, matrix products, matmul(): return jnp.einsum(spec, left, right, preferred_element_type=F32)  98 us
    pallas_call x4, Pallas kernels, reduce_layer(): pl.pallas_call(reduce_kernel, out_shape=jax.ShapeDtypeStruct((rows, colum...  85.2 us
    pallas_call x3, Pallas kernels, swap(): pl.pallas_call(functools.partial(swap_kernel, count, takes, puts, flips),...  49.1 us
    unnamed x142, local copies, waits for them, and re-layouts  18.9 us
    all_gather x4, waiting for transfers between devices, gather_layers(): lax.all_gather(unit, 'batch', axis=0, tiled=True, axis_index_groups=layer...  15.2 us
    reduce_scatter x4, waiting for transfers between devices, reduce_layers(): lax.psum_scatter(blocks, 'batch', scatter_dimension=0, tiled=True, axis_i...  13.4 us
  transfers between devices with their start and end apart: 11, of which 4 were waited for; matrix products, arithmetic and copies ran while one was open for 33% of the time, Pallas kernels for 52%

profile of v5, /device:TPU:0, one launch (start us, length us, event | category | flops | bytes accessed | tf_op | source)
XLA Modules:
  0.0 555.7 jit_solution(6045164594907845651)
XLA Ops:
  10.4 13.2 %swap_heads.1 = (bf16[4,128,512]{2,1,0:T(8,128)(2,1)}, bf16[4,64,512]{2,1,0:T(8,128)(2,1)}) custom-call(bf16[128,4096]{1,0:T(8,128)(2,1)} %refs_0_.1, bf16[64,4096]{1,0:T(8,128)(2,1)} %refs_1_.1), custom_call_target="tpu_custom_call" | custom-call | bytes 50331648 | tf_op jit(solution)/shard_map/swap_heads/pallas_call | solution.py:365
  32.5 27.3 %swap_feed.1 = (bf16[4,128,1152]{2,1,0:T(8,128)(2,1)}, bf16[4,128,960]{2,1,0:T(8,128)(2,1)}) custom-call(bf16[4,128,1152]{2,1,0:T(8,128)(2,1)} %maximum_bitcast_fusion.refs_0_, bf16[4,128,960]{2,1,0:T(8,128)(2,1)} %maximum_bitcast_fusion.1.refs_1_), custom_call_target="tpu_custom_call" | custom-call | bytes 69206016 | tf_op jit(solution)/shard_map/swap_feed/pallas_call | solution.py:365
  66.0 32.9 %gather_first.1 = (bf16[4,8,64,1536]{3,2,1,0:T(8,128)(2,1)}, bf16[8,4,16,384]{3,2,1,0:T(8,128)(2,1)}) custom-call(bf16[4,64,1536]{2,1,0:T(8,128)(2,1)} %slice.223.refs_0_, bf16[4,16,384]{2,1,0:T(8,128)(2,1)} %slice.224.refs_1_), custom_call_target="tpu_custom_call" | custom-call | bytes 106954752 | tf_op jit(solution)/shard_map/gather_first/pallas_call | solution.py:201
  111.5 17.8 %gather_latent.1 = (bf16[8,128,1024]{2,1,0:T(8,128)(2,1)}, bf16[8,128,256]{2,1,0:T(8,128)(2,1)}, bf16[8,128,256]{2,1,0:T(8,128)(2,1)}) custom-call(bf16[128,1024]{1,0:T(8,128)(2,1)} %multiply_convert_fusion.8.refs_0_, bf16[128,256]{1,0:T(8,128)(2,1)} %pad_maximum_fusion.13.refs_1_, bf16[128,256]{1,0:T(8,128)(2,1)} %slice.327.refs_2_), custom_call_target="tpu_custom_call" | custom-call | bytes 50331648 | tf_op jit(solution)/shard_map/gather_latent/pallas_call | solution.py:201
  145.3 22.4 %reduce_branch.1 = f32[128,2048]{1,0:T(8,128)S(1)} custom-call(bf16[8,128,2048]{2,1,0:T(8,128)(2,1)S(1)} %bitcast.182), custom_call_target="tpu_custom_call" | custom-call | bytes 67108864 | tf_op jit(solution)/shard_map/reduce_branch/pallas_call | solution.py:302
  169.1 38.9 %gather_feed.1 = (bf16[8,128,2048]{2,1,0:T(8,128)(2,1)}, bf16[8,128,2048]{2,1,0:T(8,128)(2,1)}) custom-call(bf16[128,2048]{1,0:T(8,128)(2,1)} %get-tuple-element.145.refs_0_, bf16[128,2048]{1,0:T(8,128)(2,1)} %get-tuple-element.144.refs_1_), custom_call_target="tpu_custom_call" | custom-call | bytes 134217728 | tf_op jit(solution)/shard_map/gather_feed/pallas_call | solution.py:201
  208.0 6.6 %fusion.2 = f32[1024,768]{0,1:T(8,128)S(1)} fusion(bf16[1024,2048]{1,0:T(8,128)(2,1)} %bitcast.238, bf16[2048,1152]{1,0:T(8,128)(2,1)} %all-gather.9.cloned.1.call-done), kind=kOutput, calls=%fused_computation.14 | convolution fusion | flops 3221225472 | bytes 10485760 | tf_op jit(solution)/shard_map/rd,df->rf/dot_general | solution.py:28
  230.5 22.3 %gather_normed.1 = bf16[8,128,2048]{2,1,0:T(8,128)(2,1)} custom-call(bf16[128,2048]{1,0:T(8,128)(2,1)} %copy-done.5), custom_call_target="tpu_custom_call" | custom-call | bytes 67108864 | tf_op jit(solution)/shard_map/gather_normed/pallas_call | solution.py:201
  252.8 9.1 %fusion = f32[1024,2048]{1,0:T(8,128)} fusion(bf16[1024,768]{0,1:T(8,128)(2,1)} %pad_maximum_fusion.4, bf16[2048,1152]{1,0:T(8,128)(2,1)} %all-gather.9.cloned.1.call-done), kind=kOutput, calls=%fused_computation.12 | convolution fusion | flops 3221225472 | bytes 13107200 | tf_op jit(solution)/shard_map/rf,df->rd/dot_general | solution.py:28
  262.0 15.2 %all-gather.11.cloned.1.call-done = bf16[2048,960]{1,0:T(8,128)(2,1)} async-done(((bf16[512,960]{1,0:T(8,128)(2,1)}), bf16[2048,960]{1,0:T(8,128)(2,1)}) %all-gather.11.cloned.1.call-update) | async-done | bytes 3932176 | tf_op jit(solution)/shard_map/all_gather | solution.py:424
  277.2 6.1 %fusion.5 = f32[1024,640]{0,1:T(8,128)S(1)} fusion(bf16[1024,2048]{1,0:T(8,128)(2,1)} %bitcast.239, bf16[2048,960]{1,0:T(8,128)(2,1)} %all-gather.11.cloned.1.call-done), kind=kOutput, calls=%fused_computation.24 | convolution fusion | flops 2684354560 | bytes 9437184 | tf_op jit(solution)/shard_map/rd,df->rf/dot_general | solution.py:28
  296.8 8.1 %add_convert_fusion.1 = bf16[1024,2048]{1,0:T(8,128)(2,1)S(1)} fusion(f32[1024,2048]{1,0:T(8,128)} %fusion, bf16[1024,640]{0,1:T(8,128)(2,1)} %pad_maximum_fusion.5, bf16[2048,960]{1,0:T(8,128)(2,1)} %all-gather.11.cloned.1.call-done), kind=kOutput, calls=%fused_computation.1 | convolution fusion | flops 2688548864 | bytes 16515072 | tf_op jit(solution)/shard_map/rf,df->rd/dot_general | solution.py:28
  304.9 22.5 %reduce_ffn_grad.1 = f32[128,2048]{1,0:T(8,128)S(1)} custom-call(bf16[8,128,2048]{2,1,0:T(8,128)(2,1)S(1)} %bitcast.181), custom_call_target="tpu_custom_call" | custom-call | bytes 67108864 | tf_op jit(solution)/shard_map/reduce_ffn_grad/pallas_call | solution.py:302
  329.5 22.5 %gather_branch.1 = bf16[8,128,2048]{2,1,0:T(8,128)(2,1)} custom-call(bf16[128,2048]{1,0:T(8,128)(2,1)} %fusion.82.refs_0_), custom_call_target="tpu_custom_call" | custom-call | bytes 67108864 | tf_op jit(solution)/shard_map/gather_branch/pallas_call | solution.py:201
  352.1 6.2 %convolution_convert_fusion.10 = bf16[1024,512]{1,0:T(8,128)(2,1)} fusion(bf16[1024,2048]{1,0:T(8,128)(2,1)} %bitcast.191, bf16[2048,512]{1,0:T(8,128)(2,1)} %bitcast.209), kind=kOutput, calls=%fused_computation.41 | convolution fusion | flops 2148007936 | bytes 7340032 | tf_op jit(solution)/shard_map/rd,df->rf/dot_general | solution.py:28
  378.0 18.0 %reduce_latent.1 = f32[128,1536]{1,0:T(8,128)S(1)} custom-call(bf16[8,128,1536]{2,1,0:T(8,128)(2,1)S(1)} %pad_maximum_fusion.2.in_ref), custom_call_target="tpu_custom_call" | custom-call | bytes 50331648 | tf_op jit(solution)/shard_map/reduce_latent/pallas_call | solution.py:302
  405.3 6.6 %fusion.35 = (f32[128]{0:T(128)}, bf16[2048]{0:T(1024)(128)(2,1)S(1)}, f32[128,2048]{1,0:T(8,128)}) fusion(bf16[128,2048]{1,0:T(8,128)(2,1)S(1)} %copy-done, f32[2048]{0:T(1024)S(1)} %convert.101, f32[128]{0:T(128)} %copy-done.51, bf16[2048,1536]{1,0:T(8,128)(2,1)} %bitcast.184, bf16[128,256]{1,0:T(8,128)(2,1)S(1)} %slice.326, ...), kind=kOutput, calls=%fused_computation.80 | convolution fusion | flops 808712064 | bytes 8270848 | tf_op jit(solution)/shard_map/re,de->rd/dot_general | solution.py:28
  422.2 20.6 %gather_last.1 = (bf16[8,128,1536]{2,1,0:T(8,128)(2,1)}, bf16[8,32,1024]{2,1,0:T(8,128)(2,1)}) custom-call(bf16[128,1536]{1,0:T(8,128)(2,1)} %pad_maximum_fusion.12.refs_0_, bf16[32,1024]{1,0:T(8,128)(2,1)} %pad.15.refs_1_), custom_call_target="tpu_custom_call" | custom-call | bytes 58720256 | tf_op jit(solution)/shard_map/gather_last/pallas_call | solution.py:201
  452.1 22.4 %reduce_feed.1 = f32[128,2048]{1,0:T(8,128)S(1)} custom-call(bf16[8,128,2048]{2,1,0:T(8,128)(2,1)S(1)} %bitcast.180), custom_call_target="tpu_custom_call" | custom-call | bytes 67108864 | tf_op jit(solution)/shard_map/reduce_feed/pallas_call | solution.py:302
  480.1 4.8 convolution_convert_fusion.5
  486.0 7.6 %all-to-all-done.1 = bf16[4,128,960]{1,2,0:T(8,128)(2,1)} async-done(((bf16[4,128,960]{1,2,0:T(8,128)(2,1)}), bf16[4,128,960]{1,2,0:T(8,128)(2,1)}, u32[]{:S(2)}, u32[]{:S(2)}) %all-to-all-start.1) | async-done | bytes 983072 | tf_op jit(solution)/shard_map/all_to_all | solution.py:670
  493.7 9.1 %reduce-scatter.9.cloned.1.call-done = bf16[768,512]{1,0:T(8,128)(2,1)} async-done(((bf16[3072,512]{1,0:T(8,128)(2,1)}), bf16[768,512]{1,0:T(8,128)(2,1)}) %reduce-scatter.9.cloned.1.call-update) | async-done | bytes 786448 | tf_op jit(solution)/shard_map/reduce_scatter | solution.py:430
  510.6 4.4 all-to-all-start.2
  531.5 8.6 %swap_last_sums.1 = bf16[128,1536]{1,0:T(8,128)(2,1)} custom-call(bf16[4,64,384]{2,1,0:T(8,128)(2,1)} %bitcast.219), custom_call_target="tpu_custom_call" | custom-call | bytes 6291456 | tf_op jit(solution)/shard_map/swap_last_sums/pallas_call | solution.py:365
  (310 shorter events, 166.7 us)
Async XLA Ops:
  7.2 55.3 %all-gather.5.cloned.1.call-start = ((), (), s32[]{:S(2)}) async-start(), calls=%async_computation.7 | async-start | bytes 1351680 | tf_op jit(solution)/shard_map/all_gather | solution.py:424
  10.3 119.0 %all-gather.7.cloned.1.call-start = ((), (), s32[]{:S(2)}) async-start(), calls=%async_computation.8 | async-start | bytes 3932160 | tf_op jit(solution)/shard_map/all_gather | solution.py:424
  25.7 182.3 %all-gather.9.cloned.1.call-start = ((), (), s32[]{:S(2)}) async-start(), calls=%async_computation.9 | async-start | bytes 5898240 | tf_op jit(solution)/shard_map/all_gather | solution.py:424
  32.5 27.4 %copy-start.62 = (s32[1,4]{1,0:T(1,128)S(1)}, s32[1,4]{1,0:T(1,128)}, u32[]{:S(2)}) copy-start(s32[1,4]{1,0:T(1,128)} %param.14) | copy-start | bytes 52
  32.5 29.8 %copy-start = (bf16[128,2048]{1,0:T(8,128)(2,1)S(1)}, bf16[128,2048]{1,0:T(8,128)(2,1)}, u32[]{:S(2)}) copy-start(bf16[128,2048]{1,0:T(8,128)(2,1)} %param.13) | copy-start | bytes 1572868
  59.8 217.3 %all-gather.11.cloned.1.call-start = ((), (), s32[]{:S(2)}) async-start(), calls=%async_computation.10 | async-start | bytes 5242880 | tf_op jit(solution)/shard_map/all_gather | solution.py:424
  60.6 46.2 %copy-start.50 = (f32[128]{0:T(128)}, f32[128]{0:T(128)S(1)}, u32[]{:S(2)}) copy-start(f32[128]{0:T(128)S(1)} %multiply_power_fusion) | copy-start | bytes 1540
  61.3 267.0 %copy-start.48 = (pred[128]{0:T(512)(128)(4,1)}, pred[128]{0:T(512)(128)(4,1)S(1)}, u32[]{:S(2)}) copy-start(pred[128]{0:T(512)(128)(4,1)S(1)} %iota_compare_fusion.8) | copy-start | bytes 388
  62.4 37.5 %copy-start.56 = (f32[128]{0:T(128)}, f32[128]{0:T(128)S(1)}, u32[]{:S(2)}) copy-start(f32[128]{0:T(128)S(1)} %fusion.33) | copy-start | bytes 1540
  62.4 42.2 %copy-start.51 = (f32[128]{0:T(128)}, f32[128]{0:T(128)S(1)}, u32[]{:S(2)}) copy-start(f32[128]{0:T(128)S(1)} %fusion.76) | copy-start | bytes 1540
  62.5 43.2 %copy-start.55 = (f32[128]{0:T(128)}, f32[128]{0:T(128)S(1)}, u32[]{:S(2)}) copy-start(f32[128]{0:T(128)S(1)} %subtract_convert_fusion.2) | copy-start | bytes 1540
  100.2 301.6 %copy-start.43 = (f32[1024]{0:T(1024)}, f32[1024]{0:T(1024)S(1)}, u32[]{:S(2)}) copy-start(f32[1024]{0:T(1024)S(1)} %reshape.372) | copy-start | bytes 12292
  104.6 30.8 %copy-start.1 = (f32[128,1536]{1,0:T(8,128)}, f32[128,1536]{1,0:T(8,128)S(1)}, u32[]{:S(2)}) copy-start(f32[128,1536]{1,0:T(8,128)S(1)} %fusion.88) | copy-start | bytes 2359300
  105.6 296.2 %copy-start.47 = (f32[128]{0:T(128)}, f32[128]{0:T(128)S(1)}, u32[]{:S(2)}) copy-start(f32[128]{0:T(128)S(1)} %fusion.77) | copy-start | bytes 1540
  109.8 28.8 %copy-start.9 = (f32[8,128,128]{2,1,0:T(8,128)}, f32[8,128,128]{2,1,0:T(8,128)S(1)}, u32[]{:S(2)}) copy-start(f32[8,128,128]{2,1,0:T(8,128)S(1)} %get-tuple-element.138) | copy-start | bytes 1572868
  109.8 253.8 %reduce-scatter.5.cloned.1.call-start = ((), (), s32[]{:S(2)}) async-start(), calls=%async_computation.11 | async-start | bytes 5898240 | tf_op jit(solution)/shard_map/reduce_scatter | solution.py:430
  167.9 160.5 %copy-start.45 = (f32[128]{0:T(128)}, f32[128]{0:T(128)S(1)}, u32[]{:S(2)}) copy-start(f32[128]{0:T(128)S(1)} %fusion.78) | copy-start | bytes 1540
  228.1 214.7 %reduce-scatter.7.cloned.1.call-start = ((), (), s32[]{:S(2)}) async-start(), calls=%async_computation.12 | async-start | bytes 4915200 | tf_op jit(solution)/shard_map/reduce_scatter | solution.py:430
  328.3 23.8 %copy-start.53 = (f32[128]{0:T(128)}, f32[128]{0:T(128)S(1)}, u32[]{:S(2)}) copy-start(f32[128]{0:T(128)S(1)} %multiply_multiply_fusion.2) | copy-start | bytes 1540
  397.2 24.9 %all-to-all-start = ((bf16[4,128,1152]{1,2,0:T(8,128)(2,1)}), bf16[4,128,1152]{1,2,0:T(8,128)(2,1)}, u32[]{:S(2)}, u32[]{:S(2)}) async-start(bf16[4,128,1152]{1,2,0:T(8,128)(2,1)} %copy_bitcast_fusion), calls=%async_computation.1 | async-start | bytes 2359296 | tf_op jit(solution)/shard_map/all_to_all | solution.py:670
  401.5 101.2 %reduce-scatter.9.cloned.1.call-start = ((), (), s32[]{:S(2)}) async-start(), calls=%async_computation.13 | async-start | bytes 3932160 | tf_op jit(solution)/shard_map/reduce_scatter | solution.py:430
  475.6 18.1 %all-to-all-start.1 = ((bf16[4,128,960]{1,2,0:T(8,128)(2,1)}), bf16[4,128,960]{1,2,0:T(8,128)(2,1)}, u32[]{:S(2)}, u32[]{:S(2)}) async-start(bf16[4,128,960]{1,2,0:T(8,128)(2,1)} %copy_bitcast_fusion.2), calls=%async_computation.3 | async-start | bytes 1966080 | tf_op jit(solution)/shard_map/all_to_all | solution.py:670
  479.8 49.3 %reduce-scatter.11.cloned.1.call-start = ((), (), s32[]{:S(2)}) async-start(), calls=%async_computation.14 | async-start | bytes 1044480 | tf_op jit(solution)/shard_map/reduce_scatter | solution.py:430
  510.6 33.0 %all-to-all-start.2 = ((bf16[8,192,512]{2,1,0:T(8,128)(2,1)}), bf16[8,192,512]{2,1,0:T(8,128)(2,1)}, u32[]{:S(2)}, u32[]{:S(2)}) async-start(bf16[8,192,512]{2,1,0:T(8,128)(2,1)} %bitcast.186), calls=%async_computation.6 | async-start | bytes 3145728 | tf_op jit(solution)/shard_map/all_to_all | solution.py:738
  (53 other events, 225.5 us)
Sparse Core Ops, SparseCore 0:
  10.5 31.1 all-gather.4
  43.8 62.9 all-gather.6
  108.4 88.0 all-gather.8
  197.9 79.2 all-gather.10
  279.3 83.7 reduce-scatter.4
  365.3 73.1 reduce-scatter.6
  442.9 59.7 reduce-scatter.8
  505.1 24.0 reduce-scatter.10

commit v6 on v5

--- a/solution.py
+++ b/solution.py
@@ -405,6 +405,105 @@
             flops=0, bytes_accessed=6 * blocks.size, transcendentals=0
         ),
         name="spread_heads",
+    )(blocks)
+
+
+def settle_kernel(count, takes, puts, results, *refs):
+    ins, outs = refs[:count], refs[count : count + len(results)]
+    landed = refs[count + len(results) : 2 * count + len(results)]
+    local_sem, send_sem, recv_sem = refs[2 * count + len(results) :]
+    base, quad, hid = place()
+    address, index = ways_of(base, quad, hid)
+    meet([address(f) for f in ALL_FLIPS])
+
+    def copy(i, j, f, owner):
+        return pltpu.make_async_remote_copy(
+            src_ref=takes[i](ins[i], index(f) // PAIR),
+            dst_ref=puts[i](landed[i], owner),
+            send_sem=send_sem.at[i, j],
+            recv_sem=recv_sem.at[i, j],
+            device_id=address(f),
+            device_id_type=MESH,
+        )
+
+    def local(i):
+        return pltpu.make_async_copy(
+            takes[i](ins[i], quad), puts[i](landed[i], index(SELF)), local_sem.at[i]
+        )
+
+    for i in range(count):
+        for j, f in enumerate(ALL_FLIPS):
+            copy(i, j, f, index(SELF)).start()
+        local(i).start()
+    for i in range(count):
+        local(i).wait()
+        for j, f in enumerate(ALL_FLIPS):
+            copy(i, j, f, index(f)).wait_recv()
+    step = 16
+    for (i, begin, end), out in zip(results, outs):
+
+        def body(r, carry, i=i, begin=begin, end=end, out=out):
+            at = pl.ds(pl.multiple_of(r * step, step), step)
+            out[at, :] = landed[i][at, begin:end].astype(F32)
+            return carry
+
+        lax.fori_loop(0, out.shape[0] // step, body, 0)
+    for i in range(count):
+        for j, f in enumerate(ALL_FLIPS):
+            copy(i, j, f, index(SELF)).wait_send()
+
+
+def settle(arrays, takes, puts, shapes, results, ident, name):
+    count = len(arrays)
+    moved = sum(s[0] * s[1] for s in shapes)
+    return pl.pallas_call(
+        functools.partial(settle_kernel, count, takes, puts, results),
+        out_shape=[jax.ShapeDtypeStruct((shapes[i][0], e - b), F32) for i, b, e in results],
+        in_specs=[pl.BlockSpec(memory_space=pl.ANY)] * count,
+        out_specs=[pl.BlockSpec(memory_space=pltpu.VMEM)] * len(results),
+        scratch_shapes=[pltpu.VMEM(s, BF) for s in shapes]
+        + [
+            pltpu.SemaphoreType.DMA((count,)),
+            pltpu.SemaphoreType.DMA((count, len(ALL_FLIPS))),
+            pltpu.SemaphoreType.DMA((count, len(ALL_FLIPS))),
+        ],
+        compiler_params=pltpu.CompilerParams(
+            collective_id=ident, has_side_effects=True, vmem_limit_bytes=24 * 2**20
+        ),
+        cost_estimate=pl.CostEstimate(flops=0, bytes_accessed=64 * moved, transcendentals=0),
+        name=name,
+    )(*arrays)
+
+
+def rows_of(begin, count):
+    return lambda ref, q: ref.at[pl.ds(pl.multiple_of(begin + q * count, 16), count)]
+
+
+def join_kernel(widths, blocks_ref, *outs):
+    total = sum(widths)
+    for i, out in enumerate(outs):
+        for q in range(QUAD):
+            begin, source = q * total, 0
+            for width in widths:
+                at = source + i * width
+                out[:, begin : begin + width] = blocks_ref[q, :, at : at + width].astype(F32)
+                begin += width
+                source += 3 * width
+
+
+def join(blocks, widths):
+    rows, columns = blocks.shape[1], QUAD * sum(widths)
+    strip = min(rows, 32)
+    return pl.pallas_call(
+        functools.partial(join_kernel, widths),
+        grid=(rows // strip,),
+        in_specs=[pl.BlockSpec((QUAD, strip, blocks.shape[2]), lambda i: (0, i, 0))],
+        out_specs=[pl.BlockSpec((strip, columns), lambda i: (i, 0))] * 3,
+        out_shape=[jax.ShapeDtypeStruct((rows, columns), F32)] * 3,
+        cost_estimate=pl.CostEstimate(
+            flops=0, bytes_accessed=18 * rows * columns, transcendentals=0
+        ),
+        name="join_feed",
     )(blocks)
 
 
@@ -664,15 +763,7 @@
     grad_tokens = (
         middle_grad + input_norm_grad + jnp.where(valid[:, None], 0.0, upstream)
     ).astype(BF)
-    quads = [[z * QUAD + q for q in range(QUAD)] for z in range(layers)]
-
-    def swap_quads(sums):
-        return lax.all_to_all(
-            sums.reshape(QUAD, part, -1), "batch", 0, 0, axis_index_groups=quads, tiled=True
-        )
-
-    feed_own = [swap_quads(after(feed_sums[0], back))]
-    first_grad = after(first_grad, head_pack, feed_own[0])
+    first_grad = after(first_grad, head_pack)
     gains = jnp.concatenate([norm_gain_grad, feed_gain_grad, latent_gain_grad])
     gains = jnp.pad(gains.reshape(-1, rank), ((0, 32 - gains.size // rank), (0, 0)))
     grad_all, gains_all = gather_layer([first_grad, gains.astype(BF)], 10, "gather_last")
@@ -686,7 +777,6 @@
 
     head_pack = after(head_pack, grad_all)
     head_sum = reduce_layers(after(head_pack, *feed_sums), layers)
-    query_sum, out_sum = head_sum[:rank_span], head_sum[rank_span:]
     normed_rows = normed_rows[0].reshape(all_rows, model)
     gain_sums = jnp.sum(gains_all.astype(F32), axis=0)
     lines = model // rank
@@ -708,7 +798,15 @@
     )
     flat = 16 * columns
     small_sums = jnp.pad(small_sums, ((0, 0), (0, flat - small_sums.shape[1])))
-    feed_own.append(swap_quads(feed_sums[1]))
+    quads = [[z * QUAD + q for q in range(QUAD)] for z in range(layers)]
+    feed_own = lax.all_to_all(
+        after(jnp.concatenate(feed_sums, axis=1), grad_all).reshape(QUAD, part, -1),
+        "batch",
+        0,
+        0,
+        axis_index_groups=quads,
+        tiled=True,
+    )
     last_pack = jnp.concatenate(
         [
             grad_first.reshape(layers, QUAD * half, columns),
@@ -716,24 +814,12 @@
         ],
         axis=1,
     ).reshape(layers * (QUAD * half + 16), columns)
-    last_pack = after(after(last_pack, feed, feed_own[1]), head_sum)
+    grads = join(feed_own, [high - low for low, high in chunks])
+    last_pack = after(after(last_pack, feed), head_sum)
     last_sum = reduce_layers(last_pack, layers)
-    first_sum = last_sum[: QUAD * half].reshape(QUAD, half, columns)
     small_sum = last_sum[QUAD * half :].astype(F32).reshape(-1)
 
-    grads = []
-    for i in range(3):
-        pieces = [
-            f[:, :, i * (high - low) : (i + 1) * (high - low)]
-            for f, (low, high) in zip(feed_own, chunks)
-        ]
-        grads.append(
-            jnp.concatenate(pieces, axis=2)
-            .transpose(1, 0, 2)
-            .reshape(part, QUAD * units)
-            .astype(F32)
-        )
-    query_sum = after(query_sum, *grads)
+    query_sum, out_sum = head_sum[:rank_span], head_sum[rank_span:]
     groups = [[z * GROUP + i for i in range(GROUP)] for z in range(layers)]
     head_own = lax.all_to_all(
         jnp.repeat(
@@ -753,9 +839,9 @@
         axis_index_groups=groups,
         tiled=True,
     )
-    [first_own] = swap(
-        [first_sum],
-        [quad_of],
+    down_own, pair_own = settle(
+        [last_sum],
+        [rows_of(0, half)],
         [
             lambda ref, i: ref.at[
                 pl.ds(pl.multiple_of(lax.rem(i, PAIR) * half, half), half),
@@ -763,19 +849,19 @@
             ],
         ],
         [(part, wide)],
-        ALL_FLIPS,
+        [(0, 0, rank), (0, rank, wide)],
         14,
-        "swap_last_sums",
-    )
-    query_own, out_own = spread(after(head_own, first_own), rank_part)
+        "settle_last",
+    )
+    query_own, out_own = spread(after(head_own, down_own), rank_part)
     return (
         output,
         grad_tokens,
         lax.dynamic_slice_in_dim(small_sum, quad * part, part),
-        first_own[:, :rank].astype(F32),
+        down_own,
         lax.dynamic_slice_in_dim(small_sum, 2 * span + quad * rank_part, rank_part),
         query_own,
-        first_own[:, rank:].astype(F32),
+        pair_own,
         out_own,
         lax.dynamic_slice_in_dim(small_sum, span + quad * part, part),
         *grads,

time: 562 us -> 558 us (level)
  Pallas kernels: 293 us -> 316 us
  waiting for transfers between devices: 36.5 us -> 24.9 us
  other arithmetic: 49.5 us -> 41.4 us
    pallas_call x4, Pallas kernels: 85.2 us -> 105 us  [reduce_layer(): pl.pallas_call(reduce_kernel, out_shape=jax.ShapeDtypeStruct((rows, colum...]
    pallas_call x0 -> x2, Pallas kernels: none -> 12.7 us  [the longest x1 8.37 us: settle(): pl.pallas_call(functools.partial(settle_kernel, count, takes, puts, resul...]
    pallas_call x3 -> x2, Pallas kernels: 49.1 us -> 40.5 us  [swap(): pl.pallas_call(functools.partial(swap_kernel, count, takes, puts, flips),...]
    all_to_all x2 -> x1, waiting for transfers between devices: 7.64 us -> 0.01 us  [per_device(): lax.all_to_all(after(jnp.concatenate(feed_sums, axis=1), grad_all).reshap...]
    convert_element_type x5 -> x0, other arithmetic: 7.04 us -> none  [the longest x3 3.61 us: per_device(): grads.append(jnp.concatenate(pieces, axis=2).transpose(1, 0, 2).reshape(p...]
    unnamed x142 -> x141, local copies, waits for them, and re-layouts: 18.9 us -> 16.1 us
  transfers between devices with their start and end apart: 11 -> 10, of which waited for: 4 -> 3; matrix products, arithmetic and copies ran while one was open for 33% -> 31% of each run, Pallas kernels for 52% -> 57%
where the time goes in v6:
time: 558 us; the launch traced here: 552 us
  Pallas kernels  316 us (57%)
  matrix products  96.9 us (17%)
  local copies, waits for them, and re-layouts  47.4 us (8%)
  other arithmetic  41.4 us (7%)
  waiting for transfers between devices  24.9 us (4%)
  between operations  15.8 us (3%)
  starting transfers between devices  9.28 us (2%)
    pallas_call x6, Pallas kernels, gather_layer(): pl.pallas_call(functools.partial(gather_kernel, count, cuts, puts), out_s...  154 us
    pallas_call x4, Pallas kernels, reduce_layer(): pl.pallas_call(reduce_kernel, out_shape=jax.ShapeDtypeStruct((rows, colum...  105 us
    dot_general x27, matrix products, matmul(): return jnp.einsum(spec, left, right, preferred_element_type=F32)  96.9 us
    pallas_call x2, Pallas kernels, swap(): pl.pallas_call(functools.partial(swap_kernel, count, takes, puts, flips),...  40.5 us
    all_gather x4, waiting for transfers between devices, gather_layers(): lax.all_gather(unit, 'batch', axis=0, tiled=True, axis_index_groups=layer...  16.4 us
    unnamed x141, local copies, waits for them, and re-layouts  16.1 us
  transfers between devices with their start and end apart: 10, of which 3 were waited for; matrix products, arithmetic and copies ran while one was open for 31% of the time, Pallas kernels for 57%

profile of v6, /device:TPU:0, one launch (start us, length us, event | category | flops | bytes accessed | tf_op | source)
XLA Modules:
  0.0 551.6 jit_solution(981983375631506564)
XLA Ops:
  10.4 13.2 %swap_heads.1 = (bf16[4,128,512]{2,1,0:T(8,128)(2,1)}, bf16[4,64,512]{2,1,0:T(8,128)(2,1)}) custom-call(bf16[128,4096]{1,0:T(8,128)(2,1)} %refs_0_.1, bf16[64,4096]{1,0:T(8,128)(2,1)} %refs_1_.1), custom_call_target="tpu_custom_call" | custom-call | bytes 50331648 | tf_op jit(solution)/shard_map/swap_heads/pallas_call | solution.py:365
  32.0 27.3 %swap_feed.1 = (bf16[4,128,1152]{2,1,0:T(8,128)(2,1)}, bf16[4,128,960]{2,1,0:T(8,128)(2,1)}) custom-call(bf16[4,128,1152]{2,1,0:T(8,128)(2,1)} %maximum_bitcast_fusion.refs_0_, bf16[4,128,960]{2,1,0:T(8,128)(2,1)} %maximum_bitcast_fusion.1.refs_1_), custom_call_target="tpu_custom_call" | custom-call | bytes 69206016 | tf_op jit(solution)/shard_map/swap_feed/pallas_call | solution.py:365
  65.5 32.9 %gather_first.1 = (bf16[4,8,64,1536]{3,2,1,0:T(8,128)(2,1)}, bf16[8,4,16,384]{3,2,1,0:T(8,128)(2,1)}) custom-call(bf16[4,64,1536]{2,1,0:T(8,128)(2,1)} %slice.187.refs_0_, bf16[4,16,384]{2,1,0:T(8,128)(2,1)} %slice.188.refs_1_), custom_call_target="tpu_custom_call" | custom-call | bytes 106954752 | tf_op jit(solution)/shard_map/gather_first/pallas_call | solution.py:201
  110.9 17.8 %gather_latent.1 = (bf16[8,128,1024]{2,1,0:T(8,128)(2,1)}, bf16[8,128,256]{2,1,0:T(8,128)(2,1)}, bf16[8,128,256]{2,1,0:T(8,128)(2,1)}) custom-call(bf16[128,1024]{1,0:T(8,128)(2,1)} %multiply_convert_fusion.8.refs_0_, bf16[128,256]{1,0:T(8,128)(2,1)} %pad_maximum_fusion.14.refs_1_, bf16[128,256]{1,0:T(8,128)(2,1)} %slice.282.refs_2_), custom_call_target="tpu_custom_call" | custom-call | bytes 50331648 | tf_op jit(solution)/shard_map/gather_latent/pallas_call | solution.py:201
  144.0 22.4 %reduce_branch.1 = f32[128,2048]{1,0:T(8,128)S(1)} custom-call(bf16[8,128,2048]{2,1,0:T(8,128)(2,1)S(1)} %bitcast.167), custom_call_target="tpu_custom_call" | custom-call | bytes 67108864 | tf_op jit(solution)/shard_map/reduce_branch/pallas_call | solution.py:302
  167.9 38.9 %gather_feed.1 = (bf16[8,128,2048]{2,1,0:T(8,128)(2,1)}, bf16[8,128,2048]{2,1,0:T(8,128)(2,1)}) custom-call(bf16[128,2048]{1,0:T(8,128)(2,1)} %get-tuple-element.123.refs_0_, bf16[128,2048]{1,0:T(8,128)(2,1)} %get-tuple-element.122.refs_1_), custom_call_target="tpu_custom_call" | custom-call | bytes 134217728 | tf_op jit(solution)/shard_map/gather_feed/pallas_call | solution.py:201
  206.8 6.6 %fusion.2 = f32[1024,768]{0,1:T(8,128)S(1)} fusion(bf16[1024,2048]{1,0:T(8,128)(2,1)} %bitcast.219, bf16[2048,1152]{1,0:T(8,128)(2,1)} %all-gather.9.cloned.1.call-done), kind=kOutput, calls=%fused_computation.14 | convolution fusion | flops 3221225472 | bytes 10485760 | tf_op jit(solution)/shard_map/rd,df->rf/dot_general | solution.py:28
  229.4 22.4 %gather_normed.1 = bf16[8,128,2048]{2,1,0:T(8,128)(2,1)} custom-call(bf16[128,2048]{1,0:T(8,128)(2,1)} %copy-done.6), custom_call_target="tpu_custom_call" | custom-call | bytes 67108864 | tf_op jit(solution)/shard_map/gather_normed/pallas_call | solution.py:201
  251.8 9.1 %fusion = f32[1024,2048]{1,0:T(8,128)} fusion(bf16[1024,768]{0,1:T(8,128)(2,1)} %pad_maximum_fusion.5, bf16[2048,1152]{1,0:T(8,128)(2,1)} %all-gather.9.cloned.1.call-done), kind=kOutput, calls=%fused_computation.12 | convolution fusion | flops 3221225472 | bytes 13107200 | tf_op jit(solution)/shard_map/rf,df->rd/dot_general | solution.py:28
  260.9 16.3 %all-gather.11.cloned.1.call-done = bf16[2048,960]{1,0:T(8,128)(2,1)} async-done(((bf16[512,960]{1,0:T(8,128)(2,1)}), bf16[2048,960]{1,0:T(8,128)(2,1)}) %all-gather.11.cloned.1.call-update) | async-done | bytes 3932176 | tf_op jit(solution)/shard_map/all_gather | solution.py:523
  277.2 6.1 %fusion.5 = f32[1024,640]{0,1:T(8,128)S(1)} fusion(bf16[1024,2048]{1,0:T(8,128)(2,1)} %bitcast.220, bf16[2048,960]{1,0:T(8,128)(2,1)} %all-gather.11.cloned.1.call-done), kind=kOutput, calls=%fused_computation.24 | convolution fusion | flops 2684354560 | bytes 9437184 | tf_op jit(solution)/shard_map/rd,df->rf/dot_general | solution.py:28
  296.8 8.1 %add_convert_fusion.1 = bf16[1024,2048]{1,0:T(8,128)(2,1)S(1)} fusion(f32[1024,2048]{1,0:T(8,128)} %fusion, bf16[1024,640]{0,1:T(8,128)(2,1)} %pad_maximum_fusion.6, bf16[2048,960]{1,0:T(8,128)(2,1)} %all-gather.11.cloned.1.call-done), kind=kOutput, calls=%fused_computation.1 | convolution fusion | flops 2688548864 | bytes 16515072 | tf_op jit(solution)/shard_map/rf,df->rd/dot_general | solution.py:28
  305.0 22.5 %reduce_ffn_grad.1 = f32[128,2048]{1,0:T(8,128)S(1)} custom-call(bf16[8,128,2048]{2,1,0:T(8,128)(2,1)S(1)} %bitcast.166), custom_call_target="tpu_custom_call" | custom-call | bytes 67108864 | tf_op jit(solution)/shard_map/reduce_ffn_grad/pallas_call | solution.py:302
  329.7 22.5 %gather_branch.1 = bf16[8,128,2048]{2,1,0:T(8,128)(2,1)} custom-call(bf16[128,2048]{1,0:T(8,128)(2,1)} %fusion.82.refs_0_), custom_call_target="tpu_custom_call" | custom-call | bytes 67108864 | tf_op jit(solution)/shard_map/gather_branch/pallas_call | solution.py:201
  352.3 6.2 %convolution_convert_fusion.10 = bf16[1024,512]{1,0:T(8,128)(2,1)} fusion(bf16[1024,2048]{1,0:T(8,128)(2,1)} %bitcast.173, bf16[2048,512]{1,0:T(8,128)(2,1)} %bitcast.190), kind=kOutput, calls=%fused_computation.43 | convolution fusion | flops 2148007936 | bytes 7340032 | tf_op jit(solution)/shard_map/rd,df->rf/dot_general | solution.py:28
  378.6 18.4 %reduce_latent.1 = f32[128,1536]{1,0:T(8,128)S(1)} custom-call(bf16[8,128,1536]{2,1,0:T(8,128)(2,1)S(1)} %pad_maximum_fusion.2.in_ref), custom_call_target="tpu_custom_call" | custom-call | bytes 50331648 | tf_op jit(solution)/shard_map/reduce_latent/pallas_call | solution.py:302
  406.7 6.5 %fusion.35 = (f32[128]{0:T(128)}, bf16[2048]{0:T(1024)(128)(2,1)S(1)}, f32[128,2048]{1,0:T(8,128)}) fusion(bf16[128,2048]{1,0:T(8,128)(2,1)S(1)} %copy-done.2, f32[2048]{0:T(1024)S(1)} %convert.95, f32[128]{0:T(128)} %copy-done.49, bf16[2048,1536]{1,0:T(8,128)(2,1)} %bitcast.169, bf16[128,256]{1,0:T(8,128)(2,1)S(1)} %slice.281, ...), kind=kOutput, calls=%fused_computation.81 | convolution fusion | flops 808712064 | bytes 8270848 | tf_op jit(solution)/shard_map/re,de->rd/dot_general | solution.py:28
  413.9 19.6 %gather_last.1 = (bf16[8,128,1536]{2,1,0:T(8,128)(2,1)}, bf16[8,32,1024]{2,1,0:T(8,128)(2,1)}) custom-call(bf16[128,1536]{1,0:T(8,128)(2,1)} %pad_maximum_fusion.13.refs_0_, bf16[32,1024]{1,0:T(8,128)(2,1)} %pad.15.refs_1_), custom_call_target="tpu_custom_call" | custom-call | bytes 58720256 | tf_op jit(solution)/shard_map/gather_last/pallas_call | solution.py:201
  433.5 5.0 reduce-scatter.7.cloned.1.call-done
  442.7 6.0 %add_convert_fusion = bf16[1024,2048]{1,0:T(8,128)(2,1)} fusion(f32[1024,2048]{1,0:T(8,128)S(1)} %fusion.13, bf16[1024,320]{0,1:T(8,128)(2,1)S(1)} %copy-done.30, bf16[2048,960]{1,0:T(8,128)(2,1)} %all-gather.11.cloned.1.call-done), kind=kOutput, calls=%fused_computation | convolution fusion | flops 1346371584 | bytes 14811136 | tf_op jit(solution)/shard_map/rf,df->rd/dot_general | solution.py:28
  450.6 4.5 all-to-all-start.1
  457.3 41.4 %reduce_feed.1 = f32[128,2048]{1,0:T(8,128)S(1)} custom-call(bf16[8,128,2048]{2,1,0:T(8,128)(2,1)S(1)} %bitcast.165), custom_call_target="tpu_custom_call" | custom-call | bytes 67108864 | tf_op jit(solution)/shard_map/reduce_feed/pallas_call | solution.py:302
  508.0 4.3 all-to-all-start
  529.6 8.4 %settle_last.1 = (f32[128,1024]{1,0:T(8,128)S(1)}, f32[128,512]{1,0:T(8,128)S(1)}) custom-call(bf16[272,384]{1,0:T(8,128)(2,1)S(1)} %copy-done.1), custom_call_target="tpu_custom_call" | custom-call | bytes 12582912 | tf_op jit(solution)/shard_map/settle_last/pallas_call | solution.py:459
  (300 shorter events, 149.3 us)
Async XLA Ops:
  7.2 54.8 %all-gather.5.cloned.1.call-start = ((), (), s32[]{:S(2)}) async-start(), calls=%async_computation.6 | async-start | bytes 1351680 | tf_op jit(solution)/shard_map/all_gather | solution.py:523
  10.3 118.5 %all-gather.7.cloned.1.call-start = ((), (), s32[]{:S(2)}) async-start(), calls=%async_computation.7 | async-start | bytes 3932160 | tf_op jit(solution)/shard_map/all_gather | solution.py:523
  25.8 181.0 %all-gather.9.cloned.1.call-start = ((), (), s32[]{:S(2)}) async-start(), calls=%async_computation.8 | async-start | bytes 5898240 | tf_op jit(solution)/shard_map/all_gather | solution.py:523
  30.9 28.6 %copy-start.62 = (s32[1,4]{1,0:T(1,128)S(1)}, s32[1,4]{1,0:T(1,128)}, u32[]{:S(2)}) copy-start(s32[1,4]{1,0:T(1,128)} %param.14) | copy-start | bytes 52
  30.9 30.9 %copy-start.2 = (bf16[128,2048]{1,0:T(8,128)(2,1)S(1)}, bf16[128,2048]{1,0:T(8,128)(2,1)}, u32[]{:S(2)}) copy-start(bf16[128,2048]{1,0:T(8,128)(2,1)} %param.13) | copy-start | bytes 1572868
  59.3 217.8 %all-gather.11.cloned.1.call-start = ((), (), s32[]{:S(2)}) async-start(), calls=%async_computation.9 | async-start | bytes 5242880 | tf_op jit(solution)/shard_map/all_gather | solution.py:523
  60.1 46.1 %copy-start.47 = (f32[128]{0:T(128)}, f32[128]{0:T(128)S(1)}, u32[]{:S(2)}) copy-start(f32[128]{0:T(128)S(1)} %multiply_power_fusion) | copy-start | bytes 1540
  60.8 267.6 %copy-start.45 = (pred[128]{0:T(512)(128)(4,1)}, pred[128]{0:T(512)(128)(4,1)S(1)}, u32[]{:S(2)}) copy-start(pred[128]{0:T(512)(128)(4,1)S(1)} %iota_compare_fusion.8) | copy-start | bytes 388
  61.9 37.5 %copy-start.55 = (f32[128]{0:T(128)}, f32[128]{0:T(128)S(1)}, u32[]{:S(2)}) copy-start(f32[128]{0:T(128)S(1)} %fusion.33) | copy-start | bytes 1540
  62.0 42.1 %copy-start.49 = (f32[128]{0:T(128)}, f32[128]{0:T(128)S(1)}, u32[]{:S(2)}) copy-start(f32[128]{0:T(128)S(1)} %fusion.76) | copy-start | bytes 1540
  62.0 43.1 %copy-start.51 = (f32[128]{0:T(128)}, f32[128]{0:T(128)S(1)}, u32[]{:S(2)}) copy-start(f32[128]{0:T(128)S(1)} %subtract_convert_fusion.2) | copy-start | bytes 1540
  99.7 297.3 %copy-start.37 = (f32[1024]{0:T(1024)}, f32[1024]{0:T(1024)S(1)}, u32[]{:S(2)}) copy-start(f32[1024]{0:T(1024)S(1)} %reshape.355) | copy-start | bytes 12292
  105.0 292.0 %copy-start.43 = (f32[128]{0:T(128)}, f32[128]{0:T(128)S(1)}, u32[]{:S(2)}) copy-start(f32[128]{0:T(128)S(1)} %fusion.77) | copy-start | bytes 1540
  109.2 28.8 %copy-start.9 = (f32[8,128,128]{2,1,0:T(8,128)}, f32[8,128,128]{2,1,0:T(8,128)S(1)}, u32[]{:S(2)}) copy-start(f32[8,128,128]{2,1,0:T(8,128)S(1)} %get-tuple-element.116) | copy-start | bytes 1572868
  109.3 254.7 %reduce-scatter.5.cloned.1.call-start = ((), (), s32[]{:S(2)}) async-start(), calls=%async_computation.10 | async-start | bytes 5898240 | tf_op jit(solution)/shard_map/reduce_scatter | solution.py:529
  166.6 161.7 %copy-start.40 = (f32[128]{0:T(128)}, f32[128]{0:T(128)S(1)}, u32[]{:S(2)}) copy-start(f32[128]{0:T(128)S(1)} %fusion.78) | copy-start | bytes 1540
  226.9 211.6 %reduce-scatter.7.cloned.1.call-start = ((), (), s32[]{:S(2)}) async-start(), calls=%async_computation.11 | async-start | bytes 4915200 | tf_op jit(solution)/shard_map/reduce_scatter | solution.py:529
  328.5 23.8 %copy-start.53 = (f32[128]{0:T(128)}, f32[128]{0:T(128)S(1)}, u32[]{:S(2)}) copy-start(f32[128]{0:T(128)S(1)} %multiply_multiply_fusion.2) | copy-start | bytes 1540
  364.0 139.5 %reduce-scatter.9.cloned.1.call-start = ((), (), s32[]{:S(2)}) async-start(), calls=%async_computation.12 | async-start | bytes 3932160 | tf_op jit(solution)/shard_map/reduce_scatter | solution.py:529
  413.2 25.5 %copy-start.26 = (bf16[1024,384]{0,1:T(8,128)(2,1)S(1)}, bf16[1024,384]{0,1:T(8,128)(2,1)}, u32[]{:S(2)}) copy-start(bf16[1024,384]{0,1:T(8,128)(2,1)} %copy-done.25) | copy-start | bytes 2359300
  450.6 55.0 %all-to-all-start.1 = ((bf16[4,128,2112]{1,2,0:T(8,128)(2,1)}), bf16[4,128,2112]{1,2,0:T(8,128)(2,1)}, u32[]{:S(2)}, u32[]{:S(2)}) async-start(bf16[4,128,2112]{1,2,0:T(8,128)(2,1)} %copy_bitcast_fusion), calls=%async_computation.5 | async-start | bytes 4325376 | tf_op jit(solution)/shard_map/all_to_all | solution.py:802
  455.1 72.9 %reduce-scatter.11.cloned.1.call-start = ((), (), s32[]{:S(2)}) async-start(), calls=%async_computation.13 | async-start | bytes 1044480 | tf_op jit(solution)/shard_map/reduce_scatter | solution.py:529
  457.3 41.4 %copy-start.12 = (bf16[8,128,2048]{2,1,0:T(8,128)(2,1)S(1)}, bf16[8,128,2048]{2,1,0:T(8,128)(2,1)}, u32[]{:S(2)}) copy-start(bf16[8,128,2048]{2,1,0:T(8,128)(2,1)} %gather_normed.1) | copy-start | bytes 12582916
  508.0 29.9 %all-to-all-start = ((bf16[8,192,512]{2,1,0:T(8,128)(2,1)}), bf16[8,192,512]{2,1,0:T(8,128)(2,1)}, u32[]{:S(2)}, u32[]{:S(2)}) async-start(bf16[8,192,512]{2,1,0:T(8,128)(2,1)} %bitcast.171), calls=%async_computation.4 | async-start | bytes 3145728 | tf_op jit(solution)/shard_map/all_to_all | solution.py:824
  (51 other events, 216.9 us)
Sparse Core Ops, SparseCore 0:
  10.5 31.1 all-gather.4
  43.8 62.9 all-gather.6
  108.4 88.0 all-gather.8
  197.9 79.2 all-gather.10
  279.3 83.7 reduce-scatter.4
  365.3 73.1 reduce-scatter.6
  440.8 60.6 reduce-scatter.8
  503.8 24.0 reduce-scatter.10

commit v7 on v6

--- a/solution.py
+++ b/solution.py
@@ -582,23 +582,6 @@
         axis=0,
     )
     first_slots = gather_layers(first_pack, layers).reshape(layers, half + EXTRA, wide)
-    out_unit, query_unit = swap(
-        [output_weight, query_up],
-        [columns_of(head_columns)] * 2,
-        [quad_of] * 2,
-        [(QUAD, part, head_columns), (QUAD, rank_part, head_columns)],
-        QUAD_FLIPS,
-        1,
-        "swap_heads",
-    )
-    head_all = gather_layers(
-        jnp.concatenate(
-            [query_unit.reshape(rank_span, head_columns), out_unit.reshape(span, head_columns)]
-        ),
-        layers,
-    ).reshape(layers, rank_span + span, head_columns)
-    query_slice = head_all[:, :rank_span].reshape(rank, head_columns)
-    out_slice = head_all[:, rank_span:].reshape(model, head_columns)
     packs = [
         jnp.concatenate(
             [
@@ -609,8 +592,46 @@
         ).transpose(1, 0, 2)
         for low, high in chunks
     ]
-    feed_units = swap(
-        packs, [quad_of] * 2, [quad_of] * 2, [p.shape for p in packs], QUAD_FLIPS, 2, "swap_feed"
+    out_unit, query_unit, feed_unit = swap(
+        [output_weight, query_up, packs[0]],
+        [columns_of(head_columns)] * 2 + [quad_of],
+        [quad_of] * 3,
+        [(QUAD, part, head_columns), (QUAD, rank_part, head_columns), packs[0].shape],
+        QUAD_FLIPS,
+        1,
+        "swap_heads",
+    )
+    folds = part // rank_part
+    thin = head_columns // folds
+    head_all = gather_layers(
+        jnp.concatenate(
+            [
+                out_unit,
+                feed_unit,
+                query_unit.reshape(QUAD, rank_part, folds, thin)
+                .transpose(0, 2, 1, 3)
+                .reshape(QUAD, part, thin),
+            ],
+            axis=2,
+        ).reshape(span, -1),
+        layers,
+    )
+    out_slice = head_all[:, :head_columns]
+    feed_weights = [head_all[:, head_columns : head_columns + packs[0].shape[2]]]
+    query_slice = (
+        head_all[:, head_columns + packs[0].shape[2] :]
+        .reshape(layers * QUAD, folds, rank_part, thin)
+        .transpose(0, 2, 1, 3)
+        .reshape(rank, head_columns)
+    )
+    [feed_unit] = swap(
+        [after(packs[1], out_unit)],
+        [quad_of],
+        [quad_of],
+        [packs[1].shape],
+        QUAD_FLIPS,
+        2,
+        "swap_feed",
     )
 
     small_width = -(-(2 * part + rank_part + lengths.shape[1]) // 128) * 128
@@ -620,10 +641,7 @@
         "gather_first",
         [inside, stacked],
     )
-    feed_weights = [
-        gather_layers(feed_units[0].reshape(span, -1), layers),
-        gather_layers(after(feed_units[1], first_weight).reshape(span, -1), layers),
-    ]
+    feed_weights.append(gather_layers(after(feed_unit, first_weight).reshape(span, -1), layers))
     first_weight = first_weight.reshape(model, wide)
     small = small[:, :, 0].transpose(1, 0, 2)
     first_gain = small[:, ::PAIR, :part].reshape(model).astype(F32)
@@ -649,6 +667,12 @@
     latent_all, key_all, value_all = gather_layer(
         [latent_normed, key_rot, value_rows], 4, "gather_latent"
     )
+    kept = jnp.where(valid[:, None], upstream, 0.0)
+    grad_rows, normed_rows = gather_layer(
+        [after(kept.astype(BF), latent_all), normed], 15, "gather_upstream"
+    )
+    grad_rows = grad_rows.reshape(all_rows, model)
+    query_slice = after(query_slice, grad_rows)
     latent_all = latent_all.reshape(all_rows, rank)
 
     positions, valids, allowed = jax.vmap(lambda one: layout(one, count_rows))(all_lengths)
@@ -673,15 +697,12 @@
     branch = reduce_layer(branch_terms.reshape(GROUP, count_rows, model), 5, "reduce_branch")
     middle = inputs + branch
     normed_ffn = norm_rows(middle, third_gain).astype(BF)
-    kept = jnp.where(valid[:, None], upstream, 0.0)
-    feed_rows, grad_rows = gather_layer([normed_ffn, kept.astype(BF)], 6, "gather_feed")
+    [feed_rows] = gather_layer([normed_ffn], 6, "gather_feed")
     feed_rows = feed_rows.reshape(all_rows, model)
-    grad_rows = grad_rows.reshape(all_rows, model)
 
     hiddens = []
     ffn_terms = jnp.zeros((all_rows, model), F32)
     grad_packs = []
-    normed_rows = []
     for weights, (low, high) in zip(feed_weights, chunks):
         width = high - low
         gate_up, down = weights[:, : 2 * width], weights[:, 2 * width :]
@@ -699,9 +720,7 @@
         grad_down = matmul("rd,rf->df", grad_rows, hidden).astype(BF)
         grad_pack = jnp.concatenate([grad_both, grad_down], axis=1)
         grad_packs.append(grad_pack)
-        if not normed_rows:
-            normed_rows = gather_layer([after(normed, grad_pack)], 15, "gather_normed")
-        feed_rows = after(feed_rows, grad_pack, normed_rows[0])
+        feed_rows = after(feed_rows, grad_pack)
         both_grad = after(both_grad, grad_pack)
         ffn_terms = ffn_terms + matmul("rf,df->rd", both_grad, gate_up)
         hiddens.append((hidden, down))
@@ -777,7 +796,7 @@
 
     head_pack = after(head_pack, grad_all)
     head_sum = reduce_layers(after(head_pack, *feed_sums), layers)
-    normed_rows = normed_rows[0].reshape(all_rows, model)
+    normed_rows = normed_rows.reshape(all_rows, model)
     gain_sums = jnp.sum(gains_all.astype(F32), axis=0)
     lines = model // rank
     columns = wide // QUAD

time: 558 us -> 552 us (0.989)
  Pallas kernels: 316 us -> 297 us
  waiting for transfers between devices: 24.9 us -> 39.4 us
  matrix products: 96.9 us -> 87.9 us
    pallas_call x4, Pallas kernels: 105 us -> 86.2 us  [reduce_layer(): pl.pallas_call(reduce_kernel, out_shape=jax.ShapeDtypeStruct((rows, colum...]
    reduce_scatter x4, waiting for transfers between devices: 8.43 us -> 24.5 us  [reduce_layers(): lax.psum_scatter(blocks, 'batch', scatter_dimension=0, tiled=True, axis_i...]
    dot_general x27, matrix products: 96.9 us -> 87.9 us  [matmul(): return jnp.einsum(spec, left, right, preferred_element_type=F32)]
    unnamed x141 -> x138, local copies, waits for them, and re-layouts: 16.1 us -> 18.7 us
    all_gather x4 -> x3, waiting for transfers between devices: 16.4 us -> 14.7 us  [gather_layers(): lax.all_gather(unit, 'batch', axis=0, tiled=True, axis_index_groups=layer...]
  transfers between devices with their start and end apart: 10 -> 9, of which waited for: 3 -> 4; matrix products, arithmetic and copies ran while one was open for 31% -> 31% of each run, Pallas kernels for 57% -> 54%
where the time goes in v7:
time: 552 us; the launch traced here: 545 us
  Pallas kernels  297 us (54%)
  matrix products  87.9 us (16%)
  local copies, waits for them, and re-layouts  50.4 us (9%)
  other arithmetic  44.6 us (8%)
  waiting for transfers between devices  39.4 us (7%)
  between operations  15.7 us (3%)
  starting transfers between devices  9.8 us (2%)
    pallas_call x6, Pallas kernels, gather_layer(): pl.pallas_call(functools.partial(gather_kernel, count, cuts, puts), out_s...  154 us
    dot_general x27, matrix products, matmul(): return jnp.einsum(spec, left, right, preferred_element_type=F32)  87.9 us
    pallas_call x4, Pallas kernels, reduce_layer(): pl.pallas_call(reduce_kernel, out_shape=jax.ShapeDtypeStruct((rows, colum...  86.2 us
    pallas_call x2, Pallas kernels, swap(): pl.pallas_call(functools.partial(swap_kernel, count, takes, puts, flips),...  40.5 us
    reduce_scatter x4, waiting for transfers between devices, reduce_layers(): lax.psum_scatter(blocks, 'batch', scatter_dimension=0, tiled=True, axis_i...  24.5 us
    unnamed x138, local copies, waits for them, and re-layouts  18.7 us
    all_gather x3, waiting for transfers between devices, gather_layers(): lax.all_gather(unit, 'batch', axis=0, tiled=True, axis_index_groups=layer...  14.7 us
  transfers between devices with their start and end apart: 9, of which 4 were waited for; matrix products, arithmetic and copies ran while one was open for 31% of the time, Pallas kernels for 54%

profile of v7, /device:TPU:0, one launch (start us, length us, event | category | flops | bytes accessed | tf_op | source)
XLA Modules:
  0.0 544.6 jit_solution(8788361723007878961)
XLA Ops:
  17.4 25.9 %swap_heads.1 = (bf16[4,128,512]{2,1,0:T(8,128)(2,1)}, bf16[4,64,512]{2,1,0:T(8,128)(2,1)}, bf16[4,128,1152]{2,1,0:T(8,128)(2,1)}) custom-call(bf16[128,4096]{1,0:T(8,128)(2,1)} %refs_0_.1, bf16[64,4096]{1,0:T(8,128)(2,1)} %refs_1_.1, bf16[4,128,1152]{2,1,0:T(8,128)(2,1)} %maximum_bitcast_fusion.refs_2_), custom_call_target="tpu_custom_call" | custom-call | bytes 88080384 | tf_op jit(solution)/shard_map/swap_heads/pallas_call | solution.py:365
  50.5 14.6 %swap_feed.1 = bf16[4,128,960]{2,1,0:T(8,128)(2,1)} custom-call(bf16[4,128,960]{2,1,0:T(8,128)(2,1)} %maximum_bitcast_fusion.1.refs_0_), custom_call_target="tpu_custom_call" | custom-call | bytes 31457280 | tf_op jit(solution)/shard_map/swap_feed/pallas_call | solution.py:365
  71.9 32.9 %gather_first.1 = (bf16[4,8,64,1536]{3,2,1,0:T(8,128)(2,1)}, bf16[8,4,16,384]{3,2,1,0:T(8,128)(2,1)}) custom-call(bf16[4,64,1536]{2,1,0:T(8,128)(2,1)} %slice.190.refs_0_, bf16[4,16,384]{2,1,0:T(8,128)(2,1)} %slice.191.refs_1_), custom_call_target="tpu_custom_call" | custom-call | bytes 106954752 | tf_op jit(solution)/shard_map/gather_first/pallas_call | solution.py:201
  113.2 17.9 %gather_latent.1 = (bf16[8,128,1024]{2,1,0:T(8,128)(2,1)}, bf16[8,128,256]{2,1,0:T(8,128)(2,1)}, bf16[8,128,256]{2,1,0:T(8,128)(2,1)}) custom-call(bf16[128,1024]{1,0:T(8,128)(2,1)} %multiply_convert_fusion.8.refs_0_, bf16[128,256]{1,0:T(8,128)(2,1)} %pad_maximum_fusion.14.refs_1_, bf16[128,256]{1,0:T(8,128)(2,1)} %slice.291.refs_2_), custom_call_target="tpu_custom_call" | custom-call | bytes 50331648 | tf_op jit(solution)/shard_map/gather_latent/pallas_call | solution.py:201
  131.0 39.4 %gather_upstream.1 = (bf16[8,128,2048]{2,1,0:T(8,128)(2,1)}, bf16[8,128,2048]{2,1,0:T(8,128)(2,1)}) custom-call(bf16[128,2048]{1,0:T(8,128)(2,1)} %fusion.31.refs_0_, bf16[128,2048]{1,0:T(8,128)(2,1)} %copy-done.5), custom_call_target="tpu_custom_call" | custom-call | bytes 134217728 | tf_op jit(solution)/shard_map/gather_upstream/pallas_call | solution.py:201
  175.0 14.7 %all-gather.6.cloned.1.call-done = bf16[2048,1920]{1,0:T(8,128)(2,1)} async-done(((bf16[512,1920]{1,0:T(8,128)(2,1)}), bf16[2048,1920]{1,0:T(8,128)(2,1)}) %all-gather.6.cloned.1.call-update) | async-done | bytes 7864336 | tf_op jit(solution)/shard_map/all_gather | solution.py:523
  204.5 23.4 %reduce_branch.1 = f32[128,2048]{1,0:T(8,128)S(1)} custom-call(bf16[8,128,2048]{2,1,0:T(8,128)(2,1)S(1)} %bitcast.167), custom_call_target="tpu_custom_call" | custom-call | bytes 67108864 | tf_op jit(solution)/shard_map/reduce_branch/pallas_call | solution.py:302
  229.1 22.0 %gather_feed.1 = bf16[8,128,2048]{2,1,0:T(8,128)(2,1)} custom-call(bf16[128,2048]{1,0:T(8,128)(2,1)} %multiply_convert_fusion.7.refs_0_), custom_call_target="tpu_custom_call" | custom-call | bytes 67108864 | tf_op jit(solution)/shard_map/gather_feed/pallas_call | solution.py:201
  251.1 6.5 %fusion.2 = f32[1024,768]{0,1:T(8,128)S(1)} fusion(bf16[1024,2048]{1,0:T(8,128)(2,1)} %bitcast.174, bf16[2048,1920]{1,0:T(8,128)(2,1)} %all-gather.6.cloned.1.call-done), kind=kOutput, calls=%fused_computation.14 | convolution fusion | flops 3221225472 | bytes 10485760 | tf_op jit(solution)/shard_map/rd,df->rf/dot_general | solution.py:28
  273.7 5.9 %fusion.5 = f32[1024,640]{0,1:T(8,128)S(1)} fusion(bf16[1024,2048]{1,0:T(8,128)(2,1)} %bitcast.175, bf16[2048,960]{1,0:T(8,128)(2,1)} %all-gather.8.cloned.1.call-done), kind=kOutput, calls=%fused_computation.24 | convolution fusion | flops 2684354560 | bytes 9437184 | tf_op jit(solution)/shard_map/rd,df->rf/dot_general | solution.py:28
  292.6 6.1 %fusion = f32[1024,2048]{1,0:T(8,128)S(1)} fusion(bf16[1024,768]{0,1:T(8,128)(2,1)} %pad_maximum_fusion.6, bf16[2048,1920]{1,0:T(8,128)(2,1)} %all-gather.6.cloned.1.call-done), kind=kOutput, calls=%fused_computation.12 | convolution fusion | flops 3221225472 | bytes 13107200 | tf_op jit(solution)/shard_map/rf,df->rd/dot_general | solution.py:28
  302.4 22.8 %reduce_ffn_grad.1 = f32[128,2048]{1,0:T(8,128)S(1)} custom-call(bf16[8,128,2048]{2,1,0:T(8,128)(2,1)S(1)} %bitcast.166), custom_call_target="tpu_custom_call" | custom-call | bytes 67108864 | tf_op jit(solution)/shard_map/reduce_ffn_grad/pallas_call | solution.py:302
  327.4 21.8 %gather_branch.1 = bf16[8,128,2048]{2,1,0:T(8,128)(2,1)} custom-call(bf16[128,2048]{1,0:T(8,128)(2,1)} %fusion.89.refs_0_), custom_call_target="tpu_custom_call" | custom-call | bytes 67108864 | tf_op jit(solution)/shard_map/gather_branch/pallas_call | solution.py:201
  349.3 6.2 %fusion.13 = bf16[1024,512]{1,0:T(8,128)(2,1)} fusion(bf16[1024,2048]{1,0:T(8,128)(2,1)} %bitcast.172, bf16[2048,1920]{1,0:T(8,128)(2,1)} %all-gather.6.cloned.1.call-done), kind=kOutput, calls=%fused_computation.47 | convolution fusion | flops 2148007936 | bytes 7340032 | tf_op jit(solution)/shard_map/rd,df->rf/dot_general | solution.py:28
  375.7 18.0 %reduce_latent.1 = f32[128,1536]{1,0:T(8,128)S(1)} custom-call(bf16[8,128,1536]{2,1,0:T(8,128)(2,1)S(1)} %pad_maximum_fusion.2.in_ref), custom_call_target="tpu_custom_call" | custom-call | bytes 50331648 | tf_op jit(solution)/shard_map/reduce_latent/pallas_call | solution.py:302
  403.5 6.5 %fusion.41 = (f32[128]{0:T(128)}, bf16[2048]{0:T(1024)(128)(2,1)S(1)}, f32[128,2048]{1,0:T(8,128)}) fusion(bf16[128,2048]{1,0:T(8,128)(2,1)S(1)} %copy-done.1, f32[2048]{0:T(1024)S(1)} %convert.95, f32[128]{0:T(128)} %copy-done.47, bf16[2048,1536]{1,0:T(8,128)(2,1)} %bitcast.169, bf16[128,256]{1,0:T(8,128)(2,1)S(1)} %slice.290, ...), kind=kOutput, calls=%fused_computation.85 | convolution fusion | flops 808712064 | bytes 8270848 | tf_op jit(solution)/shard_map/re,de->rd/dot_general | solution.py:28
  410.7 19.5 %gather_last.1 = (bf16[8,128,1536]{2,1,0:T(8,128)(2,1)}, bf16[8,32,1024]{2,1,0:T(8,128)(2,1)}) custom-call(bf16[128,1536]{1,0:T(8,128)(2,1)} %pad_maximum_fusion.13.refs_0_, bf16[32,1024]{1,0:T(8,128)(2,1)} %pad.15.refs_1_), custom_call_target="tpu_custom_call" | custom-call | bytes 58720256 | tf_op jit(solution)/shard_map/gather_last/pallas_call | solution.py:201
  439.6 22.0 %reduce_feed.1 = f32[128,2048]{1,0:T(8,128)S(1)} custom-call(bf16[8,128,2048]{2,1,0:T(8,128)(2,1)S(1)} %bitcast.165), custom_call_target="tpu_custom_call" | custom-call | bytes 67108864 | tf_op jit(solution)/shard_map/reduce_feed/pallas_call | solution.py:302
  465.2 4.7 all-to-all-start.1
  470.0 4.9 convolution_convert_fusion.5
  476.0 18.6 %reduce-scatter.9.cloned.1.call-done = bf16[768,512]{1,0:T(8,128)(2,1)} async-done(((bf16[3072,512]{1,0:T(8,128)(2,1)}), bf16[768,512]{1,0:T(8,128)(2,1)}) %reduce-scatter.9.cloned.1.call-update) | async-done | bytes 786448 | tf_op jit(solution)/shard_map/reduce_scatter | solution.py:529
  500.0 4.3 all-to-all-start
  516.6 4.4 reduce-scatter.11.cloned.1.call-done.refs_0_
  522.6 8.4 %settle_last.1 = (f32[128,1024]{1,0:T(8,128)S(1)}, f32[128,512]{1,0:T(8,128)S(1)}) custom-call(bf16[272,384]{1,0:T(8,128)(2,1)S(1)} %copy-done), custom_call_target="tpu_custom_call" | custom-call | bytes 12582912 | tf_op jit(solution)/shard_map/settle_last/pallas_call | solution.py:459
  (298 shorter events, 157.5 us)
Async XLA Ops:
  7.2 61.3 %all-gather.4.cloned.1.call-start = ((), (), s32[]{:S(2)}) async-start(), calls=%async_computation.6 | async-start | bytes 1351680 | tf_op jit(solution)/shard_map/all_gather | solution.py:523
  10.4 179.4 %all-gather.6.cloned.1.call-start = ((), (), s32[]{:S(2)}) async-start(), calls=%async_computation.7 | async-start | bytes 9830400 | tf_op jit(solution)/shard_map/all_gather | solution.py:523
  47.2 226.5 %all-gather.8.cloned.1.call-start = ((), (), s32[]{:S(2)}) async-start(), calls=%async_computation.8 | async-start | bytes 5242880 | tf_op jit(solution)/shard_map/all_gather | solution.py:523
  48.9 17.8 %copy-start.1 = (bf16[128,2048]{1,0:T(8,128)(2,1)S(1)}, bf16[128,2048]{1,0:T(8,128)(2,1)}, u32[]{:S(2)}) copy-start(bf16[128,2048]{1,0:T(8,128)(2,1)} %param.13) | copy-start | bytes 1572868
  49.2 18.3 %copy-start.6 = (bf16[128,2048]{1,0:T(8,128)(2,1)S(1)}, bf16[128,2048]{1,0:T(8,128)(2,1)}, u32[]{:S(2)}) copy-start(bf16[128,2048]{1,0:T(8,128)(2,1)} %param.25) | copy-start | bytes 1572868
  65.1 106.4 %copy-start.45 = (f32[128]{0:T(128)}, f32[128]{0:T(128)S(1)}, u32[]{:S(2)}) copy-start(f32[128]{0:T(128)S(1)} %multiply_power_fusion) | copy-start | bytes 1540
  65.8 260.3 %copy-start.43 = (pred[128]{0:T(512)(128)(4,1)}, pred[128]{0:T(512)(128)(4,1)S(1)}, u32[]{:S(2)}) copy-start(pred[128]{0:T(512)(128)(4,1)S(1)} %iota_compare_fusion.8) | copy-start | bytes 388
  67.5 43.1 %copy-start.47 = (f32[128]{0:T(128)}, f32[128]{0:T(128)S(1)}, u32[]{:S(2)}) copy-start(f32[128]{0:T(128)S(1)} %fusion.83) | copy-start | bytes 1540
  67.5 43.8 %copy-start.51 = (f32[128]{0:T(128)}, f32[128]{0:T(128)S(1)}, u32[]{:S(2)}) copy-start(f32[128]{0:T(128)S(1)} %subtract_convert_fusion.2) | copy-start | bytes 1540
  106.2 287.6 %copy-start.35 = (f32[1024]{0:T(1024)}, f32[1024]{0:T(1024)S(1)}, u32[]{:S(2)}) copy-start(f32[1024]{0:T(1024)S(1)} %reshape.342) | copy-start | bytes 12292
  112.3 281.5 %copy-start.41 = (f32[128]{0:T(128)}, f32[128]{0:T(128)S(1)}, u32[]{:S(2)}) copy-start(f32[128]{0:T(128)S(1)} %fusion.84) | copy-start | bytes 1540
  174.4 22.4 %copy-start.8 = (f32[8,128,128]{2,1,0:T(8,128)}, f32[8,128,128]{2,1,0:T(8,128)S(1)}, u32[]{:S(2)}) copy-start(f32[8,128,128]{2,1,0:T(8,128)S(1)} %get-tuple-element.118) | copy-start | bytes 1572868
  174.5 186.6 %reduce-scatter.5.cloned.1.call-start = ((), (), s32[]{:S(2)}) async-start(), calls=%async_computation.9 | async-start | bytes 5898240 | tf_op jit(solution)/shard_map/reduce_scatter | solution.py:529
  228.1 98.0 %copy-start.38 = (f32[128]{0:T(128)}, f32[128]{0:T(128)S(1)}, u32[]{:S(2)}) copy-start(f32[128]{0:T(128)S(1)} %fusion.85) | copy-start | bytes 1540
  271.2 160.5 %reduce-scatter.7.cloned.1.call-start = ((), (), s32[]{:S(2)}) async-start(), calls=%async_computation.10 | async-start | bytes 4915200 | tf_op jit(solution)/shard_map/reduce_scatter | solution.py:529
  326.2 23.0 %copy-start.49 = (f32[128]{0:T(128)}, f32[128]{0:T(128)S(1)}, u32[]{:S(2)}) copy-start(f32[128]{0:T(128)S(1)} %multiply_multiply_fusion.2) | copy-start | bytes 1540
  361.1 133.5 %reduce-scatter.9.cloned.1.call-start = ((), (), s32[]{:S(2)}) async-start(), calls=%async_computation.11 | async-start | bytes 3932160 | tf_op jit(solution)/shard_map/reduce_scatter | solution.py:529
  375.7 18.8 %copy-start.57 = (bf16[8,128,1024]{2,1,0:T(8,128)(2,1)S(1)}, bf16[8,128,1024]{2,1,0:T(8,128)(2,1)}, u32[]{:S(2)}) copy-start(bf16[8,128,1024]{2,1,0:T(8,128)(2,1)} %get-tuple-element.55) | copy-start | bytes 6291460
  410.0 21.9 %copy-start.24 = (bf16[1024,384]{0,1:T(8,128)(2,1)S(1)}, bf16[1024,384]{0,1:T(8,128)(2,1)}, u32[]{:S(2)}) copy-start(bf16[1024,384]{0,1:T(8,128)(2,1)} %copy-done.23) | copy-start | bytes 2359300
  465.2 32.3 %all-to-all-start.1 = ((bf16[4,128,2112]{1,2,0:T(8,128)(2,1)}), bf16[4,128,2112]{1,2,0:T(8,128)(2,1)}, u32[]{:S(2)}, u32[]{:S(2)}) async-start(bf16[4,128,2112]{1,2,0:T(8,128)(2,1)} %copy_bitcast_fusion), calls=%async_computation.5 | async-start | bytes 4325376 | tf_op jit(solution)/shard_map/all_to_all | solution.py:821
  469.9 51.1 %reduce-scatter.11.cloned.1.call-start = ((), (), s32[]{:S(2)}) async-start(), calls=%async_computation.12 | async-start | bytes 1044480 | tf_op jit(solution)/shard_map/reduce_scatter | solution.py:529
  497.5 6.8 %copy-start.48 = (f32[128]{0:T(128)S(1)}, f32[128]{0:T(128)}, u32[]{:S(2)}) copy-start(f32[128]{0:T(128)} %copy-done.47) | copy-start | bytes 1540
  497.6 6.8 %copy-start.50 = (f32[128]{0:T(128)S(1)}, f32[128]{0:T(128)}, u32[]{:S(2)}) copy-start(f32[128]{0:T(128)} %copy-done.49) | copy-start | bytes 1540
  500.0 31.0 %all-to-all-start = ((bf16[8,192,512]{2,1,0:T(8,128)(2,1)}), bf16[8,192,512]{2,1,0:T(8,128)(2,1)}, u32[]{:S(2)}, u32[]{:S(2)}) async-start(bf16[8,192,512]{2,1,0:T(8,128)(2,1)} %bitcast.171), calls=%async_computation.4 | async-start | bytes 3145728 | tf_op jit(solution)/shard_map/all_to_all | solution.py:843
  (48 other events, 151.1 us)
Sparse Core Ops, SparseCore 0:
  10.5 31.1 all-gather.3
  47.3 142.4 all-gather.5
  191.3 78.9 all-gather.7
  272.5 83.7 reduce-scatter.4
  361.2 70.5 reduce-scatter.6
  433.9 60.5 reduce-scatter.8
  496.8 24.0 reduce-scatter.10

commit v8 on v7

--- a/solution.py
+++ b/solution.py
@@ -324,9 +324,10 @@
     )(blocks)
 
 
-def swap_kernel(count, takes, puts, flips, *refs):
-    ins, outs = refs[:count], refs[count : 2 * count]
-    local_sem, send_sem, recv_sem = refs[2 * count :]
+def swap_kernel(count, homes, takes, puts, flips, *refs):
+    outs = refs[count:-3]
+    ins, outs = refs[:count], [outs[home] for home in homes]
+    local_sem, send_sem, recv_sem = refs[-3:]
     base, quad, hid = place()
     address, index = ways_of(base, quad, hid)
     meet([address(f) for f in flips])
@@ -359,14 +360,15 @@
 ALL_FLIPS = ((3, 1), (2, 1), (3, 0), (2, 0), (1, 1), (0, 1), (1, 0))
 
 
-def swap(arrays, takes, puts, shapes, flips, ident, name):
+def swap(arrays, takes, puts, shapes, flips, ident, name, homes=None):
     count = len(arrays)
+    homes = homes or range(count)
     moved = sum(a.size * 2 for a in arrays)
     return pl.pallas_call(
-        functools.partial(swap_kernel, count, takes, puts, flips),
-        out_shape=[jax.ShapeDtypeStruct(s, a.dtype) for s, a in zip(shapes, arrays)],
+        functools.partial(swap_kernel, count, homes, takes, puts, flips),
+        out_shape=[jax.ShapeDtypeStruct(s, BF) for s in shapes],
         in_specs=[pl.BlockSpec(memory_space=pl.ANY)] * count,
-        out_specs=[pl.BlockSpec(memory_space=pl.ANY)] * count,
+        out_specs=[pl.BlockSpec(memory_space=pl.ANY)] * len(shapes),
         scratch_shapes=[
             pltpu.SemaphoreType.DMA((count,)),
             pltpu.SemaphoreType.DMA((count, len(flips))),
@@ -592,40 +594,47 @@
         ).transpose(1, 0, 2)
         for low, high in chunks
     ]
-    out_unit, query_unit, feed_unit = swap(
-        [output_weight, query_up, packs[0]],
-        [columns_of(head_columns)] * 2 + [quad_of],
-        [quad_of] * 3,
-        [(QUAD, part, head_columns), (QUAD, rank_part, head_columns), packs[0].shape],
+    folds = part // rank_part
+    thin = head_columns // folds
+    feed_end = head_columns + packs[0].shape[2]
+
+    def fold_of(fold):
+        def take(ref, i):
+            begin = pl.multiple_of(i * head_columns, head_columns) + fold * thin
+            return ref.at[:, pl.ds(begin, thin)]
+
+        def put(ref, i):
+            rows = pl.ds(fold * rank_part, rank_part)
+            return ref.at[i // PAIR, rows, pl.ds(feed_end, thin)]
+
+        return take, put
+
+    fold_ways = [fold_of(fold) for fold in range(folds)]
+    [head_unit] = swap(
+        [output_weight, packs[0]] + [query_up] * folds,
+        [columns_of(head_columns), quad_of] + [take for take, put in fold_ways],
+        [
+            lambda ref, i: ref.at[i // PAIR, :, pl.ds(0, head_columns)],
+            lambda ref, i: ref.at[i // PAIR, :, pl.ds(head_columns, feed_end - head_columns)],
+        ]
+        + [put for take, put in fold_ways],
+        [(QUAD, part, feed_end + thin)],
         QUAD_FLIPS,
         1,
         "swap_heads",
-    )
-    folds = part // rank_part
-    thin = head_columns // folds
-    head_all = gather_layers(
-        jnp.concatenate(
-            [
-                out_unit,
-                feed_unit,
-                query_unit.reshape(QUAD, rank_part, folds, thin)
-                .transpose(0, 2, 1, 3)
-                .reshape(QUAD, part, thin),
-            ],
-            axis=2,
-        ).reshape(span, -1),
-        layers,
-    )
+        [0] * (2 + folds),
+    )
+    head_all = gather_layers(head_unit.reshape(span, -1), layers)
     out_slice = head_all[:, :head_columns]
-    feed_weights = [head_all[:, head_columns : head_columns + packs[0].shape[2]]]
+    feed_weights = [head_all[:, head_columns:feed_end]]
     query_slice = (
-        head_all[:, head_columns + packs[0].shape[2] :]
+        head_all[:, feed_end:]
         .reshape(layers * QUAD, folds, rank_part, thin)
         .transpose(0, 2, 1, 3)
         .reshape(rank, head_columns)
     )
     [feed_unit] = swap(
-        [after(packs[1], out_unit)],
+        [after(packs[1], head_unit)],
         [quad_of],
         [quad_of],
         [packs[1].shape],

time: 552 us -> 548 us (level)
  transfers between devices with their start and end apart: 9 -> 9, of which waited for: 4 -> 4; matrix products, arithmetic and copies ran while one was open for 31% -> 30% of each run, Pallas kernels for 54% -> 54%
where the time goes in v8:
time: 548 us; the launch traced here: 541 us
  Pallas kernels  297 us (54%)
  matrix products  88 us (16%)
  local copies, waits for them, and re-layouts  49.3 us (9%)
  other arithmetic  41.8 us (8%)
  waiting for transfers between devices  39.5 us (7%)
  between operations  15.7 us (3%)
  starting transfers between devices  9.81 us (2%)
    pallas_call x6, Pallas kernels, gather_layer(): pl.pallas_call(functools.partial(gather_kernel, count, cuts, puts), out_s...  153 us
    dot_general x27, matrix products, matmul(): return jnp.einsum(spec, left, right, preferred_element_type=F32)  88 us
    pallas_call x4, Pallas kernels, reduce_layer(): pl.pallas_call(reduce_kernel, out_shape=jax.ShapeDtypeStruct((rows, colum...  86.2 us
    pallas_call x2, Pallas kernels, swap(): pl.pallas_call(functools.partial(swap_kernel, count, homes, takes, puts,...  40.6 us
    reduce_scatter x4, waiting for transfers between devices, reduce_layers(): lax.psum_scatter(blocks, 'batch', scatter_dimension=0, tiled=True, axis_i...  24.6 us
    unnamed x138, local copies, waits for them, and re-layouts  18.7 us
    all_gather x3, waiting for transfers between devices, gather_layers(): lax.all_gather(unit, 'batch', axis=0, tiled=True, axis_index_groups=layer...  14.8 us
  transfers between devices with their start and end apart: 9, of which 4 were waited for; matrix products, arithmetic and copies ran while one was open for 30% of the time, Pallas kernels for 54%

profile of v8, /device:TPU:0, one launch (start us, length us, event | category | flops | bytes accessed | tf_op | source)
XLA Modules:
  0.0 540.8 jit_solution(8398151671650198518)
XLA Ops:
  17.4 25.9 %swap_heads.1 = bf16[4,128,1920]{2,1,0:T(8,128)(2,1)} custom-call(bf16[128,4096]{1,0:T(8,128)(2,1)} %refs_0_.1, bf16[4,128,1152]{2,1,0:T(8,128)(2,1)} %maximum_bitcast_fusion.refs_1_, bf16[64,4096]{1,0:T(8,128)(2,1)} %refs_3_.1, bf16[64,4096]{1,0:T(8,128)(2,1)} %refs_3_.1), custom_call_target="tpu_custom_call" | custom-call | bytes 104857600 | tf_op jit(solution)/shard_map/swap_heads/pallas_call | solution.py:367
  46.7 14.6 %swap_feed.1 = bf16[4,128,960]{2,1,0:T(8,128)(2,1)} custom-call(bf16[4,128,960]{2,1,0:T(8,128)(2,1)} %maximum_bitcast_fusion.1.refs_0_), custom_call_target="tpu_custom_call" | custom-call | bytes 31457280 | tf_op jit(solution)/shard_map/swap_feed/pallas_call | solution.py:367
  68.1 32.9 %gather_first.1 = (bf16[4,8,64,1536]{3,2,1,0:T(8,128)(2,1)}, bf16[8,4,16,384]{3,2,1,0:T(8,128)(2,1)}) custom-call(bf16[4,64,1536]{2,1,0:T(8,128)(2,1)} %slice.190.refs_0_, bf16[4,16,384]{2,1,0:T(8,128)(2,1)} %slice.191.refs_1_), custom_call_target="tpu_custom_call" | custom-call | bytes 106954752 | tf_op jit(solution)/shard_map/gather_first/pallas_call | solution.py:201
  109.3 17.9 %gather_latent.1 = (bf16[8,128,1024]{2,1,0:T(8,128)(2,1)}, bf16[8,128,256]{2,1,0:T(8,128)(2,1)}, bf16[8,128,256]{2,1,0:T(8,128)(2,1)}) custom-call(bf16[128,1024]{1,0:T(8,128)(2,1)} %multiply_convert_fusion.8.refs_0_, bf16[128,256]{1,0:T(8,128)(2,1)} %pad_maximum_fusion.13.refs_1_, bf16[128,256]{1,0:T(8,128)(2,1)} %slice.291.refs_2_), custom_call_target="tpu_custom_call" | custom-call | bytes 50331648 | tf_op jit(solution)/shard_map/gather_latent/pallas_call | solution.py:201
  127.2 39.4 %gather_upstream.1 = (bf16[8,128,2048]{2,1,0:T(8,128)(2,1)}, bf16[8,128,2048]{2,1,0:T(8,128)(2,1)}) custom-call(bf16[128,2048]{1,0:T(8,128)(2,1)} %fusion.31.refs_0_, bf16[128,2048]{1,0:T(8,128)(2,1)} %copy-done.5), custom_call_target="tpu_custom_call" | custom-call | bytes 134217728 | tf_op jit(solution)/shard_map/gather_upstream/pallas_call | solution.py:201
  171.2 14.8 %all-gather.6.cloned.1.call-done = bf16[2048,1920]{1,0:T(8,128)(2,1)} async-done(((bf16[512,1920]{1,0:T(8,128)(2,1)}), bf16[2048,1920]{1,0:T(8,128)(2,1)}) %all-gather.6.cloned.1.call-update) | async-done | bytes 7864336 | tf_op jit(solution)/shard_map/all_gather | solution.py:525
  200.7 23.4 %reduce_branch.1 = f32[128,2048]{1,0:T(8,128)S(1)} custom-call(bf16[8,128,2048]{2,1,0:T(8,128)(2,1)S(1)} %bitcast.164), custom_call_target="tpu_custom_call" | custom-call | bytes 67108864 | tf_op jit(solution)/shard_map/reduce_branch/pallas_call | solution.py:302
  225.3 22.0 %gather_feed.1 = bf16[8,128,2048]{2,1,0:T(8,128)(2,1)} custom-call(bf16[128,2048]{1,0:T(8,128)(2,1)} %multiply_convert_fusion.7.refs_0_), custom_call_target="tpu_custom_call" | custom-call | bytes 67108864 | tf_op jit(solution)/shard_map/gather_feed/pallas_call | solution.py:201
  247.3 6.5 %fusion.2 = f32[1024,768]{0,1:T(8,128)S(1)} fusion(bf16[1024,2048]{1,0:T(8,128)(2,1)} %bitcast.172, bf16[2048,1920]{1,0:T(8,128)(2,1)} %all-gather.6.cloned.1.call-done), kind=kOutput, calls=%fused_computation.14 | convolution fusion | flops 3221225472 | bytes 10485760 | tf_op jit(solution)/shard_map/rd,df->rf/dot_general | solution.py:28
  269.9 5.9 %fusion.5 = f32[1024,640]{0,1:T(8,128)S(1)} fusion(bf16[1024,2048]{1,0:T(8,128)(2,1)} %bitcast.173, bf16[2048,960]{1,0:T(8,128)(2,1)} %all-gather.8.cloned.1.call-done), kind=kOutput, calls=%fused_computation.24 | convolution fusion | flops 2684354560 | bytes 9437184 | tf_op jit(solution)/shard_map/rd,df->rf/dot_general | solution.py:28
  288.7 6.1 %fusion = f32[1024,2048]{1,0:T(8,128)S(1)} fusion(bf16[1024,768]{0,1:T(8,128)(2,1)} %pad_maximum_fusion.5, bf16[2048,1920]{1,0:T(8,128)(2,1)} %all-gather.6.cloned.1.call-done), kind=kOutput, calls=%fused_computation.12 | convolution fusion | flops 3221225472 | bytes 13107200 | tf_op jit(solution)/shard_map/rf,df->rd/dot_general | solution.py:28
  298.6 22.8 %reduce_ffn_grad.1 = f32[128,2048]{1,0:T(8,128)S(1)} custom-call(bf16[8,128,2048]{2,1,0:T(8,128)(2,1)S(1)} %bitcast.163), custom_call_target="tpu_custom_call" | custom-call | bytes 67108864 | tf_op jit(solution)/shard_map/reduce_ffn_grad/pallas_call | solution.py:302
  323.6 21.7 %gather_branch.1 = bf16[8,128,2048]{2,1,0:T(8,128)(2,1)} custom-call(bf16[128,2048]{1,0:T(8,128)(2,1)} %fusion.89.refs_0_), custom_call_target="tpu_custom_call" | custom-call | bytes 67108864 | tf_op jit(solution)/shard_map/gather_branch/pallas_call | solution.py:201
  345.4 6.3 %fusion.13 = bf16[1024,512]{1,0:T(8,128)(2,1)} fusion(bf16[1024,2048]{1,0:T(8,128)(2,1)} %bitcast.170, bf16[2048,1920]{1,0:T(8,128)(2,1)} %all-gather.6.cloned.1.call-done), kind=kOutput, calls=%fused_computation.46 | convolution fusion | flops 2148007936 | bytes 7340032 | tf_op jit(solution)/shard_map/rd,df->rf/dot_general | solution.py:28
  371.8 18.0 %reduce_latent.1 = f32[128,1536]{1,0:T(8,128)S(1)} custom-call(bf16[8,128,1536]{2,1,0:T(8,128)(2,1)S(1)} %pad_maximum_fusion.2.in_ref), custom_call_target="tpu_custom_call" | custom-call | bytes 50331648 | tf_op jit(solution)/shard_map/reduce_latent/pallas_call | solution.py:302
  399.6 6.5 %fusion.41 = (f32[128]{0:T(128)}, bf16[2048]{0:T(1024)(128)(2,1)S(1)}, f32[128,2048]{1,0:T(8,128)}) fusion(bf16[128,2048]{1,0:T(8,128)(2,1)S(1)} %copy-done.1, f32[2048]{0:T(1024)S(1)} %convert.95, f32[128]{0:T(128)} %copy-done.47, bf16[2048,1536]{1,0:T(8,128)(2,1)} %bitcast.166, bf16[128,256]{1,0:T(8,128)(2,1)S(1)} %slice.290, ...), kind=kOutput, calls=%fused_computation.84 | convolution fusion | flops 808712064 | bytes 8270848 | tf_op jit(solution)/shard_map/re,de->rd/dot_general | solution.py:28
  406.8 19.5 %gather_last.1 = (bf16[8,128,1536]{2,1,0:T(8,128)(2,1)}, bf16[8,32,1024]{2,1,0:T(8,128)(2,1)}) custom-call(bf16[128,1536]{1,0:T(8,128)(2,1)} %pad_maximum_fusion.12.refs_0_, bf16[32,1024]{1,0:T(8,128)(2,1)} %pad.15.refs_1_), custom_call_target="tpu_custom_call" | custom-call | bytes 58720256 | tf_op jit(solution)/shard_map/gather_last/pallas_call | solution.py:201
  435.8 22.0 %reduce_feed.1 = f32[128,2048]{1,0:T(8,128)S(1)} custom-call(bf16[8,128,2048]{2,1,0:T(8,128)(2,1)S(1)} %bitcast.162), custom_call_target="tpu_custom_call" | custom-call | bytes 67108864 | tf_op jit(solution)/shard_map/reduce_feed/pallas_call | solution.py:302
  461.4 4.7 all-to-all-start.1
  466.2 4.9 convolution_convert_fusion.5
  472.1 18.6 %reduce-scatter.9.cloned.1.call-done = bf16[768,512]{1,0:T(8,128)(2,1)} async-done(((bf16[3072,512]{1,0:T(8,128)(2,1)}), bf16[768,512]{1,0:T(8,128)(2,1)}) %reduce-scatter.9.cloned.1.call-update) | async-done | bytes 786448 | tf_op jit(solution)/shard_map/reduce_scatter | solution.py:531
  496.2 4.3 all-to-all-start
  512.8 4.4 reduce-scatter.11.cloned.1.call-done.refs_0_
  518.8 8.4 %settle_last.1 = (f32[128,1024]{1,0:T(8,128)S(1)}, f32[128,512]{1,0:T(8,128)S(1)}) custom-call(bf16[272,384]{1,0:T(8,128)(2,1)S(1)} %copy-done), custom_call_target="tpu_custom_call" | custom-call | bytes 12582912 | tf_op jit(solution)/shard_map/settle_last/pallas_call | solution.py:461
  (295 shorter events, 153.7 us)
Async XLA Ops:
  7.2 57.4 %all-gather.4.cloned.1.call-start = ((), (), s32[]{:S(2)}) async-start(), calls=%async_computation.6 | async-start | bytes 1351680 | tf_op jit(solution)/shard_map/all_gather | solution.py:525
  10.4 175.6 %all-gather.6.cloned.1.call-start = ((), (), s32[]{:S(2)}) async-start(), calls=%async_computation.7 | async-start | bytes 9830400 | tf_op jit(solution)/shard_map/all_gather | solution.py:525
  43.4 226.5 %all-gather.8.cloned.1.call-start = ((), (), s32[]{:S(2)}) async-start(), calls=%async_computation.8 | async-start | bytes 5242880 | tf_op jit(solution)/shard_map/all_gather | solution.py:525
  45.1 17.8 %copy-start.1 = (bf16[128,2048]{1,0:T(8,128)(2,1)S(1)}, bf16[128,2048]{1,0:T(8,128)(2,1)}, u32[]{:S(2)}) copy-start(bf16[128,2048]{1,0:T(8,128)(2,1)} %param.13) | copy-start | bytes 1572868
  45.4 18.3 %copy-start.6 = (bf16[128,2048]{1,0:T(8,128)(2,1)S(1)}, bf16[128,2048]{1,0:T(8,128)(2,1)}, u32[]{:S(2)}) copy-start(bf16[128,2048]{1,0:T(8,128)(2,1)} %param.25) | copy-start | bytes 1572868
  61.3 106.3 %copy-start.45 = (f32[128]{0:T(128)}, f32[128]{0:T(128)S(1)}, u32[]{:S(2)}) copy-start(f32[128]{0:T(128)S(1)} %multiply_power_fusion) | copy-start | bytes 1540
  62.0 260.3 %copy-start.43 = (pred[128]{0:T(512)(128)(4,1)}, pred[128]{0:T(512)(128)(4,1)S(1)}, u32[]{:S(2)}) copy-start(pred[128]{0:T(512)(128)(4,1)S(1)} %iota_compare_fusion.8) | copy-start | bytes 388
  63.6 43.1 %copy-start.47 = (f32[128]{0:T(128)}, f32[128]{0:T(128)S(1)}, u32[]{:S(2)}) copy-start(f32[128]{0:T(128)S(1)} %fusion.83) | copy-start | bytes 1540
  63.6 43.8 %copy-start.51 = (f32[128]{0:T(128)}, f32[128]{0:T(128)S(1)}, u32[]{:S(2)}) copy-start(f32[128]{0:T(128)S(1)} %subtract_convert_fusion.2) | copy-start | bytes 1540
  102.3 287.6 %copy-start.35 = (f32[1024]{0:T(1024)}, f32[1024]{0:T(1024)S(1)}, u32[]{:S(2)}) copy-start(f32[1024]{0:T(1024)S(1)} %reshape.336) | copy-start | bytes 12292
  108.5 281.4 %copy-start.41 = (f32[128]{0:T(128)}, f32[128]{0:T(128)S(1)}, u32[]{:S(2)}) copy-start(f32[128]{0:T(128)S(1)} %fusion.84) | copy-start | bytes 1540
  170.6 22.5 %copy-start.8 = (f32[8,128,128]{2,1,0:T(8,128)}, f32[8,128,128]{2,1,0:T(8,128)S(1)}, u32[]{:S(2)}) copy-start(f32[8,128,128]{2,1,0:T(8,128)S(1)} %get-tuple-element.112) | copy-start | bytes 1572868
  170.6 186.5 %reduce-scatter.5.cloned.1.call-start = ((), (), s32[]{:S(2)}) async-start(), calls=%async_computation.9 | async-start | bytes 5898240 | tf_op jit(solution)/shard_map/reduce_scatter | solution.py:531
  224.3 97.9 %copy-start.38 = (f32[128]{0:T(128)}, f32[128]{0:T(128)S(1)}, u32[]{:S(2)}) copy-start(f32[128]{0:T(128)S(1)} %fusion.85) | copy-start | bytes 1540
  267.4 160.5 %reduce-scatter.7.cloned.1.call-start = ((), (), s32[]{:S(2)}) async-start(), calls=%async_computation.10 | async-start | bytes 4915200 | tf_op jit(solution)/shard_map/reduce_scatter | solution.py:531
  322.4 23.0 %copy-start.49 = (f32[128]{0:T(128)}, f32[128]{0:T(128)S(1)}, u32[]{:S(2)}) copy-start(f32[128]{0:T(128)S(1)} %multiply_multiply_fusion.2) | copy-start | bytes 1540
  357.2 133.6 %reduce-scatter.9.cloned.1.call-start = ((), (), s32[]{:S(2)}) async-start(), calls=%async_computation.11 | async-start | bytes 3932160 | tf_op jit(solution)/shard_map/reduce_scatter | solution.py:531
  371.8 18.8 %copy-start.57 = (bf16[8,128,1024]{2,1,0:T(8,128)(2,1)S(1)}, bf16[8,128,1024]{2,1,0:T(8,128)(2,1)}, u32[]{:S(2)}) copy-start(bf16[8,128,1024]{2,1,0:T(8,128)(2,1)} %get-tuple-element.52) | copy-start | bytes 6291460
  406.1 22.0 %copy-start.24 = (bf16[1024,384]{0,1:T(8,128)(2,1)S(1)}, bf16[1024,384]{0,1:T(8,128)(2,1)}, u32[]{:S(2)}) copy-start(bf16[1024,384]{0,1:T(8,128)(2,1)} %copy-done.23) | copy-start | bytes 2359300
  461.4 32.4 %all-to-all-start.1 = ((bf16[4,128,2112]{1,2,0:T(8,128)(2,1)}), bf16[4,128,2112]{1,2,0:T(8,128)(2,1)}, u32[]{:S(2)}, u32[]{:S(2)}) async-start(bf16[4,128,2112]{1,2,0:T(8,128)(2,1)} %copy_bitcast_fusion), calls=%async_computation.5 | async-start | bytes 4325376 | tf_op jit(solution)/shard_map/all_to_all | solution.py:830
  466.1 51.1 %reduce-scatter.11.cloned.1.call-start = ((), (), s32[]{:S(2)}) async-start(), calls=%async_computation.12 | async-start | bytes 1044480 | tf_op jit(solution)/shard_map/reduce_scatter | solution.py:531
  493.7 6.8 %copy-start.48 = (f32[128]{0:T(128)S(1)}, f32[128]{0:T(128)}, u32[]{:S(2)}) copy-start(f32[128]{0:T(128)} %copy-done.47) | copy-start | bytes 1540
  493.8 6.8 %copy-start.50 = (f32[128]{0:T(128)S(1)}, f32[128]{0:T(128)}, u32[]{:S(2)}) copy-start(f32[128]{0:T(128)} %copy-done.49) | copy-start | bytes 1540
  496.2 31.0 %all-to-all-start = ((bf16[8,192,512]{2,1,0:T(8,128)(2,1)}), bf16[8,192,512]{2,1,0:T(8,128)(2,1)}, u32[]{:S(2)}, u32[]{:S(2)}) async-start(bf16[8,192,512]{2,1,0:T(8,128)(2,1)} %bitcast.169), calls=%async_computation.4 | async-start | bytes 3145728 | tf_op jit(solution)/shard_map/all_to_all | solution.py:852
  (48 other events, 151.2 us)
Sparse Core Ops, SparseCore 0:
  10.5 31.1 all-gather.3
  43.5 142.4 all-gather.5
  187.5 78.9 all-gather.7
  268.7 83.7 reduce-scatter.4
  357.3 70.6 reduce-scatter.6
  430.1 60.5 reduce-scatter.8
  493.0 24.1 reduce-scatter.10

commit v9 on v8

--- a/solution.py
+++ b/solution.py
@@ -772,10 +772,10 @@
     grad_out = matmul("rd,rf->df", after(branch_rows, back), mixed).astype(BF)
     head_pack = jnp.concatenate(
         [
-            grad_query.reshape(layers, rank_span, head_columns),
-            grad_out.reshape(layers, span, head_columns),
-        ],
-        axis=1,
+            grad_query.reshape(layers, QUAD, rank_part, head_columns),
+            grad_out.reshape(layers, QUAD, part, head_columns),
+        ],
+        axis=2,
     ).reshape(rank + model, head_columns)
 
     latent_normed_grad = back[:, :rank]
@@ -847,17 +847,10 @@
     last_sum = reduce_layers(last_pack, layers)
     small_sum = last_sum[QUAD * half :].astype(F32).reshape(-1)
 
-    query_sum, out_sum = head_sum[:rank_span], head_sum[rank_span:]
     groups = [[z * GROUP + i for i in range(GROUP)] for z in range(layers)]
     head_own = lax.all_to_all(
         jnp.repeat(
-            jnp.concatenate(
-                [
-                    query_sum.reshape(QUAD, rank_part, head_columns),
-                    out_sum.reshape(QUAD, part, head_columns),
-                ],
-                axis=1,
-            ),
+            head_sum.reshape(QUAD, rank_part + part, head_columns),
             PAIR,
             axis=0,
         ),

time: 548 us -> 548 us (level)
  transfers between devices with their start and end apart: 9 -> 9, of which waited for: 4 -> 5; matrix products, arithmetic and copies ran while one was open for 30% -> 29% of each run, Pallas kernels for 54% -> 54%
where the time goes in v9:
time: 548 us; the launch traced here: 541 us
  Pallas kernels  297 us (54%)
  matrix products  88 us (16%)
  local copies, waits for them, and re-layouts  47.3 us (9%)
  waiting for transfers between devices  42.5 us (8%)
  other arithmetic  40.9 us (7%)
  between operations  15.7 us (3%)
  starting transfers between devices  9.8 us (2%)
    pallas_call x6, Pallas kernels, gather_layer(): pl.pallas_call(functools.partial(gather_kernel, count, cuts, puts), out_s...  153 us
    dot_general x27, matrix products, matmul(): return jnp.einsum(spec, left, right, preferred_element_type=F32)  88 us
    pallas_call x4, Pallas kernels, reduce_layer(): pl.pallas_call(reduce_kernel, out_shape=jax.ShapeDtypeStruct((rows, colum...  86.2 us
    pallas_call x2, Pallas kernels, swap(): pl.pallas_call(functools.partial(swap_kernel, count, homes, takes, puts,...  40.6 us
    reduce_scatter x4, waiting for transfers between devices, reduce_layers(): lax.psum_scatter(blocks, 'batch', scatter_dimension=0, tiled=True, axis_i...  25.8 us
    unnamed x138, local copies, waits for them, and re-layouts  18.7 us
    all_gather x3, waiting for transfers between devices, gather_layers(): lax.all_gather(unit, 'batch', axis=0, tiled=True, axis_index_groups=layer...  14.8 us
  transfers between devices with their start and end apart: 9, of which 5 were waited for; matrix products, arithmetic and copies ran while one was open for 29% of the time, Pallas kernels for 54%

profile of v9, /device:TPU:0, one launch (start us, length us, event | category | flops | bytes accessed | tf_op | source)
XLA Modules:
  0.0 540.8 jit_solution(12044969347513370148)
XLA Ops:
  17.4 25.9 %swap_heads.1 = bf16[4,128,1920]{2,1,0:T(8,128)(2,1)} custom-call(bf16[128,4096]{1,0:T(8,128)(2,1)} %refs_0_.1, bf16[4,128,1152]{2,1,0:T(8,128)(2,1)} %maximum_bitcast_fusion.refs_1_, bf16[64,4096]{1,0:T(8,128)(2,1)} %refs_3_.1, bf16[64,4096]{1,0:T(8,128)(2,1)} %refs_3_.1), custom_call_target="tpu_custom_call" | custom-call | bytes 104857600 | tf_op jit(solution)/shard_map/swap_heads/pallas_call | solution.py:367
  46.7 14.6 %swap_feed.1 = bf16[4,128,960]{2,1,0:T(8,128)(2,1)} custom-call(bf16[4,128,960]{2,1,0:T(8,128)(2,1)} %maximum_bitcast_fusion.1.refs_0_), custom_call_target="tpu_custom_call" | custom-call | bytes 31457280 | tf_op jit(solution)/shard_map/swap_feed/pallas_call | solution.py:367
  68.1 32.9 %gather_first.1 = (bf16[4,8,64,1536]{3,2,1,0:T(8,128)(2,1)}, bf16[8,4,16,384]{3,2,1,0:T(8,128)(2,1)}) custom-call(bf16[4,64,1536]{2,1,0:T(8,128)(2,1)} %slice.182.refs_0_, bf16[4,16,384]{2,1,0:T(8,128)(2,1)} %slice.183.refs_1_), custom_call_target="tpu_custom_call" | custom-call | bytes 106954752 | tf_op jit(solution)/shard_map/gather_first/pallas_call | solution.py:201
  109.3 17.9 %gather_latent.1 = (bf16[8,128,1024]{2,1,0:T(8,128)(2,1)}, bf16[8,128,256]{2,1,0:T(8,128)(2,1)}, bf16[8,128,256]{2,1,0:T(8,128)(2,1)}) custom-call(bf16[128,1024]{1,0:T(8,128)(2,1)} %multiply_convert_fusion.8.refs_0_, bf16[128,256]{1,0:T(8,128)(2,1)} %pad_maximum_fusion.12.refs_1_, bf16[128,256]{1,0:T(8,128)(2,1)} %slice.281.refs_2_), custom_call_target="tpu_custom_call" | custom-call | bytes 50331648 | tf_op jit(solution)/shard_map/gather_latent/pallas_call | solution.py:201
  127.2 39.4 %gather_upstream.1 = (bf16[8,128,2048]{2,1,0:T(8,128)(2,1)}, bf16[8,128,2048]{2,1,0:T(8,128)(2,1)}) custom-call(bf16[128,2048]{1,0:T(8,128)(2,1)} %fusion.31.refs_0_, bf16[128,2048]{1,0:T(8,128)(2,1)} %copy-done.5), custom_call_target="tpu_custom_call" | custom-call | bytes 134217728 | tf_op jit(solution)/shard_map/gather_upstream/pallas_call | solution.py:201
  171.2 14.8 %all-gather.6.cloned.1.call-done = bf16[2048,1920]{1,0:T(8,128)(2,1)} async-done(((bf16[512,1920]{1,0:T(8,128)(2,1)}), bf16[2048,1920]{1,0:T(8,128)(2,1)}) %all-gather.6.cloned.1.call-update) | async-done | bytes 7864336 | tf_op jit(solution)/shard_map/all_gather | solution.py:525
  200.7 23.4 %reduce_branch.1 = f32[128,2048]{1,0:T(8,128)S(1)} custom-call(bf16[8,128,2048]{2,1,0:T(8,128)(2,1)S(1)} %bitcast.163), custom_call_target="tpu_custom_call" | custom-call | bytes 67108864 | tf_op jit(solution)/shard_map/reduce_branch/pallas_call | solution.py:302
  225.3 22.0 %gather_feed.1 = bf16[8,128,2048]{2,1,0:T(8,128)(2,1)} custom-call(bf16[128,2048]{1,0:T(8,128)(2,1)} %multiply_convert_fusion.7.refs_0_), custom_call_target="tpu_custom_call" | custom-call | bytes 67108864 | tf_op jit(solution)/shard_map/gather_feed/pallas_call | solution.py:201
  247.3 6.5 %fusion.2 = f32[1024,768]{0,1:T(8,128)S(1)} fusion(bf16[1024,2048]{1,0:T(8,128)(2,1)} %bitcast.171, bf16[2048,1920]{1,0:T(8,128)(2,1)} %all-gather.6.cloned.1.call-done), kind=kOutput, calls=%fused_computation.14 | convolution fusion | flops 3221225472 | bytes 10485760 | tf_op jit(solution)/shard_map/rd,df->rf/dot_general | solution.py:28
  269.9 5.9 %fusion.5 = f32[1024,640]{0,1:T(8,128)S(1)} fusion(bf16[1024,2048]{1,0:T(8,128)(2,1)} %bitcast.172, bf16[2048,960]{1,0:T(8,128)(2,1)} %all-gather.8.cloned.1.call-done), kind=kOutput, calls=%fused_computation.24 | convolution fusion | flops 2684354560 | bytes 9437184 | tf_op jit(solution)/shard_map/rd,df->rf/dot_general | solution.py:28
  288.7 6.1 %fusion = f32[1024,2048]{1,0:T(8,128)S(1)} fusion(bf16[1024,768]{0,1:T(8,128)(2,1)} %pad_maximum_fusion.5, bf16[2048,1920]{1,0:T(8,128)(2,1)} %all-gather.6.cloned.1.call-done), kind=kOutput, calls=%fused_computation.12 | convolution fusion | flops 3221225472 | bytes 13107200 | tf_op jit(solution)/shard_map/rf,df->rd/dot_general | solution.py:28
  298.6 22.8 %reduce_ffn_grad.1 = f32[128,2048]{1,0:T(8,128)S(1)} custom-call(bf16[8,128,2048]{2,1,0:T(8,128)(2,1)S(1)} %bitcast.162), custom_call_target="tpu_custom_call" | custom-call | bytes 67108864 | tf_op jit(solution)/shard_map/reduce_ffn_grad/pallas_call | solution.py:302
  323.6 21.7 %gather_branch.1 = bf16[8,128,2048]{2,1,0:T(8,128)(2,1)} custom-call(bf16[128,2048]{1,0:T(8,128)(2,1)} %fusion.89.refs_0_), custom_call_target="tpu_custom_call" | custom-call | bytes 67108864 | tf_op jit(solution)/shard_map/gather_branch/pallas_call | solution.py:201
  345.4 6.3 %fusion.13 = bf16[1024,512]{1,0:T(8,128)(2,1)} fusion(bf16[1024,2048]{1,0:T(8,128)(2,1)} %bitcast.169, bf16[2048,1920]{1,0:T(8,128)(2,1)} %all-gather.6.cloned.1.call-done), kind=kOutput, calls=%fused_computation.46 | convolution fusion | flops 2148007936 | bytes 7340032 | tf_op jit(solution)/shard_map/rd,df->rf/dot_general | solution.py:28
  371.8 18.0 %reduce_latent.1 = f32[128,1536]{1,0:T(8,128)S(1)} custom-call(bf16[8,128,1536]{2,1,0:T(8,128)(2,1)S(1)} %pad_maximum_fusion.2.in_ref), custom_call_target="tpu_custom_call" | custom-call | bytes 50331648 | tf_op jit(solution)/shard_map/reduce_latent/pallas_call | solution.py:302
  399.7 6.5 %fusion.41 = (f32[128]{0:T(128)}, bf16[2048]{0:T(1024)(128)(2,1)S(1)}, f32[128,2048]{1,0:T(8,128)}) fusion(bf16[128,2048]{1,0:T(8,128)(2,1)S(1)} %copy-done.1, f32[2048]{0:T(1024)S(1)} %convert.95, f32[128]{0:T(128)} %copy-done.47, bf16[2048,1536]{1,0:T(8,128)(2,1)} %bitcast.165, bf16[128,256]{1,0:T(8,128)(2,1)S(1)} %slice.280, ...), kind=kOutput, calls=%fused_computation.84 | convolution fusion | flops 808712064 | bytes 8270848 | tf_op jit(solution)/shard_map/re,de->rd/dot_general | solution.py:28
  406.8 19.5 %gather_last.1 = (bf16[8,128,1536]{2,1,0:T(8,128)(2,1)}, bf16[8,32,1024]{2,1,0:T(8,128)(2,1)}) custom-call(bf16[128,1536]{1,0:T(8,128)(2,1)} %pad_maximum_fusion.11.refs_0_, bf16[32,1024]{1,0:T(8,128)(2,1)} %pad.15.refs_1_), custom_call_target="tpu_custom_call" | custom-call | bytes 58720256 | tf_op jit(solution)/shard_map/gather_last/pallas_call | solution.py:201
  435.8 22.0 %reduce_feed.1 = f32[128,2048]{1,0:T(8,128)S(1)} custom-call(bf16[8,128,2048]{2,1,0:T(8,128)(2,1)S(1)} %bitcast.161), custom_call_target="tpu_custom_call" | custom-call | bytes 67108864 | tf_op jit(solution)/shard_map/reduce_feed/pallas_call | solution.py:302
  461.4 4.7 all-to-all-start.1
  466.2 4.9 convolution_convert_fusion.5
  472.1 18.6 %reduce-scatter.9.cloned.1.call-done = bf16[768,512]{1,0:T(8,128)(2,1)} async-done(((bf16[3072,512]{1,0:T(8,128)(2,1)}), bf16[768,512]{1,0:T(8,128)(2,1)}) %reduce-scatter.9.cloned.1.call-update) | async-done | bytes 786448 | tf_op jit(solution)/shard_map/reduce_scatter | solution.py:531
  495.0 4.3 all-to-all-start
  511.5 5.6 %reduce-scatter.11.cloned.1.call-done.refs_0_ = bf16[272,384]{1,0:T(8,128)(2,1)} async-done(((bf16[1088,384]{1,0:T(8,128)(2,1)}), bf16[272,384]{1,0:T(8,128)(2,1)}) %reduce-scatter.11.cloned.1.call-update) | async-done | bytes 208912 | tf_op jit(solution)/shard_map/reduce_scatter | solution.py:531
  518.8 8.4 %settle_last.1 = (f32[128,1024]{1,0:T(8,128)S(1)}, f32[128,512]{1,0:T(8,128)S(1)}) custom-call(bf16[272,384]{1,0:T(8,128)(2,1)S(1)} %copy-done), custom_call_target="tpu_custom_call" | custom-call | bytes 12582912 | tf_op jit(solution)/shard_map/settle_last/pallas_call | solution.py:461
  (292 shorter events, 152.5 us)
Async XLA Ops:
  7.2 57.4 %all-gather.4.cloned.1.call-start = ((), (), s32[]{:S(2)}) async-start(), calls=%async_computation.6 | async-start | bytes 1351680 | tf_op jit(solution)/shard_map/all_gather | solution.py:525
  10.4 175.6 %all-gather.6.cloned.1.call-start = ((), (), s32[]{:S(2)}) async-start(), calls=%async_computation.7 | async-start | bytes 9830400 | tf_op jit(solution)/shard_map/all_gather | solution.py:525
  43.4 226.5 %all-gather.8.cloned.1.call-start = ((), (), s32[]{:S(2)}) async-start(), calls=%async_computation.8 | async-start | bytes 5242880 | tf_op jit(solution)/shard_map/all_gather | solution.py:525
  45.1 17.8 %copy-start.1 = (bf16[128,2048]{1,0:T(8,128)(2,1)S(1)}, bf16[128,2048]{1,0:T(8,128)(2,1)}, u32[]{:S(2)}) copy-start(bf16[128,2048]{1,0:T(8,128)(2,1)} %param.13) | copy-start | bytes 1572868
  45.4 18.3 %copy-start.6 = (bf16[128,2048]{1,0:T(8,128)(2,1)S(1)}, bf16[128,2048]{1,0:T(8,128)(2,1)}, u32[]{:S(2)}) copy-start(bf16[128,2048]{1,0:T(8,128)(2,1)} %param.25) | copy-start | bytes 1572868
  61.3 106.3 %copy-start.45 = (f32[128]{0:T(128)}, f32[128]{0:T(128)S(1)}, u32[]{:S(2)}) copy-start(f32[128]{0:T(128)S(1)} %multiply_power_fusion) | copy-start | bytes 1540
  62.0 260.3 %copy-start.43 = (pred[128]{0:T(512)(128)(4,1)}, pred[128]{0:T(512)(128)(4,1)S(1)}, u32[]{:S(2)}) copy-start(pred[128]{0:T(512)(128)(4,1)S(1)} %iota_compare_fusion.8) | copy-start | bytes 388
  63.6 43.1 %copy-start.47 = (f32[128]{0:T(128)}, f32[128]{0:T(128)S(1)}, u32[]{:S(2)}) copy-start(f32[128]{0:T(128)S(1)} %fusion.83) | copy-start | bytes 1540
  63.6 43.8 %copy-start.49 = (f32[128]{0:T(128)}, f32[128]{0:T(128)S(1)}, u32[]{:S(2)}) copy-start(f32[128]{0:T(128)S(1)} %subtract_convert_fusion.2) | copy-start | bytes 1540
  102.3 287.6 %copy-start.35 = (f32[1024]{0:T(1024)}, f32[1024]{0:T(1024)S(1)}, u32[]{:S(2)}) copy-start(f32[1024]{0:T(1024)S(1)} %reshape.332) | copy-start | bytes 12292
  108.5 281.4 %copy-start.41 = (f32[128]{0:T(128)}, f32[128]{0:T(128)S(1)}, u32[]{:S(2)}) copy-start(f32[128]{0:T(128)S(1)} %fusion.84) | copy-start | bytes 1540
  170.6 22.5 %copy-start.8 = (f32[8,128,128]{2,1,0:T(8,128)}, f32[8,128,128]{2,1,0:T(8,128)S(1)}, u32[]{:S(2)}) copy-start(f32[8,128,128]{2,1,0:T(8,128)S(1)} %get-tuple-element.112) | copy-start | bytes 1572868
  170.6 186.5 %reduce-scatter.5.cloned.1.call-start = ((), (), s32[]{:S(2)}) async-start(), calls=%async_computation.9 | async-start | bytes 5898240 | tf_op jit(solution)/shard_map/reduce_scatter | solution.py:531
  224.3 97.9 %copy-start.38 = (f32[128]{0:T(128)}, f32[128]{0:T(128)S(1)}, u32[]{:S(2)}) copy-start(f32[128]{0:T(128)S(1)} %fusion.85) | copy-start | bytes 1540
  267.4 160.5 %reduce-scatter.7.cloned.1.call-start = ((), (), s32[]{:S(2)}) async-start(), calls=%async_computation.10 | async-start | bytes 4915200 | tf_op jit(solution)/shard_map/reduce_scatter | solution.py:531
  322.4 23.0 %copy-start.51 = (f32[128]{0:T(128)}, f32[128]{0:T(128)S(1)}, u32[]{:S(2)}) copy-start(f32[128]{0:T(128)S(1)} %multiply_multiply_fusion.2) | copy-start | bytes 1540
  357.2 133.6 %reduce-scatter.9.cloned.1.call-start = ((), (), s32[]{:S(2)}) async-start(), calls=%async_computation.11 | async-start | bytes 3932160 | tf_op jit(solution)/shard_map/reduce_scatter | solution.py:531
  371.8 18.8 %copy-start.57 = (bf16[8,128,1024]{2,1,0:T(8,128)(2,1)S(1)}, bf16[8,128,1024]{2,1,0:T(8,128)(2,1)}, u32[]{:S(2)}) copy-start(bf16[8,128,1024]{2,1,0:T(8,128)(2,1)} %get-tuple-element.52) | copy-start | bytes 6291460
  406.1 21.9 %copy-start.24 = (bf16[1024,384]{0,1:T(8,128)(2,1)S(1)}, bf16[1024,384]{0,1:T(8,128)(2,1)}, u32[]{:S(2)}) copy-start(bf16[1024,384]{0,1:T(8,128)(2,1)} %copy-done.23) | copy-start | bytes 2359300
  461.4 31.1 %all-to-all-start.1 = ((bf16[4,128,2112]{1,2,0:T(8,128)(2,1)}), bf16[4,128,2112]{1,2,0:T(8,128)(2,1)}, u32[]{:S(2)}, u32[]{:S(2)}) async-start(bf16[4,128,2112]{1,2,0:T(8,128)(2,1)} %copy_bitcast_fusion), calls=%async_computation.5 | async-start | bytes 4325376 | tf_op jit(solution)/shard_map/all_to_all | solution.py:830
  466.1 51.1 %reduce-scatter.11.cloned.1.call-start = ((), (), s32[]{:S(2)}) async-start(), calls=%async_computation.12 | async-start | bytes 1044480 | tf_op jit(solution)/shard_map/reduce_scatter | solution.py:531
  492.5 6.8 %copy-start.48 = (f32[128]{0:T(128)S(1)}, f32[128]{0:T(128)}, u32[]{:S(2)}) copy-start(f32[128]{0:T(128)} %copy-done.47) | copy-start | bytes 1540
  492.6 6.8 %copy-start.52 = (f32[128]{0:T(128)S(1)}, f32[128]{0:T(128)}, u32[]{:S(2)}) copy-start(f32[128]{0:T(128)} %copy-done.51) | copy-start | bytes 1540
  495.0 32.2 %all-to-all-start = ((bf16[8,192,512]{2,1,0:T(8,128)(2,1)}), bf16[8,192,512]{2,1,0:T(8,128)(2,1)}, u32[]{:S(2)}, u32[]{:S(2)}) async-start(bf16[8,192,512]{2,1,0:T(8,128)(2,1)} %bitcast.168), calls=%async_computation.4 | async-start | bytes 3145728 | tf_op jit(solution)/shard_map/all_to_all | solution.py:851
  (48 other events, 151.2 us)
Sparse Core Ops, SparseCore 0:
  10.5 31.1 all-gather.3
  43.5 142.4 all-gather.5
  187.5 78.9 all-gather.7
  268.7 83.7 reduce-scatter.4
  357.3 70.6 reduce-scatter.6
  430.1 60.5 reduce-scatter.8
  493.0 24.1 reduce-scatter.10
